TPU v7x, 32 devices: a whole 2x2x4 slice. The times are simulated.
32 devices in a mesh: dp: 8 (over z, x), fsdp: 4 (over y, core).
Axes of the slice: x: 2, y: 2, z: 4, core: 2. Of those that a mesh axis runs over, the one named last changes fastest.
Arguments:
- tokens: bfloat16 [25600, 768], P(('dp', 'fsdp')), may hold values from -6 to 6
- prev_kv: bfloat16 [2, 25600, 768], P(None, ('dp', 'fsdp')), may hold values from -6 to 6
- memory: bfloat16 [2, 6400, 768], P(None, ('dp', 'fsdp')), may hold values from -6 to 6
- valid_frames: int32 [32], P(('dp', 'fsdp')), may hold values from 4 to 8, as said below
- mem_len: int32 [32], P(('dp', 'fsdp')), may hold values from 50 to 200, as said below
- ln1_gain: float32 [768], replicated, may hold values from 0.1 to 1.9
- ln1_bias: float32 [768], replicated, may hold values from -1.75 to 1.75
- w_qkv: bfloat16 [768, 2304], P('dp', 'fsdp'), may hold values from -0.21875 to 0.21875
- qkv_bias: float32 [2304], replicated, may hold values from -1.75 to 1.75
- pool_conv: float32 [3, 27, 96], replicated, may hold values from -1.25 to 1.25
- pool_gain: float32 [3, 96], replicated, may hold values from 0.1 to 1.9
- pool_bias: float32 [3, 96], replicated, may hold values from -1.75 to 1.75
- rel_time: float32 [15, 96], replicated, may hold values from -0.625 to 0.625
- rel_space: float32 [2, 19, 96], replicated, may hold values from -0.625 to 0.625
- compress: float32 [2, 4, 96], replicated, may hold values from -3 to 3
- w_proj: bfloat16 [768, 768], P('dp', 'fsdp'), may hold values from -0.21875 to 0.21875
- proj_bias: float32 [768], replicated, may hold values from -1.75 to 1.75
- ln2_gain: float32 [768], replicated, may hold values from 0.1 to 1.9
- ln2_bias: float32 [768], replicated, may hold values from -1.75 to 1.75
- w_fc1: bfloat16 [768, 3072], P('dp', 'fsdp'), may hold values from -0.21875 to 0.21875
- fc1_bias: float32 [3072], replicated, may hold values from -1.75 to 1.75
- w_fc2: bfloat16 [3072, 768], P('dp', 'fsdp'), may hold values from -0.109375 to 0.109375
- fc2_bias: float32 [768], replicated, may hold values from -1.75 to 1.75
- cotangent: bfloat16 [25600, 768], P(('dp', 'fsdp')), may hold values from -6 to 6
Outputs:
- out: bfloat16 [25600, 768], P(('dp', 'fsdp'))
- grad_tokens: float32 [25600, 768], P(('dp', 'fsdp'))
- grad_ln1_gain: float32 [768], replicated
- grad_ln1_bias: float32 [768], replicated
- grad_w_qkv: float32 [768, 2304], P('dp', 'fsdp')
- grad_qkv_bias: float32 [2304], replicated
- grad_pool_conv: float32 [3, 27, 96], replicated
- grad_pool_gain: float32 [3, 96], replicated
- grad_pool_bias: float32 [3, 96], replicated
- grad_rel_time: float32 [15, 96], replicated
- grad_rel_space: float32 [2, 19, 96], replicated
- grad_compress: float32 [2, 4, 96], replicated
- grad_w_proj: float32 [768, 768], P('dp', 'fsdp')
- grad_proj_bias: float32 [768], replicated
- grad_ln2_gain: float32 [768], replicated
- grad_ln2_bias: float32 [768], replicated
- grad_w_fc1: float32 [768, 3072], P('dp', 'fsdp')
- grad_fc1_bias: float32 [3072], replicated
- grad_w_fc2: float32 [3072, 768], P('dp', 'fsdp')
- grad_fc2_bias: float32 [768], replicated
Inputs may be any that keep to these rules, and one draw needn't show every extreme that they name: `valid_frames`: some clip has all 8 frames. `mem_len`: some clip has all 200 memory rows.
All inputs are finite; a program needn't handle non-finite values.
Results may differ from a plain program's by a relative error of at most 0.017.
Values may be sent and summed in bfloat16 or wider, within the bound.
A program may use at most 576 MiB of HBM per device.

v0:
```python
from functools import partial

import jax
import jax.numpy as jnp
from jax import lax
from jax.sharding import PartitionSpec as P

D = 768
HEADS = 8
HEAD_DIM = 96
FRAMES = 8
HEIGHT = 10
WIDTH = 10
ROWS = 800
MEM = 200
KEYS = 1200


EPSILON = 1e-06


def rounded(values):
    return lax.optimization_barrier(values.astype(jnp.bfloat16)).astype(jnp.float32)


def normalize(values, scale_gain, shift_bias):
    average = jnp.mean(values, axis=-1, keepdims=True)
    centred = values - average
    variance = jnp.mean(centred * centred, axis=-1, keepdims=True)
    return centred * lax.rsqrt(variance + EPSILON) * scale_gain + shift_bias


def relative_index(length):
    counter = jnp.arange(length, dtype=jnp.int32)
    return counter[:, None] - counter[None, :] + (length - 1)


def pool_clip(mixed, pool_conv, pool_gain, pool_bias):
    grid = mixed.reshape(FRAMES, HEIGHT, WIDTH, 3, HEADS, HEAD_DIM)
    padded = jnp.pad(grid, ((1, 1), (1, 1), (1, 1), (0, 0), (0, 0), (0, 0)))
    pooled = jnp.zeros_like(grid)
    for offset in range(27):
        step_time, step_height, step_width = (offset // 9, offset // 3 % 3, offset % 3)
        window = padded[
            step_time : step_time + FRAMES,
            step_height : step_height + HEIGHT,
            step_width : step_width + WIDTH,
        ]
        pooled = pooled + window * pool_conv[:, offset, :][:, None, :]
    normed_pool = normalize(pooled, pool_gain[:, None, :], pool_bias[:, None, :])
    return normed_pool.reshape(ROWS, 3 * D)


def squeeze_clip(compress, previous):
    earlier = previous.reshape(2, FRAMES, HEIGHT // 2, 2, WIDTH // 2, 2, HEADS, HEAD_DIM)
    squeezed = jnp.zeros((2, FRAMES, HEIGHT // 2, WIDTH // 2, HEADS, HEAD_DIM), jnp.float32)
    for offset in range(4):
        squeezed = (
            squeezed
            + earlier[:, :, :, offset // 2, :, offset % 2]
            * compress[:, offset, :][:, None, None, None, None, :]
        )
    return squeezed.reshape(2, MEM, HEADS, HEAD_DIM).transpose(0, 2, 1, 3)


def build_tables(rel_time, rel_space):
    return (
        rel_time[relative_index(FRAMES)],
        rel_space[0][relative_index(HEIGHT)],
        rel_space[1][relative_index(WIDTH)],
    )


def relative_terms(query, tables):
    time_table, height_table, width_table = tables
    grid = query.reshape(FRAMES, HEIGHT, WIDTH, HEAD_DIM)
    along_time = jnp.einsum("thwc,tkc->thwk", grid, time_table)
    along_height = jnp.einsum("thwc,hkc->thwk", grid, height_table)
    along_width = jnp.einsum("thwc,wkc->thwk", grid, width_table)
    return (along_time, along_height, along_width)


def score_terms(query, keys, along_time, along_height, along_width):
    relative = (
        along_time[:, :, :, :, None, None]
        + along_height[:, :, :, None, :, None]
        + along_width[:, :, :, None, None, :]
    ).reshape(ROWS, ROWS)
    scores = jnp.dot(query, keys.T) * HEAD_DIM ** (-0.5)
    return jnp.concatenate([scores[:, : 2 * MEM], scores[:, 2 * MEM :] + relative], axis=1)


def masked_softmax(scores, key_ok):
    scores = jnp.where(key_ok[None, :] > 0, scores, -1000000000.0)
    largest = jnp.max(scores, axis=1, keepdims=True)
    weights = jnp.exp(scores - largest)
    return weights / jnp.sum(weights, axis=1, keepdims=True)


def head_output(probs, values, query):
    return jnp.dot(probs, values) + query


def head_forward(item, tables):
    query, keys, values, key_ok = item
    along_time, along_height, along_width = relative_terms(query, tables)
    scores = score_terms(query, keys, along_time, along_height, along_width)
    probs = rounded(masked_softmax(scores, key_ok))
    return head_output(probs, values, query)


def head_backward(item, tables):
    query, keys, values, key_ok, upstream = item
    along, pull_relative = jax.vjp(relative_terms, query, tables)
    scores, pull_scores = jax.vjp(score_terms, query, keys, along[0], along[1], along[2])
    probs_full, pull_softmax = jax.vjp(partial(masked_softmax, key_ok=key_ok), scores)
    probs = rounded(probs_full)
    unused_out, pull_output = jax.vjp(head_output, probs, values, query)
    grad_probs, grad_values, query_first = pull_output(upstream)
    (grad_scores,) = pull_softmax(grad_probs)
    query_second, grad_keys, grad_time, grad_height, grad_width = pull_scores(rounded(grad_scores))
    query_third, grad_tables = pull_relative(
        (rounded(grad_time), rounded(grad_height), rounded(grad_width))
    )
    return (query_first + query_second + query_third, grad_keys, grad_values, grad_tables)


def collect(shards):
    columns = (
        lax.all_gather(shards[0], "fsdp", axis=1, tiled=True),
        lax.all_gather(shards[1], "fsdp", axis=1, tiled=True),
        lax.all_gather(shards[2], "fsdp", axis=1, tiled=True),
        lax.all_gather(shards[3], "fsdp", axis=1, tiled=True),
    )
    return (
        lax.all_gather(columns[0], "dp", axis=0, tiled=True),
        lax.all_gather(columns[1], "dp", axis=0, tiled=True),
        lax.all_gather(columns[2], "dp", axis=0, tiled=True),
        lax.all_gather(columns[3], "dp", axis=0, tiled=True),
    )


def column_sum(values):
    return jnp.sum(values.astype(jnp.float32), axis=0)


def on_device(
    tokens,
    prev_kv,
    memory,
    valid_frames,
    mem_len,
    ln1_gain,
    ln1_bias,
    w_qkv,
    qkv_bias,
    pool_conv,
    pool_gain,
    pool_bias,
    rel_time,
    rel_space,
    compress,
    w_proj,
    proj_bias,
    ln2_gain,
    ln2_bias,
    w_fc1,
    fc1_bias,
    w_fc2,
    fc2_bias,
    cotangent,
):
    clips = valid_frames.shape[0]
    inputs = tokens.astype(jnp.float32)
    earlier = prev_kv.astype(jnp.float32).reshape(2, clips, ROWS, D).transpose(1, 0, 2, 3)
    older = memory.astype(jnp.float32).reshape(2, clips, MEM, D).transpose(1, 0, 2, 3)
    older = older.reshape(clips, 2, MEM, HEADS, HEAD_DIM).transpose(0, 1, 3, 2, 4)
    row_frame = jnp.arange(ROWS, dtype=jnp.int32) // (HEIGHT * WIDTH)
    valid_clip = (row_frame[None, :] < valid_frames[:, None]).astype(jnp.float32)
    valid = valid_clip.reshape(clips * ROWS)
    memory_ok = (jnp.arange(MEM, dtype=jnp.int32)[None, :] < mem_len[:, None]).astype(jnp.float32)
    key_ok = jnp.concatenate([memory_ok, jnp.ones((clips, MEM), jnp.float32), valid_clip], axis=1)
    shards = (w_qkv, w_proj, w_fc1, w_fc2)
    gathered = collect(shards)
    weight_qkv, weight_proj, weight_one, weight_two = gathered
    normed_full, pull_first_norm = jax.vjp(normalize, inputs, ln1_gain, ln1_bias)
    normed = normed_full.astype(jnp.bfloat16)
    mixed = (jnp.dot(normed, weight_qkv, preferred_element_type=jnp.float32) + qkv_bias) * valid[
        :, None
    ]

    def pool_all(mixed_clips, conv_taps, gains, biases):
        return jax.vmap(pool_clip, in_axes=(0, None, None, None))(
            mixed_clips, conv_taps, gains, biases
        )

    pooled_full, pull_pool = jax.vjp(
        pool_all, mixed.reshape(clips, ROWS, 3 * D), pool_conv, pool_gain, pool_bias
    )
    pooled = rounded(pooled_full)
    heads_first = pooled.reshape(clips, ROWS, 3, HEADS, HEAD_DIM).transpose(2, 0, 3, 1, 4)

    def squeeze_all(taps):
        return jax.vmap(squeeze_clip, in_axes=(None, 0))(taps, earlier)

    squeezed_full, pull_squeeze = jax.vjp(squeeze_all, compress)
    squeezed = rounded(squeezed_full)
    keys = jnp.concatenate([older[:, 0], squeezed[:, 0], heads_first[1]], axis=2)
    values = jnp.concatenate([older[:, 1], squeezed[:, 1], heads_first[2]], axis=2)
    tables_full, pull_tables = jax.vjp(build_tables, rel_time, rel_space)
    tables = tuple((rounded(table) for table in tables_full))
    items = clips * HEADS
    query_items = heads_first[0].reshape(items, ROWS, HEAD_DIM)
    key_items = keys.reshape(items, KEYS, HEAD_DIM)
    value_items = values.reshape(items, KEYS, HEAD_DIM)
    ok_items = jnp.repeat(key_ok, HEADS, axis=0)
    attended_full = lax.map(
        partial(head_forward, tables=tables), (query_items, key_items, value_items, ok_items)
    )
    attended = (
        attended_full.reshape(clips, HEADS, ROWS, HEAD_DIM)
        .transpose(0, 2, 1, 3)
        .reshape(clips * ROWS, D)
    )
    attended = attended.astype(jnp.bfloat16)
    middle = inputs + jnp.dot(attended, weight_proj, preferred_element_type=jnp.float32) + proj_bias
    hidden_full, pull_second_norm = jax.vjp(normalize, middle, ln2_gain, ln2_bias)
    hidden = hidden_full.astype(jnp.bfloat16)
    before = jnp.dot(hidden, weight_one, preferred_element_type=jnp.float32) + fc1_bias
    activated_full, pull_gelu = jax.vjp(partial(jax.nn.gelu, approximate=False), before)
    activated = activated_full.astype(jnp.bfloat16)
    result = middle + jnp.dot(activated, weight_two, preferred_element_type=jnp.float32) + fc2_bias
    back_qkv, back_proj, back_one, back_two = collect(shards)
    upstream = cotangent.astype(jnp.float32)
    grad_two = jnp.dot(activated.T, upstream, preferred_element_type=jnp.float32)
    grad_two_bias = column_sum(upstream)
    grad_act = jnp.dot(upstream, back_two.T, preferred_element_type=jnp.float32)
    (grad_before,) = pull_gelu(grad_act)
    grad_before = grad_before.astype(jnp.bfloat16)
    grad_one = jnp.dot(hidden.T, grad_before, preferred_element_type=jnp.float32)
    grad_one_bias = column_sum(grad_before)
    grad_hidden = jnp.dot(grad_before, back_one.T, preferred_element_type=jnp.float32)
    grad_mid_norm, grad_second_gain, grad_second_bias = pull_second_norm(grad_hidden)
    grad_middle = upstream + grad_mid_norm
    grad_projected = grad_middle.astype(jnp.bfloat16)
    grad_proj = jnp.dot(attended.T, grad_projected, preferred_element_type=jnp.float32)
    grad_proj_bias = column_sum(grad_projected)
    grad_attended = jnp.dot(grad_projected, back_proj.T, preferred_element_type=jnp.float32).astype(
        jnp.bfloat16
    )
    grad_heads = (
        grad_attended.astype(jnp.float32)
        .reshape(clips, ROWS, HEADS, HEAD_DIM)
        .transpose(0, 2, 1, 3)
    )
    grad_heads = grad_heads.reshape(items, ROWS, HEAD_DIM)
    grad_query, grad_keys, grad_values, grad_tables = lax.map(
        partial(head_backward, tables=tables),
        (query_items, key_items, value_items, ok_items, grad_heads),
    )
    grad_tables = tuple((jnp.sum(table, axis=0) for table in grad_tables))
    grad_time_table, grad_space_table = pull_tables(grad_tables)
    grad_keys = grad_keys.reshape(clips, HEADS, KEYS, HEAD_DIM)
    grad_values = grad_values.reshape(clips, HEADS, KEYS, HEAD_DIM)
    grad_squeezed = jnp.stack(
        [grad_keys[:, :, MEM : 2 * MEM], grad_values[:, :, MEM : 2 * MEM]], axis=1
    )
    (grad_compress,) = pull_squeeze(grad_squeezed)
    grad_stack = jnp.stack(
        [
            grad_query.reshape(clips, HEADS, ROWS, HEAD_DIM),
            grad_keys[:, :, 2 * MEM :],
            grad_values[:, :, 2 * MEM :],
        ]
    )
    grad_pooled = rounded(grad_stack.transpose(1, 3, 0, 2, 4).reshape(clips, ROWS, 3 * D))
    grad_mixed, grad_conv, grad_pool_gain, grad_pool_bias = pull_pool(grad_pooled)
    grad_mixed = (grad_mixed.reshape(clips * ROWS, 3 * D) * valid[:, None]).astype(jnp.bfloat16)
    grad_qkv = jnp.dot(normed.T, grad_mixed, preferred_element_type=jnp.float32)
    grad_qkv_bias = column_sum(grad_mixed)
    grad_normed = jnp.dot(grad_mixed, back_qkv.T, preferred_element_type=jnp.float32)
    grad_first_input, grad_first_gain, grad_first_bias = pull_first_norm(grad_normed)
    token_grads = grad_middle + grad_first_input
    row_sums = (
        lax.psum_scatter(grad_qkv, "dp", scatter_dimension=0, tiled=True),
        lax.psum_scatter(grad_proj, "dp", scatter_dimension=0, tiled=True),
        lax.psum_scatter(grad_one, "dp", scatter_dimension=0, tiled=True),
        lax.psum_scatter(grad_two, "dp", scatter_dimension=0, tiled=True),
    )
    sums = (
        lax.psum_scatter(
            row_sums[0].astype(jnp.bfloat16), "fsdp", scatter_dimension=1, tiled=True
        ).astype(jnp.float32),
        lax.psum_scatter(
            row_sums[1].astype(jnp.bfloat16), "fsdp", scatter_dimension=1, tiled=True
        ).astype(jnp.float32),
        lax.psum_scatter(
            row_sums[2].astype(jnp.bfloat16), "fsdp", scatter_dimension=1, tiled=True
        ).astype(jnp.float32),
        lax.psum_scatter(
            row_sums[3].astype(jnp.bfloat16), "fsdp", scatter_dimension=1, tiled=True
        ).astype(jnp.float32),
    )
    totals = lax.psum(
        (
            grad_first_gain,
            grad_first_bias,
            grad_qkv_bias,
            grad_conv,
            grad_pool_gain,
            grad_pool_bias,
            grad_time_table,
            grad_space_table,
            grad_compress,
            grad_proj_bias,
            grad_second_gain,
            grad_second_bias,
            grad_one_bias,
            grad_two_bias,
        ),
        ("dp", "fsdp"),
    )
    output = result.astype(jnp.bfloat16)
    return (
        output,
        token_grads,
        totals[0],
        totals[1],
        sums[0],
        totals[2],
        totals[3],
        totals[4],
        totals[5],
        totals[6],
        totals[7],
        totals[8],
        sums[1],
        totals[9],
        totals[10],
        totals[11],
        sums[2],
        totals[12],
        sums[3],
        totals[13],
    )


def solution(mesh):
    placed = (
        P(("dp", "fsdp"), None),
        P(None, ("dp", "fsdp"), None),
        P(None, ("dp", "fsdp"), None),
        P(("dp", "fsdp")),
        P(("dp", "fsdp")),
        P(),
        P(),
        P("dp", "fsdp"),
        P(),
        P(),
        P(),
        P(),
        P(),
        P(),
        P(),
        P("dp", "fsdp"),
        P(),
        P(),
        P(),
        P("dp", "fsdp"),
        P(),
        P("dp", "fsdp"),
        P(),
        P(("dp", "fsdp"), None),
    )
    return jax.shard_map(
        on_device,
        mesh=mesh,
        in_specs=placed,
        out_specs=(
            P(("dp", "fsdp"), None),
            P(("dp", "fsdp"), None),
            P(),
            P(),
            P("dp", "fsdp"),
            P(),
            P(),
            P(),
            P(),
            P(),
            P(),
            P(),
            P("dp", "fsdp"),
            P(),
            P(),
            P(),
            P("dp", "fsdp"),
            P(),
            P("dp", "fsdp"),
            P(),
        ),
        check_vma=False,
    )
```

profile of v0, /device:TPU:0, one launch (start us, length us, event | category | flops | bytes accessed | tf_op | source)
XLA Modules:
  0.0 3006.3 jit_solution(3797885851138101074)
XLA Ops:
  103.1 81.4 %fusion.128 = (f32[8,10,10,3,8]{4,3,2,1,0:T(4,128)S(1)}, f32[1,8,10,10,3,8,96]{6,5,4,3,2,1,0:T(8,128)}) fusion(f32[3,96]{1,0:T(4,128)S(1)} %get-tuple-element.687, f32[3,96]{1,0:T(4,128)S(1)} %get-tuple-element.688, f32[3,96]{1,0:T(4,128)S(1)} %get-tuple-element.695, f32[3,96]{1,0:T(4,128)S(1)} %get-tuple-element.696, f32[3,96]{1,0:T(4,128)S(1)} %get-tuple-element.697, ...), kind=kLoop, calls=%fused_computation.376 | loop fusion | flops 99513600 | bytes 14853504 | tf_op jit(solution)/shard_map/jvp(vmap())/reduce_sum | solution.py:27
  244.1 527.6 %while.30 = (s32[]{:T(128)}, bf16[8,800,96]{1,2,0:T(8,128)(2,1)}, f32[8,1200]{1,0:T(8,128)S(1)}, f32[8,800,96]{2,1,0:T(8,128)}, bf16[8,1200,96]{2,1,0:T(8,128)(2...) while((s32[]{:T(128)}, bf16[8,800,96]{1,2,0:T(8,128)(2,1)}, ...), condition=%wide.region_7.8_spmd, body=%wide.region_4.7_spmd.sunk | while | flops 386841216 | bytes 56934544 | solution.py:217
  269.6 30.7 %add.828 = f32[800,800]{1,0:T(8,128)} reshape(f32[8,10,10,8,10,10]{5,4,3,2,1,0:T(8,128)} %broadcast_add_fusion.11) | data formatting | bytes 5120000 | tf_op jit(solution)/shard_map/while/body/eval_jaxpr/add | solution.py:85
  789.4 32.0 %convert_reduce_fusion.1 = (f32[3072]{0:T(1024)}, bf16[800,3072]{1,0:T(8,128)(2,1)S(1)}, f32[800,3072]{1,0:T(8,128)}) fusion(f32[800,3072]{1,0:T(8,128)} %fusion.121, f32[3072]{0:T(1024)S(1)} %copy-done.113, bf16[800,768]{1,0:T(8,128)(2,1)} %param.51, bf16[3072,768]{0,1:T(8,128)(2,1)} %all-gather.12.cloned.1.call-done), kind=kOutput, calls=%fused_computation.149 | convolution fusion | flops 3959190528 | bytes 30547968 | tf_op jit(solution)/shard_map/dot_general | solution.py:237
  840.0 1127.8 %while.31 = (s32[]{:T(128)}, bf16[8,800,96]{1,2,0:T(8,128)(2,1)}, f32[8,1200,96]{1,2,0:T(8,128)}, f32[8,1200,96]{1,2,0:T(8,128)}, f32[8,8,8,96]{3,2,1,0:T(8,128)...) while((s32[]{:T(128)}, bf16[8,800,96]{1,2,0:T(8,128)(2,1)}, ...), condition=%wide.region_21.22_spmd, body=%wide.region_12.0_spmd.sunk | while | flops 974532352 | bytes 119826960 | solution.py:257
  865.9 30.7 %add.839 = f32[800,800]{1,0:T(8,128)} reshape(f32[8,10,10,8,10,10]{5,4,3,2,1,0:T(8,128)} %broadcast_add_fusion.13) | data formatting | bytes 5120000 | tf_op jit(solution)/shard_map/while/body/eval_jaxpr/jvp()/add | solution.py:85
  918.1 32.3 %reshape.1188 = f32[8,10,10,8,10,10]{5,4,3,2,1,0:T(8,128)} reshape(f32[800,800]{1,0:T(8,128)} %copy-done.4) | data formatting | bytes 5120000 | tf_op jit(solution)/shard_map/while/body/eval_jaxpr/transpose(jvp())/reshape | solution.py:88
  1006.8 30.7 %add.839 = f32[800,800]{1,0:T(8,128)} reshape(f32[8,10,10,8,10,10]{5,4,3,2,1,0:T(8,128)} %broadcast_add_fusion.13) | data formatting | bytes 5120000 | tf_op jit(solution)/shard_map/while/body/eval_jaxpr/jvp()/add | solution.py:85
  1059.0 32.3 %reshape.1188 = f32[8,10,10,8,10,10]{5,4,3,2,1,0:T(8,128)} reshape(f32[800,800]{1,0:T(8,128)} %copy-done.4) | data formatting | bytes 5120000 | tf_op jit(solution)/shard_map/while/body/eval_jaxpr/transpose(jvp())/reshape | solution.py:88
  1147.7 30.7 %add.839 = f32[800,800]{1,0:T(8,128)} reshape(f32[8,10,10,8,10,10]{5,4,3,2,1,0:T(8,128)} %broadcast_add_fusion.13) | data formatting | bytes 5120000 | tf_op jit(solution)/shard_map/while/body/eval_jaxpr/jvp()/add | solution.py:85
  1200.0 32.3 %reshape.1188 = f32[8,10,10,8,10,10]{5,4,3,2,1,0:T(8,128)} reshape(f32[800,800]{1,0:T(8,128)} %copy-done.4) | data formatting | bytes 5120000 | tf_op jit(solution)/shard_map/while/body/eval_jaxpr/transpose(jvp())/reshape | solution.py:88
  1288.6 30.7 %add.839 = f32[800,800]{1,0:T(8,128)} reshape(f32[8,10,10,8,10,10]{5,4,3,2,1,0:T(8,128)} %broadcast_add_fusion.13) | data formatting | bytes 5120000 | tf_op jit(solution)/shard_map/while/body/eval_jaxpr/jvp()/add | solution.py:85
  1340.9 32.3 %reshape.1188 = f32[8,10,10,8,10,10]{5,4,3,2,1,0:T(8,128)} reshape(f32[800,800]{1,0:T(8,128)} %copy-done.4) | data formatting | bytes 5120000 | tf_op jit(solution)/shard_map/while/body/eval_jaxpr/transpose(jvp())/reshape | solution.py:88
  1481.8 32.3 %reshape.1188 = f32[8,10,10,8,10,10]{5,4,3,2,1,0:T(8,128)} reshape(f32[800,800]{1,0:T(8,128)} %copy-done.4) | data formatting | bytes 5120000 | tf_op jit(solution)/shard_map/while/body/eval_jaxpr/transpose(jvp())/reshape | solution.py:88
  1622.6 32.3 %reshape.1188 = f32[8,10,10,8,10,10]{5,4,3,2,1,0:T(8,128)} reshape(f32[800,800]{1,0:T(8,128)} %copy-done.4) | data formatting | bytes 5120000 | tf_op jit(solution)/shard_map/while/body/eval_jaxpr/transpose(jvp())/reshape | solution.py:88
  1763.5 32.3 %reshape.1188 = f32[8,10,10,8,10,10]{5,4,3,2,1,0:T(8,128)} reshape(f32[800,800]{1,0:T(8,128)} %copy-done.4) | data formatting | bytes 5120000 | tf_op jit(solution)/shard_map/while/body/eval_jaxpr/transpose(jvp())/reshape | solution.py:88
  1904.4 32.3 %reshape.1188 = f32[8,10,10,8,10,10]{5,4,3,2,1,0:T(8,128)} reshape(f32[800,800]{1,0:T(8,128)} %copy-done.4) | data formatting | bytes 5120000 | tf_op jit(solution)/shard_map/while/body/eval_jaxpr/transpose(jvp())/reshape | solution.py:88
  2078.8 30.7 %broadcast_multiply_fusion.1 = (f32[1,8,10,10,3,8,96]{6,5,4,3,2,1,0:T(8,128)}, f32[1,8,10,10,3,8,96]{6,5,4,3,2,1,0:T(8,128)}, f32[1,8,10,10,3,8,96]{6,5,4,3,2,1,...) fusion(f32[1,8,10,10,3,8,96]{6,5,4,3,2,1,0:T(8,128)} %get-tuple, ...), kind=kLoop, calls=%fused_computation.204 | loop fusion | flops 16588800 | bytes 73738368 | tf_op jit(solution)/shard_map/transpose(jvp(vmap()))/mul | solution.py:49
  2109.7 57.5 %broadcast_multiply_fusion = (f32[1,8,10,10,3,8,96]{6,5,4,3,2,1,0:T(8,128)}, f32[1,8,10,10,3,8,96]{6,5,4,3,2,1,0:T(8,128)}, f32[1,8,10,10,3,8,96]{6,5,4,3,2,1,0:...) fusion(f32[1,8,10,10,3,8,96]{6,5,4,3,2,1,0:T(8,128)} %get-tuple, ...), kind=kLoop, calls=%fused_computation.203 | loop fusion | flops 33177600 | bytes 140103936 | tf_op jit(solution)/shard_map/transpose(jvp(vmap()))/mul | solution.py:49
  2167.3 70.2 %pad_add_fusion = f32[1,10,12,12,3,8,96]{6,5,4,3,2,1,0:T(8,128)} fusion(f32[1,8,10,10,3,8,96]{6,5,4,3,2,1,0:T(8,128)} %get-tuple-element.618, f32[1,8,10,10,3,8,96]{6,5,4,3,2,1,0:T(8,128)} %get-tuple-element.619, f32[1,8,10,10,3,8,96]{6,5,4,3,2,1,0:T(8,128)} %get-tuple-element.620, f32[1,8,10,10,3,8,96]{6,5,4,3,2,1,0:T(8,128)} %get-tuple-element.621, ...), kind=kLoop, calls=%fused_computation.139 | loop fusion | flops 66355200 | bytes 168099840 | tf_op jit(solution)/shard_map/transpose(jvp(vmap()))/add_any | solution.py:44
  2332.1 60.5 %multiply_reduce_fusion.28 = (f32[3,96]{1,0:T(4,128)S(1)}, f32[3,96]{1,0:T(4,128)S(1)}, f32[3,96]{1,0:T(4,128)S(1)}, f32[3,96]{1,0:T(4,128)S(1)}, f32[3,96]{1,0:...) fusion(f32[1,8,10,10,3,8,96]{6,5,4,3,2,1,0:T(8,128)} %get-tuple, ...), kind=kLoop, calls=%fused_computation.177 | loop fusion | flops 66350016 | bytes 14766336 | tf_op jit(solution)/shard_map/transpose(jvp(vmap()))/reduce_sum | solution.py:49
  2411.1 163.2 %reduce-scatter.23.cloned.1.call-done = f32[384,768]{1,0:T(8,128)} async-done(((f32[3072,768]{1,0:T(8,128)}), f32[384,768]{1,0:T(8,128)}) %reduce-scatter.23.cloned.1.call-update) | async-done | bytes 1179664 | tf_op jit(solution)/shard_map/reduce_scatter | solution.py:288
  2576.9 163.9 %reduce-scatter.19.cloned.1.call-done = f32[96,3072]{1,0:T(8,128)} async-done(((f32[768,3072]{1,0:T(8,128)}), f32[96,3072]{1,0:T(8,128)}) %reduce-scatter.19.cloned.1.call-update) | async-done | bytes 1179664 | tf_op jit(solution)/shard_map/reduce_scatter | solution.py:287
  2751.9 130.9 %all-reduce.65.cloned.1.call-done = (f32[768]{0:T(1024)}, f32[768]{0:T(1024)}, f32[2304]{0:T(1024)}, f32[3,27,96]{2,0,1:T(4,128)}, f32[3,96]{1,0:T(4,128)}, /*in...) async-done(((f32[768]{0:T(1024)}, f32[768]{0:T(1024)}, ...) | async-done | bytes 96784 | tf_op jit(solution)/shard_map/psum | solution.py:304
  (995 shorter events, 1783.5 us)
Async XLA Ops:
  7.3 76.5 %all-gather.6.cloned.1.call-start = ((), (), s32[]{:S(2)}) async-start(), calls=%async_computation.8 | async-start | bytes 3981312 | tf_op jit(solution)/shard_map/all_gather | solution.py:136
  17.6 757.6 %all-gather.8.cloned.1.call-start = ((), (), s32[]{:S(2)}) async-start(), calls=%async_computation.9 | async-start | bytes 1327104 | tf_op jit(solution)/shard_map/all_gather | solution.py:137
  25.0 755.1 %all-gather.10.cloned.1.call-start = ((), (), s32[]{:S(2)}) async-start(), calls=%async_computation.10 | async-start | bytes 5308416 | tf_op jit(solution)/shard_map/all_gather | solution.py:138
  34.3 755.1 %all-gather.12.cloned.1.call-start = ((), (), s32[]{:S(2)}) async-start(), calls=%async_computation.11 | async-start | bytes 5308416 | tf_op jit(solution)/shard_map/all_gather | solution.py:139
  42.5 2364.3 %reduce-scatter.17.cloned.1.call-start = ((), (), s32[]{:S(2)}) async-start(), calls=%async_computation.13 | async-start | bytes 2654208 | tf_op jit(solution)/shard_map/reduce_scatter | solution.py:286
  2167.2 241.5 %reduce-scatter.15.cloned.1.call-start = ((), (), s32[]{:S(2)}) async-start(), calls=%async_computation.12 | async-start | bytes 7962624 | tf_op jit(solution)/shard_map/reduce_scatter | solution.py:285
  2167.3 70.2 %copy-start.37 = (f32[8,10,10]{2,1,0:T(8,128)S(1)}, f32[8,10,10]{2,1,0:T(8,128)}, u32[]{:S(2)}) copy-start(f32[8,10,10]{2,1,0:T(8,128)} %fusion.98) | copy-start | bytes 9604
  2279.6 294.6 %reduce-scatter.23.cloned.1.call-start = ((), (), s32[]{:S(2)}) async-start(), calls=%async_computation.16 | async-start | bytes 10616832 | tf_op jit(solution)/shard_map/reduce_scatter | solution.py:288
  2302.2 438.6 %reduce-scatter.19.cloned.1.call-start = ((), (), s32[]{:S(2)}) async-start(), calls=%async_computation.14 | async-start | bytes 10616832 | tf_op jit(solution)/shard_map/reduce_scatter | solution.py:287
  2314.2 568.6 %all-reduce.65.cloned.1.call-start = ((), (), s32[]{:S(2)}) async-start(), calls=%async_computation.20 | async-start | bytes 290816 | tf_op jit(solution)/shard_map/psum | solution.py:304
  2332.0 60.5 %copy-start.116 = (f32[3,96]{1,0:T(4,128)S(1)}, f32[3,96]{1,0:T(4,128)}, u32[]{:S(2)}) copy-start(f32[3,96]{1,0:T(4,128)} %get-tuple-element.508) | copy-start | bytes 3460
  2332.0 60.5 %copy-start.117 = (f32[3,96]{1,0:T(4,128)S(1)}, f32[3,96]{1,0:T(4,128)}, u32[]{:S(2)}) copy-start(f32[3,96]{1,0:T(4,128)} %get-tuple-element.509) | copy-start | bytes 3460
  2332.0 60.6 %copy-start.118 = (f32[3,96]{1,0:T(4,128)S(1)}, f32[3,96]{1,0:T(4,128)}, u32[]{:S(2)}) copy-start(f32[3,96]{1,0:T(4,128)} %get-tuple-element.510) | copy-start | bytes 3460
  2332.0 60.6 %copy-start.119 = (f32[3,96]{1,0:T(4,128)S(1)}, f32[3,96]{1,0:T(4,128)}, u32[]{:S(2)}) copy-start(f32[3,96]{1,0:T(4,128)} %get-tuple-element.511) | copy-start | bytes 3460
  2332.1 60.6 %copy-start.120 = (f32[3,96]{1,0:T(4,128)S(1)}, f32[3,96]{1,0:T(4,128)}, u32[]{:S(2)}) copy-start(f32[3,96]{1,0:T(4,128)} %get-tuple-element.512) | copy-start | bytes 3460
  2332.1 60.6 %copy-start.121 = (f32[3,96]{1,0:T(4,128)S(1)}, f32[3,96]{1,0:T(4,128)}, u32[]{:S(2)}) copy-start(f32[3,96]{1,0:T(4,128)} %get-tuple-element.513) | copy-start | bytes 3460
  2332.1 60.6 %copy-start.122 = (f32[3,96]{1,0:T(4,128)S(1)}, f32[3,96]{1,0:T(4,128)}, u32[]{:S(2)}) copy-start(f32[3,96]{1,0:T(4,128)} %get-tuple-element.514) | copy-start | bytes 3460
  2332.1 60.6 %copy-start.123 = (f32[3,96]{1,0:T(4,128)S(1)}, f32[3,96]{1,0:T(4,128)}, u32[]{:S(2)}) copy-start(f32[3,96]{1,0:T(4,128)} %get-tuple-element.515) | copy-start | bytes 3460
  2406.7 336.3 %copy-start.135 = (f32[768]{0:T(1024)S(1)}, f32[768]{0:T(1024)}, u32[]{:S(2)}) copy-start(f32[768]{0:T(1024)} %param.50) | copy-start | bytes 9220
  2406.7 501.7 %reduce-scatter.27.cloned.1.call-start = ((), (), s32[]{:S(2)}) async-start(), calls=%async_computation.18 | async-start | bytes 245760
  2408.6 524.6 %reduce-scatter.25.cloned.1.call-start = ((), (), s32[]{:S(2)}) async-start(), calls=%async_computation.17 | async-start | bytes 737280
  2411.0 546.8 %reduce-scatter.29.cloned.1.call-start = ((), (), s32[]{:S(2)}) async-start(), calls=%async_computation.19 | async-start | bytes 737280
  2576.6 406.0 %reduce-scatter.21.cloned.1.call-start = ((), (), s32[]{:S(2)}) async-start(), calls=%async_computation.15 | async-start | bytes 737280 | tf_op jit(solution)/shard_map/reduce_scatter | solution.py:297
  2743.0 256.5 %copy-start.1 = (f32[15,96]{1,0:T(8,128)S(1)}, f32[15,96]{1,0:T(8,128)}, u32[]{:S(2)}) copy-start(f32[15,96]{1,0:T(8,128)} %param.40) | copy-start | bytes 17284
  (174 other events, 2591.3 us)
Sparse Core Ops, SparseCore 0:
  17.7 66.0 all-gather.5
  86.5 39.5 all-gather.7
  128.3 78.6 all-gather.9
  208.9 79.1 all-gather.11
  2167.3 67.6 reduce-scatter.16
  2279.7 127.8 reduce-scatter.14
  2411.6 162.5 reduce-scatter.22
  2578.2 162.5 reduce-scatter.18
  2750.1 132.6 all-reduce.64
  2885.8 22.5 reduce-scatter.26
  2911.1 22.0 reduce-scatter.24
  2935.7 22.0 reduce-scatter.28
  2960.5 22.0 reduce-scatter.20
where the time goes:
time: 3020 us; the launch traced here: 3010 us
  other arithmetic  1070 us (35%)
  local copies, waits for them, and re-layouts  1030 us (34%)
  waiting for transfers between devices  555 us (18%)
  matrix products  297 us (10%)
  blocking collectives  31.8 us (1%)
    add x16, local copies, waits for them, and re-layouts, score_terms(): along_time[:, :, :, :, None, None] + along_height[:, :, :, None, :, None]  491 us
    add x32, other arithmetic, score_terms(): along_time[:, :, :, :, None, None] + along_height[:, :, :, None, :, None]  299 us
    reshape x8, local copies, waits for them, and re-layouts, score_terms(): relative = (along_time[:, :, :, :, None, None] + along_height[:, :, :, No...  259 us
    reduce_scatter x1, waiting for transfers between devices, on_device(): lax.psum_scatter(grad_one, 'dp', scatter_dimension=0, tiled=True)  164 us
    reduce_scatter x1, waiting for transfers between devices, on_device(): lax.psum_scatter(grad_two, 'dp', scatter_dimension=0, tiled=True)  163 us
    reduce_sum x8, other arithmetic, score_terms(): along_time[:, :, :, :, None, None] + along_height[:, :, :, None, :, None]  156 us
    psum x1, waiting for transfers between devices, on_device(): lax.psum((grad_first_gain, grad_first_bias, grad_qkv_bias, grad_conv, gra...  131 us
    reduce_sum x2, other arithmetic, pool_clip(): pooled = pooled + window * pool_conv[:, offset, :][:, None, :]  90.9 us
  transfers between devices with their start and end apart: 13, of which 8 were waited for; matrix products, arithmetic and copies ran while one was open for 33% of the time, Pallas kernels for 0%

commit v1 on v0

v1 whole, which is shorter than its diff:
```python
import functools

import jax
import jax.numpy as jnp
import numpy as np
from jax import lax
from jax.experimental import pallas as pl
from jax.experimental.pallas import tpu as pltpu
from jax.sharding import PartitionSpec as P

D = 768
FF = 3072
HEADS = 8
HEAD_DIM = 96
LANES = 128
FRAMES = 8
HEIGHT = 10
WIDTH = 10
PLACES = HEIGHT * WIDTH
ROWS = 800
MEM = 200
GROUP = 384
GROUP_HEADS = 4
QKV = 3 * D
KEY_ROWS = 1280
MEM_AT = 800
SQUEEZE_AT = 1024
REST = KEY_ROWS - ROWS
TABLE = 384
EPSILON = 1e-06
SCALE = HEAD_DIM**-0.5
ROOT = HEAD_DIM**0.5
LOG2E = 1.4426950408889634
MASKED = -1e9
MASK_LANE = 124
ROW_BLOCK = 160
BF16 = jnp.bfloat16
F32 = jnp.float32
VMEM_LIMIT = 60 * 1024 * 1024


def constants():
    place = np.arange(PLACES).repeat(FRAMES)
    row_t = np.tile(np.arange(FRAMES), PLACES)
    row_i, row_j = place // WIDTH, place % WIDTH
    one_hot = np.zeros((KEY_ROWS, LANES), np.float32)
    rows = np.arange(ROWS)
    one_hot[rows, 96 + row_t] = 1
    one_hot[rows, 104 + row_i] = 1
    one_hot[rows, 114 + row_j] = 1
    own = np.zeros((ROWS, TABLE), np.float32)
    fold = np.zeros((TABLE, LANES), np.float32)
    pick = np.zeros((TABLE, LANES), np.float32)
    for base, length, row_at, lane, offset in (
        (0, FRAMES, row_t, 96, 0),
        (64, HEIGHT, row_i, 104, 15),
        (164, WIDTH, row_j, 114, 34),
    ):
        for a in range(length):
            for b in range(length):
                column = base + a * length + b
                own[:, column] = row_at == a
                fold[column, lane + b] = 1
                pick[column, offset + a - b + length - 1] = 1
    return one_hot, own, fold, pick


def lane_index(shape):
    return lax.broadcasted_iota(jnp.int32, shape, len(shape) - 1)


def dot(a, b, contract=((1,), (0,)), precision=None):
    return lax.dot_general(a, b, (contract, ((), ())), preferred_element_type=F32, precision=precision)


def layer_stats(values, width):
    average = jnp.sum(values, axis=-1, keepdims=True) * (1.0 / width)
    centred = values - average
    variance = jnp.sum(centred * centred, axis=-1, keepdims=True) * (1.0 / width)
    return centred, lax.rsqrt(variance + EPSILON)


def params(**more):
    return pltpu.CompilerParams(vmem_limit_bytes=VMEM_LIMIT, **more)


def whole(shape):
    return pl.BlockSpec(shape, lambda *_: (0,) * len(shape))


def tiles_of(values):
    return [values[:, at : at + LANES] for at in range(0, values.shape[1], LANES)]


def read_place(wide_ref, place):
    parts = [wide_ref[tile, pl.ds(place, FRAMES, stride=PLACES), :] for tile in range(wide_ref.shape[0])]
    return jnp.concatenate(parts, axis=1)


def write_place(wide_ref, place, values):
    for tile, part in enumerate(tiles_of(values)):
        wide_ref[tile, pl.ds(place, FRAMES, stride=PLACES), :] = part


def wide_scratch(columns):
    return pltpu.VMEM((columns // LANES, ROWS, LANES), F32)


def prepare_kernel(
    frames_ref, length_ref, tokens_ref, cot_ref, gain_ref, bias_ref, one_hot_ref, tables_ref, pick_ref,
    x_ref, normed_ref, upstream_ref, aug_ref, table_ref, wide_ref,
):
    def permute(source_ref, target_ref):
        for tile, part in enumerate(tiles_of(source_ref[...])):
            wide_ref[tile] = part.astype(F32)

        @pl.loop(0, PLACES // 2)
        def _(pair):
            first = read_place(wide_ref, 2 * pair)
            second = read_place(wide_ref, 2 * pair + 1)
            at = pl.multiple_of(pair * 16, 16)
            target_ref[pl.ds(at, 16), :] = jnp.concatenate([first, second], axis=0).astype(BF16)

    permute(cot_ref, upstream_ref)
    permute(tokens_ref, x_ref)
    centred, rs = layer_stats(x_ref[...].astype(F32), D)
    normed_ref[...] = (centred * rs * gain_ref[...] + bias_ref[...]).astype(BF16)
    row = lax.broadcasted_iota(jnp.int32, (KEY_ROWS, LANES), 0)
    frames, length = frames_ref[0], length_ref[0]
    place = jnp.where(row < MEM_AT, row & 7, jnp.where(row < SQUEEZE_AT, row - MEM_AT, row - SQUEEZE_AT))
    limit = jnp.where(row < MEM_AT, frames, jnp.where(row < SQUEEZE_AT, length, MEM))
    off = jnp.where(place >= limit, jnp.where(lane_index((KEY_ROWS, LANES)) == MASK_LANE, MASKED, 0.0), 0.0)
    aug_ref[...] = (one_hot_ref[...].astype(F32) + off).astype(BF16)
    table_ref[...] = dot(pick_ref[...], tables_ref[...].astype(BF16)).astype(BF16)


def prepare(frames, length, tokens, cot, gain, bias, one_hot, tables, pick):
    smem = pl.BlockSpec(memory_space=pltpu.SMEM)
    vmem = pl.BlockSpec(memory_space=pltpu.VMEM)
    return pl.pallas_call(
        prepare_kernel,
        out_shape=(
            jax.ShapeDtypeStruct((ROWS, D), BF16),
            jax.ShapeDtypeStruct((ROWS, D), BF16),
            jax.ShapeDtypeStruct((ROWS, D), BF16),
            jax.ShapeDtypeStruct((KEY_ROWS, LANES), BF16),
            jax.ShapeDtypeStruct((TABLE, LANES), BF16),
        ),
        in_specs=[smem, smem] + [vmem] * 7,
        out_specs=(vmem,) * 5,
        scratch_shapes=[wide_scratch(D)],
        compiler_params=params(),
        name="prepare",
    )(frames, length, tokens, cot, gain, bias, one_hot, tables, pick)


def squeeze_kernel(prev_ref, mem_ref, taps_ref, rest_ref, tap_ref, wide_ref, sums_ref, parts_ref):
    for tile, part in enumerate(tiles_of(prev_ref[0])):
        wide_ref[tile] = part.astype(F32)

    @pl.loop(0, HEIGHT // 2)
    def _(i):
        for j in range(WIDTH // 2):
            total = None
            at = pl.multiple_of((i * (WIDTH // 2) + j) * FRAMES, FRAMES)
            for tap in range(4):
                place = (2 * i + tap // 2) * WIDTH + 2 * j + tap % 2
                part = read_place(wide_ref, place)
                parts_ref[tap, pl.ds(at, FRAMES), :] = part
                term = part * taps_ref[0, tap : tap + 1, :]
                total = term if total is None else total + term
            sums_ref[pl.ds(at, FRAMES), :] = total

    def head_of(values, head):
        return values[:, HEAD_DIM * head : HEAD_DIM * head + HEAD_DIM]

    old = mem_ref[0].astype(F32)
    for head in range(GROUP_HEADS):
        rest = jnp.concatenate(
            [
                head_of(old, head),
                jnp.zeros((SQUEEZE_AT - MEM_AT - MEM, HEAD_DIM), F32),
                head_of(sums_ref[...], head),
                jnp.zeros((KEY_ROWS - SQUEEZE_AT - MEM, HEAD_DIM), F32),
            ],
            axis=0,
        )
        rest = jnp.concatenate([rest, jnp.zeros((REST, LANES - HEAD_DIM), F32)], axis=1)
        rest_ref[0, head] = rest.astype(BF16)
        for tap in range(4):
            part = jnp.concatenate([head_of(parts_ref[tap], head), jnp.zeros((8, HEAD_DIM), F32)], axis=0)
            part = jnp.concatenate([part, jnp.zeros((208, LANES - HEAD_DIM), F32)], axis=1)
            tap_ref[0, head, tap] = part.astype(BF16)


def squeeze(prev, memory, taps):
    return pl.pallas_call(
        squeeze_kernel,
        grid=(2, 2),
        out_shape=(
            jax.ShapeDtypeStruct((2, HEADS, REST, LANES), BF16),
            jax.ShapeDtypeStruct((2, HEADS, 4, 208, LANES), BF16),
        ),
        in_specs=[
            pl.BlockSpec((1, ROWS, GROUP), lambda s, g: (s, 0, g)),
            pl.BlockSpec((1, MEM, GROUP), lambda s, g: (s, 0, g)),
            pl.BlockSpec((1, 4, GROUP), lambda s, g: (s, 0, 0)),
        ],
        out_specs=(
            pl.BlockSpec((1, GROUP_HEADS, REST, LANES), lambda s, g: (s, g, 0, 0)),
            pl.BlockSpec((1, GROUP_HEADS, 4, 208, LANES), lambda s, g: (s, g, 0, 0, 0)),
        ),
        scratch_shapes=[
            wide_scratch(GROUP),
            pltpu.VMEM((MEM, GROUP), F32),
            pltpu.VMEM((4, MEM, GROUP), F32),
        ],
        compiler_params=params(),
        name="squeeze",
    )(prev, memory, taps)


def shift_frames(values, step):
    frame = lax.broadcasted_iota(jnp.int32, values.shape, values.ndim - 2)
    moved = pltpu.roll(values, step % FRAMES, values.ndim - 2)
    edge = 0 if step == 1 else FRAMES - 1
    return jnp.where(frame == edge, 0.0, moved)


def convolve(grid_ref, taps_ref, flip, i, lanes):
    sums = [None, None, None]
    for b in range(3):
        for e in range(3):
            window = grid_ref[i + b, e : e + WIDTH, :, lanes]
            for a in range(3):
                tap = 9 * a + 3 * b + e
                term = window * taps_ref[0, 26 - tap if flip else tap, :, lanes][None]
                sums[a] = term if sums[a] is None else sums[a] + term
    return sums[1] + shift_frames(sums[0], 1) + shift_frames(sums[2], -1)


def clear_border(grid_ref):
    grid_ref[...] = jnp.zeros(grid_ref.shape, grid_ref.dtype)


def qkv_kernel(
    frames_ref, normed_ref, shards_ref, qkv_bias_ref, taps_ref, gain_ref, bias_ref,
    heads_ref, vhat_ref, mixed_ref, weight_ref, grid_ref, pooled_ref,
):
    step = pl.program_id(0)

    @pl.when(step == 0)
    def _():
        clear_border(grid_ref)
        columns = shards_ref.shape[3]
        for f in range(shards_ref.shape[1]):
            weight_ref[:, f * columns : (f + 1) * columns] = shards_ref[:, f].reshape(D, columns)

    at = pl.multiple_of(step * GROUP, LANES)
    mixed = dot(normed_ref[...], weight_ref[:, pl.ds(at, GROUP)]) + qkv_bias_ref[...]
    row = lax.broadcasted_iota(jnp.int32, (ROWS, GROUP), 0)
    mixed = jnp.where((row & 7) < frames_ref[0], mixed, 0.0)
    mixed_ref[...] = mixed.astype(BF16)
    grid_ref[1 : HEIGHT + 1, 1 : WIDTH + 1] = mixed.reshape(HEIGHT, WIDTH, FRAMES, GROUP)

    @pl.loop(0, HEIGHT)
    def _(i):
        for tile in range(GROUP // LANES):
            lanes = slice(tile * LANES, tile * LANES + LANES)
            line = convolve(grid_ref, taps_ref, False, i, lanes)
            at = pl.multiple_of(i * WIDTH * FRAMES, WIDTH * FRAMES)
            pooled_ref[pl.ds(at, WIDTH * FRAMES), lanes] = line.reshape(WIDTH * FRAMES, LANES)

    lane = lane_index((ROWS, LANES))
    for head in range(GROUP_HEADS):
        values = pooled_ref[:, HEAD_DIM * head : HEAD_DIM * head + LANES]
        values = jnp.where(lane < HEAD_DIM, values, 0.0)
        average = jnp.sum(values, axis=-1, keepdims=True) * (1.0 / HEAD_DIM)
        centred = jnp.where(lane < HEAD_DIM, values - average, 0.0)
        variance = jnp.sum(centred * centred, axis=-1, keepdims=True) * (1.0 / HEAD_DIM)
        rs = lax.rsqrt(variance + EPSILON)
        vhat = centred * rs
        heads_ref[head] = (vhat * gain_ref[0] + bias_ref[0]).astype(BF16)
        high = rs.astype(BF16).astype(F32)
        extra = jnp.where(lane == HEAD_DIM, high, jnp.where(lane == HEAD_DIM + 1, rs - high, 0.0))
        vhat_ref[head] = (vhat + extra).astype(BF16)


def query_key_value(frames, normed, shards, qkv_bias, taps, gain, bias):
    smem = pl.BlockSpec(memory_space=pltpu.SMEM)
    return pl.pallas_call(
        qkv_kernel,
        grid=(6,),
        out_shape=(
            jax.ShapeDtypeStruct((3 * HEADS, ROWS, LANES), BF16),
            jax.ShapeDtypeStruct((3 * HEADS, ROWS, LANES), BF16),
            jax.ShapeDtypeStruct((ROWS, QKV), BF16),
            jax.ShapeDtypeStruct((D, QKV), BF16),
        ),
        in_specs=[
            smem,
            whole((ROWS, D)),
            whole(shards.shape),
            pl.BlockSpec((1, GROUP), lambda g: (0, g)),
            pl.BlockSpec((1, 27, 8, GROUP), lambda g: (g // 2, 0, 0, 0)),
            pl.BlockSpec((1, 1, LANES), lambda g: (g // 2, 0, 0)),
            pl.BlockSpec((1, 1, LANES), lambda g: (g // 2, 0, 0)),
        ],
        out_specs=(
            pl.BlockSpec((GROUP_HEADS, ROWS, LANES), lambda g: (g, 0, 0)),
            pl.BlockSpec((GROUP_HEADS, ROWS, LANES), lambda g: (g, 0, 0)),
            pl.BlockSpec((ROWS, GROUP), lambda g: (0, g)),
            whole((D, QKV)),
        ),
        scratch_shapes=[
            pltpu.VMEM((HEIGHT + 2, WIDTH + 2, FRAMES, GROUP), F32),
            pltpu.VMEM((ROWS, GROUP + LANES), F32),
        ],
        compiler_params=params(),
        name="query_key_value",
    )(frames, normed, shards, qkv_bias, taps, gain, bias)


def attend_kernel(
    q_ref, k_ref, v_ref, krest_ref, vrest_ref, aug_ref, table_ref, own_ref, fold_ref,
    weights_ref, pv_ref, out_ref, keys_ref, vals_ref, query_ref,
):
    lane = lane_index((KEY_ROWS, LANES))
    keys_ref[:ROWS] = k_ref[0] + aug_ref[:ROWS]
    keys_ref[ROWS:] = krest_ref[0, 0] + aug_ref[ROWS:]
    one = jnp.where(lane == HEAD_DIM, 1.0, 0.0).astype(BF16)
    vals_ref[:ROWS] = v_ref[0] + one[:ROWS]
    vals_ref[ROWS:] = vrest_ref[0, 0] + one[ROWS:]
    query = q_ref[0]
    every = (dot(query, table_ref[...], ((1,), (1,))) * ROOT).astype(BF16) * own_ref[...]
    relative = dot(every, fold_ref[...])
    marked = jnp.where(lane[:ROWS] == MASK_LANE, 1.0, relative)
    query_ref[...] = (query.astype(F32) + marked).astype(BF16)

    @pl.loop(0, ROWS // ROW_BLOCK)
    def _(block):
        rows = pl.ds(pl.multiple_of(block * ROW_BLOCK, ROW_BLOCK), ROW_BLOCK)
        scores = dot(query_ref[rows, :], keys_ref[...], ((1,), (1,)))
        largest = jnp.max(scores, axis=1, keepdims=True)
        weights = jnp.exp2((scores - largest) * (SCALE * LOG2E)).astype(BF16)
        weights_ref[0, rows, :] = weights
        total = dot(weights, vals_ref[...])
        inverse = 1.0 / total[:, HEAD_DIM : HEAD_DIM + 1]
        lane = lane_index((ROW_BLOCK, LANES))
        pv = jnp.where(lane < HEAD_DIM, total * inverse, 0.0)
        out_ref[0, rows, :] = (pv + q_ref[0, rows, :].astype(F32)).astype(BF16)
        high = inverse.astype(BF16).astype(F32)
        extra = jnp.where(lane == HEAD_DIM, high, jnp.where(lane == HEAD_DIM + 1, inverse - high, 0.0))
        pv_ref[0, rows, :] = (pv + extra).astype(BF16)


def attend(heads, rest, aug, table, own, fold):
    head = (1, ROWS, LANES)
    tail = (1, 1, REST, LANES)
    return pl.pallas_call(
        attend_kernel,
        grid=(HEADS,),
        out_shape=(
            jax.ShapeDtypeStruct((HEADS, ROWS, KEY_ROWS), BF16),
            jax.ShapeDtypeStruct((HEADS, ROWS, LANES), BF16),
            jax.ShapeDtypeStruct((HEADS, ROWS, LANES), BF16),
        ),
        in_specs=[
            pl.BlockSpec(head, lambda h: (h, 0, 0)),
            pl.BlockSpec(head, lambda h: (HEADS + h, 0, 0)),
            pl.BlockSpec(head, lambda h: (2 * HEADS + h, 0, 0)),
            pl.BlockSpec(tail, lambda h: (0, h, 0, 0)),
            pl.BlockSpec(tail, lambda h: (1, h, 0, 0)),
            whole((KEY_ROWS, LANES)),
            whole((TABLE, LANES)),
            whole((ROWS, TABLE)),
            whole((TABLE, LANES)),
        ],
        out_specs=(
            pl.BlockSpec((1, ROWS, KEY_ROWS), lambda h: (h, 0, 0)),
            pl.BlockSpec(head, lambda h: (h, 0, 0)),
            pl.BlockSpec(head, lambda h: (h, 0, 0)),
        ),
        scratch_shapes=[
            pltpu.VMEM((KEY_ROWS, LANES), BF16),
            pltpu.VMEM((KEY_ROWS, LANES), BF16),
            pltpu.VMEM((ROWS, LANES), BF16),
        ],
        compiler_params=params(),
        name="attend",
    )(heads, heads, heads, rest, rest, aug, table, own, fold)


CHUNK = 384
CHUNKS = FF // CHUNK


def middle_kernel(
    att_ref, x_ref, up_ref, wp_ref, w1_ref, w2_ref, pb_ref, g2_ref, b2_ref, fb1_ref, fb2_ref,
    out_ref, dmid_ref, datt_ref, gp_ref, gw1_ref, gw2_ref, small_ref, gb1_ref,
    packed_ref, proj_ref, mid_ref, hidden_ref, total_ref, dhid_ref, wide_ref,
):
    step = pl.program_id(0)
    sides = wp_ref.shape[1]
    part = D // sides

    @pl.when(step == 0)
    def _():
        for head in range(HEADS):
            packed_ref[:, HEAD_DIM * head : HEAD_DIM * (head + 1)] = att_ref[head][:, :HEAD_DIM]
        for f in range(sides):
            proj_ref[:, f * part : (f + 1) * part] = wp_ref[:, f].reshape(D, part)
        middle = x_ref[...].astype(F32) + dot(packed_ref[...], proj_ref[...]) + pb_ref[...]
        mid_ref[...] = middle
        centred, rs = layer_stats(middle, D)
        hidden_ref[...] = (centred * rs * g2_ref[...] + b2_ref[...]).astype(BF16)
        total_ref[...] = middle + fb2_ref[...]
        dhid_ref[...] = jnp.zeros((ROWS, D), F32)

    w1 = w1_ref[:, 0].reshape(D, CHUNK)
    w2 = jnp.concatenate([w2_ref[0, f] for f in range(sides)], axis=1)
    before = dot(hidden_ref[...], w1) + fb1_ref[...]
    erf = lax.erf(before * (2.0**-0.5))
    cdf = 0.5 * (1.0 + erf)
    activated = (before * cdf).astype(BF16)
    slope = cdf + before * (jnp.exp(before * before * -0.5) * 0.3989422804014327)
    dbefore = dot(up_ref[...], w2, ((1,), (1,))) * slope
    dbefore_low = dbefore.astype(BF16)
    gb1_ref[...] = jnp.sum(dbefore_low.astype(F32), axis=0, keepdims=True)
    total_ref[...] += dot(activated, w2)
    grad_two = dot(activated, up_ref[...], ((0,), (0,))).astype(BF16)
    for f in range(sides):
        gw2_ref[0, f] = grad_two[:, f * part : (f + 1) * part]
    dhid_ref[...] += dot(dbefore_low, w1, ((1,), (1,)))
    gw1_ref[:, 0] = dot(hidden_ref[...], dbefore_low, ((0,), (0,))).astype(BF16).reshape(gw1_ref.shape[0], -1, CHUNK)

    @pl.when(step == CHUNKS - 1)
    def _():
        @pl.loop(0, PLACES)
        def _(place):
            at = pl.multiple_of(place * FRAMES, FRAMES)
            write_place(wide_ref, place, total_ref[pl.ds(at, FRAMES), :])

        for tile in range(D // LANES):
            out_ref[:, tile * LANES : (tile + 1) * LANES] = wide_ref[tile].astype(BF16)
        upstream = up_ref[...].astype(F32)
        dhidden = dhid_ref[...]
        centred, rs = layer_stats(mid_ref[...], D)
        vhat = centred * rs
        dgain = jnp.sum(dhidden * vhat, axis=0, keepdims=True)
        dbias = jnp.sum(dhidden, axis=0, keepdims=True)
        scaled = dhidden * g2_ref[...]
        first = jnp.sum(scaled, axis=1, keepdims=True) * (1.0 / D)
        second = jnp.sum(scaled * vhat, axis=1, keepdims=True) * (1.0 / D)
        dmiddle = upstream + rs * (scaled - first - vhat * second)
        dmid_ref[...] = dmiddle
        dproj = dmiddle.astype(BF16)
        small_ref[0:1, :] = jnp.sum(dproj.astype(F32), axis=0, keepdims=True)
        small_ref[1:2, :] = dgain
        small_ref[2:3, :] = dbias
        small_ref[3:4, :] = jnp.sum(upstream, axis=0, keepdims=True)
        small_ref[4:8, :] = jnp.zeros((4, D), F32)
        grad_proj = dot(packed_ref[...], dproj, ((0,), (0,))).astype(BF16)
        for f in range(sides):
            gp_ref[:, f] = grad_proj[:, f * part : (f + 1) * part].reshape(gp_ref.shape[0], -1, part)
        datt = dot(dproj, proj_ref[...], ((1,), (1,))).astype(BF16)
        for head in range(HEADS):
            datt_ref[head] = jnp.concatenate(
                [datt[:, HEAD_DIM * head : HEAD_DIM * (head + 1)], jnp.zeros((ROWS, LANES - HEAD_DIM), BF16)],
                axis=1,
            )


def feed_forward(att, x, up, wp, w1, w2, pb, g2, b2, fb1, fb2):
    once = pl.Buffered(1)

    def kept(shape):
        return pl.BlockSpec(shape, lambda *_: (0,) * len(shape), pipeline_mode=once)

    w1_block = (w1.shape[0], 1, w1.shape[2], CHUNK)
    w2_block = (1,) + w2.shape[1:]
    w1_spec = pl.BlockSpec(w1_block, lambda c: (0, c // 2, 0, c % 2))
    w2_spec = pl.BlockSpec(w2_block, lambda c: (c, 0, 0, 0))
    return pl.pallas_call(
        middle_kernel,
        grid=(CHUNKS,),
        out_shape=(
            jax.ShapeDtypeStruct((ROWS, D), BF16),
            jax.ShapeDtypeStruct((ROWS, D), F32),
            jax.ShapeDtypeStruct((HEADS, ROWS, LANES), BF16),
            jax.ShapeDtypeStruct(wp.shape, BF16),
            jax.ShapeDtypeStruct(w1.shape, BF16),
            jax.ShapeDtypeStruct(w2.shape, BF16),
            jax.ShapeDtypeStruct((8, D), F32),
            jax.ShapeDtypeStruct((1, FF), F32),
        ),
        in_specs=[
            kept((HEADS, ROWS, LANES)),
            kept((ROWS, D)),
            kept((ROWS, D)),
            kept(wp.shape),
            w1_spec,
            w2_spec,
            kept((1, D)),
            kept((1, D)),
            kept((1, D)),
            pl.BlockSpec((1, CHUNK), lambda c: (0, c)),
            kept((1, D)),
        ],
        out_specs=(
            kept((ROWS, D)),
            kept((ROWS, D)),
            kept((HEADS, ROWS, LANES)),
            kept(wp.shape),
            w1_spec,
            w2_spec,
            kept((8, D)),
            pl.BlockSpec((1, CHUNK), lambda c: (0, c)),
        ),
        scratch_shapes=[
            pltpu.VMEM((ROWS, D), BF16),
            pltpu.VMEM((D, D), BF16),
            pltpu.VMEM((ROWS, D), F32),
            pltpu.VMEM((ROWS, D), BF16),
            pltpu.VMEM((ROWS, D), F32),
            pltpu.VMEM((ROWS, D), F32),
            wide_scratch(D),
        ],
        compiler_params=params(),
        name="feed_forward",
    )(att, x, up, wp, w1, w2, pb, g2, b2, fb1, fb2)


def attend_back_kernel(
    q_ref, k_ref, v_ref, krest_ref, vrest_ref, aug_ref, table_ref, own_ref, fold_ref, pick_ref,
    weights_ref, pv_ref, datt_ref, parts_ref,
    grads_ref, gtable_ref, gtaps_ref,
    keys_ref, vals_ref, up_ref, slopes_ref, gsum_ref,
):
    step = pl.program_id(0)
    lane = lane_index((KEY_ROWS, LANES))
    row_lane = lane[:ROWS]

    @pl.when(step == 0)
    def _():
        gsum_ref[...] = jnp.zeros((TABLE, LANES), F32)
        gtaps_ref[...] = jnp.zeros((2, 4, LANES), F32)

    keys_ref[:ROWS] = k_ref[0] + aug_ref[:ROWS]
    keys_ref[ROWS:] = krest_ref[0, 0] + aug_ref[ROWS:]
    one = jnp.where((lane >= HEAD_DIM) & (lane < HEAD_DIM + 3), 1.0, 0.0).astype(BF16)
    vals_ref[:ROWS] = v_ref[0] + one[:ROWS]
    vals_ref[ROWS:] = vrest_ref[0, 0] + one[ROWS:]
    pv = pv_ref[0].astype(F32)
    inverse = pv[:, HEAD_DIM : HEAD_DIM + 1] + pv[:, HEAD_DIM + 1 : HEAD_DIM + 2]
    datt = datt_ref[0].astype(F32)
    upstream = (datt * inverse).astype(BF16).astype(F32)
    mean = jnp.sum(upstream * pv, axis=1, keepdims=True)
    high = mean.astype(BF16).astype(F32)
    low = (mean - high).astype(BF16).astype(F32)
    least = mean - high - low
    extra = jnp.where(
        row_lane == HEAD_DIM,
        -high,
        jnp.where(row_lane == HEAD_DIM + 1, -low, jnp.where(row_lane == HEAD_DIM + 2, -least, 0.0)),
    )
    up_ref[...] = (upstream + extra).astype(BF16)

    @pl.loop(0, ROWS // ROW_BLOCK)
    def _(block):
        rows = pl.ds(pl.multiple_of(block * ROW_BLOCK, ROW_BLOCK), ROW_BLOCK)
        dprobs = dot(up_ref[rows, :], vals_ref[...], ((1,), (1,)))
        slopes_ref[rows, :] = (weights_ref[0, rows, :].astype(F32) * dprobs).astype(BF16)

    dvals = dot(weights_ref[0], up_ref[...], ((0,), (0,)))
    dkeys = dot(slopes_ref[...], q_ref[0], ((0,), (0,))) * SCALE
    dquery = dot(slopes_ref[...], keys_ref[...])
    spread = dot(dquery.astype(BF16), fold_ref[...], ((1,), (1,))).astype(BF16) * own_ref[...]
    gsum_ref[...] += dot(spread, q_ref[0], ((0,), (0,)))
    dquery = dquery * SCALE + datt + dot(spread, table_ref[...])
    grads_ref[0, 0] = dquery.astype(BF16)
    grads_ref[1, 0] = dkeys[:ROWS].astype(BF16)
    grads_ref[2, 0] = dvals[:ROWS].astype(BF16)
    for s, whole_grad in ((0, dkeys), (1, dvals)):
        piece = whole_grad[SQUEEZE_AT : SQUEEZE_AT + MEM]
        for tap in range(4):
            product = piece * parts_ref[s, 0, tap].astype(F32)[:MEM]
            gtaps_ref[s, tap : tap + 1, :] += jnp.sum(product, axis=0, keepdims=True)

    @pl.when(step == HEADS - 1)
    def _():
        gtable_ref[...] = dot(pick_ref[...], gsum_ref[...], ((0,), (0,)), lax.Precision.HIGHEST)


def attend_back(heads, rest, aug, table, own, fold, pick, weights, pv, datt, parts):
    head = (1, ROWS, LANES)
    tail = (1, 1, REST, LANES)
    own_head = pl.BlockSpec(head, lambda h: (h, 0, 0))
    return pl.pallas_call(
        attend_back_kernel,
        grid=(HEADS,),
        out_shape=(
            jax.ShapeDtypeStruct((3, HEADS, ROWS, LANES), BF16),
            jax.ShapeDtypeStruct((LANES, LANES), F32),
            jax.ShapeDtypeStruct((2, 4, LANES), F32),
        ),
        in_specs=[
            own_head,
            pl.BlockSpec(head, lambda h: (HEADS + h, 0, 0)),
            pl.BlockSpec(head, lambda h: (2 * HEADS + h, 0, 0)),
            pl.BlockSpec(tail, lambda h: (0, h, 0, 0)),
            pl.BlockSpec(tail, lambda h: (1, h, 0, 0)),
            whole((KEY_ROWS, LANES)),
            whole((TABLE, LANES)),
            whole((ROWS, TABLE)),
            whole((TABLE, LANES)),
            whole((TABLE, LANES)),
            pl.BlockSpec((1, ROWS, KEY_ROWS), lambda h: (h, 0, 0)),
            own_head,
            own_head,
            pl.BlockSpec((2, 1, 4, 208, LANES), lambda h: (0, h, 0, 0, 0)),
        ],
        out_specs=(
            pl.BlockSpec((3, 1, ROWS, LANES), lambda h: (0, h, 0, 0)),
            whole((LANES, LANES)),
            whole((2, 4, LANES)),
        ),
        scratch_shapes=[
            pltpu.VMEM((KEY_ROWS, LANES), BF16),
            pltpu.VMEM((KEY_ROWS, LANES), BF16),
            pltpu.VMEM((ROWS, LANES), BF16),
            pltpu.VMEM((ROWS, KEY_ROWS), BF16),
            pltpu.VMEM((TABLE, LANES), F32),
        ],
        compiler_params=params(),
        name="attend_back",
    )(heads, heads, heads, rest, rest, aug, table, own, fold, pick.astype(F32), weights, pv, datt, parts)


def qkv_back_kernel(
    frames_ref, grads_ref, vhat_ref, mixed_ref, weight_ref, normed_ref, x_ref, dmid_ref, taps_ref, gain_ref, g1_ref,
    gtok_ref, gqkv_ref, gbias_ref, gtaps_ref, gpool_ref, small_ref,
    grid_ref, dgrid_ref, dpool_ref, dmix_ref, dnorm_ref, sums_ref, wide_ref,
):
    step = pl.program_id(0)

    @pl.when(step == 0)
    def _():
        clear_border(grid_ref)
        clear_border(dgrid_ref)
        dnorm_ref[...] = jnp.zeros((ROWS, D), F32)

    lane = lane_index((ROWS, LANES))
    for head in range(GROUP_HEADS):
        dy = grads_ref[0, head].astype(F32)
        dy = jnp.where(lane < HEAD_DIM, dy, 0.0)
        vhat = vhat_ref[head].astype(F32)
        rs = vhat[:, HEAD_DIM : HEAD_DIM + 1] + vhat[:, HEAD_DIM + 1 : HEAD_DIM + 2]
        product = dy * vhat
        gpool_ref[head, 0:1, :] = jnp.sum(product, axis=0, keepdims=True)
        gpool_ref[head, 1:2, :] = jnp.sum(dy, axis=0, keepdims=True)
        scaled = dy * gain_ref[0]
        first = jnp.sum(scaled, axis=1, keepdims=True) * (1.0 / HEAD_DIM)
        second = jnp.sum(product * gain_ref[0], axis=1, keepdims=True) * (1.0 / HEAD_DIM)
        dpool = rs * (scaled - first - vhat * second)
        dpool_ref[:, HEAD_DIM * head : HEAD_DIM * (head + 1)] = dpool[:, :HEAD_DIM]
    dgrid_ref[1 : HEIGHT + 1, 1 : WIDTH + 1] = dpool_ref[...].reshape(HEIGHT, WIDTH, FRAMES, GROUP)
    grid_ref[1 : HEIGHT + 1, 1 : WIDTH + 1] = mixed_ref[...].astype(F32).reshape(HEIGHT, WIDTH, FRAMES, GROUP)
    sums_ref[...] = jnp.zeros(sums_ref.shape, F32)

    @pl.loop(0, HEIGHT)
    def _(i):
        for tile in range(GROUP // LANES):
            lanes = slice(tile * LANES, tile * LANES + LANES)
            line = convolve(dgrid_ref, taps_ref, True, i, lanes)
            frame = lax.broadcasted_iota(jnp.int32, line.shape, 1)
            line = jnp.where(frame < frames_ref[0], line, 0.0)
            at = pl.multiple_of(i * WIDTH * FRAMES, WIDTH * FRAMES)
            dmix_ref[pl.ds(at, WIDTH * FRAMES), lanes] = line.reshape(WIDTH * FRAMES, LANES).astype(BF16)
            own = dgrid_ref[i + 1, 1 : WIDTH + 1, :, lanes]
            moved = (shift_frames(own, -1), own, shift_frames(own, 1))
            for b in range(3):
                for e in range(3):
                    window = grid_ref[i + b, e : e + WIDTH, :, lanes]
                    for a in range(3):
                        tap = 9 * a + 3 * b + e
                        sums_ref[tap, :, lanes] += jnp.sum(window * moved[a], axis=0)

    for tap in range(27):
        gtaps_ref[0, tap : tap + 1, :] = jnp.sum(sums_ref[tap], axis=0, keepdims=True)
    dmixed = dmix_ref[...]
    gbias_ref[...] = jnp.sum(dmixed.astype(F32), axis=0, keepdims=True)
    gqkv_ref[...] = dot(normed_ref[...], dmixed, ((0,), (0,))).astype(BF16)
    dnorm_ref[...] += dot(dmixed, weight_ref[...], ((1,), (1,)))

    @pl.when(step == 5)
    def _():
        dy = dnorm_ref[...]
        centred, rs = layer_stats(x_ref[...].astype(F32), D)
        vhat = centred * rs
        small_ref[0:1, :] = jnp.sum(dy * vhat, axis=0, keepdims=True)
        small_ref[1:2, :] = jnp.sum(dy, axis=0, keepdims=True)
        small_ref[2:8, :] = jnp.zeros((6, D), F32)
        scaled = dy * g1_ref[...]
        first = jnp.sum(scaled, axis=1, keepdims=True) * (1.0 / D)
        second = jnp.sum(scaled * vhat, axis=1, keepdims=True) * (1.0 / D)
        dnorm_ref[...] = dmid_ref[...] + rs * (scaled - first - vhat * second)

        @pl.loop(0, PLACES)
        def _(place):
            at = pl.multiple_of(place * FRAMES, FRAMES)
            write_place(wide_ref, place, dnorm_ref[pl.ds(at, FRAMES), :])

        for tile in range(D // LANES):
            gtok_ref[:, tile * LANES : (tile + 1) * LANES] = wide_ref[tile]


def qkv_back(frames, grads, vhat, mixed, weight, normed, x, dmid, taps, gain, g1):
    smem = pl.BlockSpec(memory_space=pltpu.SMEM)
    once = pl.Buffered(1)

    def kept(shape):
        return pl.BlockSpec(shape, lambda *_: (0,) * len(shape), pipeline_mode=once)

    return pl.pallas_call(
        qkv_back_kernel,
        grid=(6,),
        out_shape=(
            jax.ShapeDtypeStruct((ROWS, D), F32),
            jax.ShapeDtypeStruct((D, QKV), BF16),
            jax.ShapeDtypeStruct((1, QKV), F32),
            jax.ShapeDtypeStruct((6, 27, GROUP), F32),
            jax.ShapeDtypeStruct((3 * HEADS, 2, LANES), F32),
            jax.ShapeDtypeStruct((8, D), F32),
        ),
        in_specs=[
            smem,
            pl.BlockSpec((1, GROUP_HEADS, ROWS, LANES), lambda g: (g // 2, g % 2, 0, 0)),
            pl.BlockSpec((GROUP_HEADS, ROWS, LANES), lambda g: (g, 0, 0)),
            pl.BlockSpec((ROWS, GROUP), lambda g: (0, g)),
            pl.BlockSpec((D, GROUP), lambda g: (0, g)),
            kept((ROWS, D)),
            kept((ROWS, D)),
            kept((ROWS, D)),
            pl.BlockSpec((1, 27, 8, GROUP), lambda g: (g // 2, 0, 0, 0)),
            pl.BlockSpec((1, 1, LANES), lambda g: (g // 2, 0, 0)),
            kept((1, D)),
        ],
        out_specs=(
            kept((ROWS, D)),
            pl.BlockSpec((D, GROUP), lambda g: (0, g)),
            pl.BlockSpec((1, GROUP), lambda g: (0, g)),
            pl.BlockSpec((1, 27, GROUP), lambda g: (g, 0, 0)),
            pl.BlockSpec((GROUP_HEADS, 2, LANES), lambda g: (g, 0, 0)),
            kept((8, D)),
        ),
        scratch_shapes=[
            pltpu.VMEM((HEIGHT + 2, WIDTH + 2, FRAMES, GROUP), F32),
            pltpu.VMEM((HEIGHT + 2, WIDTH + 2, FRAMES, GROUP), F32),
            pltpu.VMEM((ROWS, GROUP), F32),
            pltpu.VMEM((ROWS, GROUP), BF16),
            pltpu.VMEM((ROWS, D), F32),
            pltpu.VMEM((27, FRAMES, GROUP), F32),
            wide_scratch(D),
        ],
        compiler_params=params(),
        name="qkv_back",
    )(frames, grads, vhat, mixed, weight, normed, x, dmid, taps, gain, g1)


def row(vector):
    return vector.reshape(1, -1)


def tiled_lanes(array):
    return jnp.concatenate([array] * GROUP_HEADS, axis=-1)


def head_lanes(array):
    return jnp.pad(array, [(0, 0)] * (array.ndim - 1) + [(0, LANES - HEAD_DIM)])


def clip_work(
    tokens, prev_kv, memory, valid_frames, mem_len, ln1_gain, ln1_bias, qkv_bias, pool_conv, pool_gain, pool_bias,
    rel_time, rel_space, compress, proj_bias, ln2_gain, ln2_bias, fc1_bias, fc2_bias, cotangent, gathered,
):
    one_hot, own, fold, pick = (jnp.asarray(c, BF16) for c in constants())
    tables = jnp.concatenate([rel_time, rel_space[0], rel_space[1]], axis=0)
    tables = jnp.pad(tables, ((0, LANES - tables.shape[0]), (0, LANES - HEAD_DIM)))
    taps = jnp.broadcast_to(tiled_lanes(pool_conv)[:, :, None, :], (3, 27, 8, GROUP))
    gains, biases = head_lanes(pool_gain)[:, None], head_lanes(pool_bias)[:, None]
    x, normed, upstream, aug, table = prepare(
        valid_frames, mem_len, tokens, cotangent, row(ln1_gain), row(ln1_bias), one_hot, tables, pick
    )
    rest, parts = squeeze(prev_kv, memory, tiled_lanes(compress))
    w_qkv, w_proj, w_fc1, w_fc2 = gathered
    heads, vhat, mixed, weight = query_key_value(valid_frames, normed, w_qkv, row(qkv_bias), taps, gains, biases)
    weights, pv, attended = attend(heads, rest, aug, table, own, fold)
    out, dmid, datt, gp, gw1, gw2, small_two, gb1 = feed_forward(
        attended, x, upstream, w_proj, w_fc1, w_fc2, row(proj_bias), row(ln2_gain), row(ln2_bias),
        row(fc1_bias), row(fc2_bias),
    )
    grads, gtable, gcompress = attend_back(heads, rest, aug, table, own, fold, pick, weights, pv, datt, parts)
    gtok, gqkv, gqkv_bias, gtaps, gpool, small_one = qkv_back(
        valid_frames, grads, vhat, mixed, weight, normed, x, dmid, taps, gains, row(ln1_gain)
    )
    gconv = jnp.sum(gtaps.reshape(3, 2, 27, GROUP_HEADS, HEAD_DIM), axis=(1, 3))
    gpool = jnp.sum(gpool.reshape(3, HEADS, 2, LANES), axis=1)[:, :, :HEAD_DIM]
    smalls = (
        small_one[0], small_one[1], gqkv_bias[0], gconv, gpool[:, 0], gpool[:, 1],
        gtable[:15, :HEAD_DIM], gtable[15:53, :HEAD_DIM].reshape(2, 19, HEAD_DIM), gcompress[:, :, :HEAD_DIM],
        small_two[0], small_two[1], small_two[2], gb1[0], small_two[3],
    )
    return out, gtok, (gqkv, gp, gw1, gw2), smalls


DP_BLOCKS = 8


def canonical(gathered, dp, fsdp):
    rows, columns = gathered.shape[2:]
    if dp == DP_BLOCKS:
        return gathered
    joined = gathered.reshape(DP_BLOCKS, dp // DP_BLOCKS, fsdp, rows, columns).transpose(0, 2, 1, 3, 4)
    return joined.reshape(DP_BLOCKS, fsdp, dp // DP_BLOCKS * rows, columns)


def device_blocks(blocks, dp, fsdp):
    rows, columns = blocks.shape[2:]
    if dp == DP_BLOCKS:
        return blocks
    split = blocks.reshape(DP_BLOCKS, fsdp, dp // DP_BLOCKS, rows * DP_BLOCKS // dp, columns).transpose(0, 2, 1, 3, 4)
    return split.reshape(dp, fsdp, rows * DP_BLOCKS // dp, columns)


def on_device(dp, fsdp):
    axes = ("dp", "fsdp")

    def gather(shard):
        flat = lax.all_gather(shard, axes, axis=0, tiled=False)
        return canonical(flat.reshape((dp, fsdp) + shard.shape), dp, fsdp)

    def scatter(blocks):
        split = device_blocks(blocks, dp, fsdp)
        split = split.reshape((dp * fsdp,) + split.shape[2:])
        return lax.psum_scatter(split, axes, scatter_dimension=0, tiled=False).astype(F32)

    def run(
        tokens, prev_kv, memory, valid_frames, mem_len, ln1_gain, ln1_bias, w_qkv, qkv_bias, pool_conv, pool_gain,
        pool_bias, rel_time, rel_space, compress, w_proj, proj_bias, ln2_gain, ln2_bias, w_fc1, fc1_bias, w_fc2,
        fc2_bias, cotangent,
    ):
        gathered = tuple(gather(shard) for shard in (w_qkv, w_proj, w_fc1, w_fc2))
        out, gtok, big, smalls = clip_work(
            tokens, prev_kv, memory, valid_frames, mem_len, ln1_gain, ln1_bias, qkv_bias, pool_conv, pool_gain,
            pool_bias, rel_time, rel_space, compress, proj_bias, ln2_gain, ln2_bias, fc1_bias, fc2_bias, cotangent,
            gathered,
        )
        gqkv, gp, gw1, gw2 = big
        gqkv = gqkv.reshape(DP_BLOCKS, D // DP_BLOCKS, fsdp, QKV // fsdp).transpose(0, 2, 1, 3)
        sums = [scatter(g) for g in (gqkv, gp, gw1, gw2)]
        flat = jnp.concatenate([s.reshape(-1) for s in smalls])
        flat = lax.psum(flat, axes)
        totals, at = [], 0
        for s in smalls:
            totals.append(flat[at : at + s.size].reshape(s.shape))
            at += s.size
        return (
            out, gtok, totals[0], totals[1], sums[0], totals[2], totals[3], totals[4], totals[5], totals[6],
            totals[7], totals[8], sums[1], totals[9], totals[10], totals[11], sums[2], totals[12], sums[3], totals[13],
        )

    return run


def solution(mesh):
    both = P(("dp", "fsdp"))
    rows = P(("dp", "fsdp"), None)
    second = P(None, ("dp", "fsdp"), None)
    blocks = P("dp", "fsdp")
    none = P()
    return jax.shard_map(
        on_device(mesh.shape["dp"], mesh.shape["fsdp"]),
        mesh=mesh,
        in_specs=(
            rows, second, second, both, both, none, none, blocks, none, none, none, none, none, none, none, blocks,
            none, none, none, blocks, none, blocks, none, rows,
        ),
        out_specs=(
            rows, rows, none, none, blocks, none, none, none, none, none, none, none, blocks, none, none, none,
            blocks, none, blocks, none,
        ),
        check_vma=False,
    )
```

time: 3020 us -> 991 us (0.33)
  other arithmetic: 1070 us -> 10.3 us
  local copies, waits for them, and re-layouts: 1030 us -> 59.3 us
  matrix products: 297 us -> 0 us
  Pallas kernels: 0 us -> 240 us
  waiting for transfers between devices: 555 us -> 664 us
  blocking collectives: 31.8 us -> 0 us
    add x16 -> x0, local copies, waits for them, and re-layouts: 491 us -> none  [score_terms(): along_time[:, :, :, :, None, None] + along_height[:, :, :, None, :, None]]
    reduce_sum x52 -> x2, other arithmetic: 460 us -> 0.9 us  [the longest x1 0.76 us: clip_work(): gpool = jnp.sum(gpool.reshape(3, HEADS, 2, LANES), axis=1)[:, :, :HEAD_DIM]]
    add x48 -> x0, other arithmetic: 355 us -> none  [the longest x32 299 us: score_terms(): along_time[:, :, :, :, None, None] + along_height[:, :, :, None, :, None]]
    dot_general x164 -> x0, matrix products: 297 us -> none  [the longest x32 82.9 us: score_terms(): scores = jnp.dot(query, keys.T) * HEAD_DIM ** (-0.5)]
    reshape x44 -> x19, local copies, waits for them, and re-layouts: 306 us -> 31.9 us  [the longest x1 9.37 us: run(): gqkv.reshape(DP_BLOCKS, D // DP_BLOCKS, fsdp, QKV // fsdp)]
    pallas_call x0 -> x7, Pallas kernels: none -> 240 us  [the longest x1 60.8 us: qkv_back(): pl.pallas_call(qkv_back_kernel, grid=(6,), out_shape=(jax.ShapeDtypeStruc...]
    all_gather x4, waiting for transfers between devices: 4.71 us -> 145 us  [gather(): flat = lax.all_gather(shard, axes, axis=0, tiled=False)]
    mul x2 -> x0, other arithmetic: 88.2 us -> none  [pool_clip(): pooled = pooled + window * pool_conv[:, offset, :][:, None, :]]
  transfers between devices with their start and end apart: 13 -> 9, of which waited for: 8 -> 8; matrix products, arithmetic and copies ran while one was open for 33% -> 6% of each run, Pallas kernels for 0% -> 8%
where the time goes in v1:
time: 991 us; the launch traced here: 989 us
  waiting for transfers between devices  664 us (67%)
  Pallas kernels  240 us (24%)
  local copies, waits for them, and re-layouts  59.3 us (6%)
  between operations  15.3 us (2%)
  other arithmetic  10.3 us (1%)
    reduce_scatter x4, waiting for transfers between devices, scatter(): lax.psum_scatter(split, axes, scatter_dimension=0, tiled=False).astype(F32)  419 us
    all_gather x4, waiting for transfers between devices, gather(): flat = lax.all_gather(shard, axes, axis=0, tiled=False)  145 us
    psum x1, waiting for transfers between devices, run(): flat = lax.psum(flat, axes)  95.8 us
    pallas_call x1, Pallas kernels, qkv_back(): pl.pallas_call(qkv_back_kernel, grid=(6,), out_shape=(jax.ShapeDtypeStruc...  60.8 us
    pallas_call x1, Pallas kernels, feed_forward(): pl.pallas_call(middle_kernel, grid=(CHUNKS,), out_shape=(jax.ShapeDtypeSt...  48.5 us
    pallas_call x1, Pallas kernels, attend_back(): pl.pallas_call(attend_back_kernel, grid=(HEADS,), out_shape=(jax.ShapeDty...  47.4 us
    pallas_call x1, Pallas kernels, attend(): pl.pallas_call(attend_kernel, grid=(HEADS,), out_shape=(jax.ShapeDtypeStr...  36.4 us
    pallas_call x1, Pallas kernels, query_key_value(): pl.pallas_call(qkv_kernel, grid=(6,), out_shape=(jax.ShapeDtypeStruct((3...  35.4 us
  transfers between devices with their start and end apart: 9, of which 8 were waited for; matrix products, arithmetic and copies ran while one was open for 6% of the time, Pallas kernels for 8%

profile of v1, /device:TPU:0, one launch (start us, length us, event | category | flops | bytes accessed | tf_op | source)
XLA Modules:
  0.0 989.5 jit_solution(10458759068191275309)
XLA Ops:
  22.8 1.5 pad_maximum_fusion.1.taps_ref
  24.3 6.0 squeeze.41
  30.9 5.5 prepare.1
  36.6 38.4 %all-gather.9.cloned.1.call-done = bf16[3072,576]{1,0:T(8,128)(2,1)} async-done(((bf16[96,576]{1,0:T(8,128)(2,1)}), bf16[3072,576]{1,0:T(8,128)(2,1)}) %all-gather.9.cloned.1.call-update) | async-done | bytes 3538960 | tf_op jit(solution)/shard_map/all_gather | solution.py:840
  76.0 35.4 %query_key_value.1 = (bf16[24,800,128]{2,1,0:T(8,128)(2,1)}, bf16[24,800,128]{2,1,0:T(8,128)(2,1)}, bf16[800,2304]{1,0:T(8,128)(2,1)}, bf16[768,2304]{1,0:T(8,128)(2,1)}) custom-call(s32[1]{0:T(128)S(6)} %copy.64.frames_ref, bf16[800,768]{1,0:T(8,128)(2,1)} %get-tuple-element.51.normed_ref, bf16[8,4,96,576]{3,2,1,0:T(8,128)(2,1)} %bitcast.35, ...), custom_call_target="tpu_custom_call" | custom-call | tf_op jit(solution)/shard_map/query_key_value/pallas_call | solution.py:291
  111.4 36.4 %attend.1 = (bf16[8,800,1280]{2,1,0:T(8,128)(2,1)}, bf16[8,800,128]{2,1,0:T(8,128)(2,1)}, bf16[8,800,128]{2,1,0:T(8,128)(2,1)}) custom-call(bf16[24,800,128]{2,1,0:T(8,128)(2,1)} %get-tuple-element.52.q_ref.k_ref.v_ref, bf16[24,800,128]{2,1,0:T(8,128)(2,1)} %get-tuple-element.52.q_ref.k_ref.v_ref, bf16[24,800,128]{2,1,0:T(8,128)(2,1)} %get-tuple-element.52.q_ref.k_ref.v_ref, ...), custom_call_target="tpu_custom_call" | custom-call | tf_op jit(solution)/shard_map/attend/pallas_call | solution.py:360
  147.8 8.0 copy.55
  155.8 41.6 %all-gather.11.cloned.1.call-done = bf16[3072,192]{1,0:T(8,128)(2,1)} async-done(((bf16[96,192]{1,0:T(8,128)(2,1)}), bf16[3072,192]{1,0:T(8,128)(2,1)}) %all-gather.11.cloned.1.call-update) | async-done | bytes 1179664 | tf_op jit(solution)/shard_map/all_gather | solution.py:840
  197.4 65.3 %all-gather.13.cloned.1.call-done = bf16[3072,768]{1,0:T(8,128)(2,1)} async-done(((bf16[96,768]{1,0:T(8,128)(2,1)}), bf16[3072,768]{1,0:T(8,128)(2,1)}) %all-gather.13.cloned.1.call-update) | async-done | bytes 4718608 | tf_op jit(solution)/shard_map/all_gather | solution.py:840
  262.6 48.5 %feed_forward.1 = (bf16[800,768]{1,0:T(8,128)(2,1)}, f32[800,768]{1,0:T(8,128)}, bf16[8,800,128]{2,1,0:T(8,128)(2,1)}, bf16[8,4,96,192]{3,2,1,0:T(8,128)(2,1)}, ...) custom-call(bf16[8,800,128]{2,1,0:T(8,128)(2,1)} %get-tuple-element.56, ...), custom_call_target="tpu_custom_call" | custom-call | tf_op jit(solution)/shard_map/feed_forward/pallas_call | solution.py:484
  311.1 47.4 %attend_back.1 = (bf16[3,8,800,128]{3,2,1,0:T(8,128)(2,1)}, f32[128,128]{1,0:T(8,128)}, f32[2,4,128]{2,1,0:T(4,128)}) custom-call(bf16[24,800,128]{2,1,0:T(8,128)(2,1)} %get-tuple-element.52.q_ref.k_ref.v_ref, bf16[24,800,128]{2,1,0:T(8,128)(2,1)} %get-tuple-element.52.q_ref.k_ref.v_ref, bf16[24,800,128]{2,1,0:T(8,128)(2,1)} %get-tuple-element.52.q_ref.k_ref.v_ref, ...), custom_call_target="tpu_custom_call" | custom-call | tf_op jit(solution)/shard_map/attend_back/pallas_call | solution.py:599
  360.7 60.8 %qkv_back.1 = (f32[800,768]{1,0:T(8,128)}, bf16[768,2304]{1,0:T(8,128)(2,1)}, f32[1,2304]{1,0:T(1,128)}, f32[6,27,384]{2,1,0:T(8,128)}, f32[24,2,128]{2,1,0:T(2,128)}, /*index=5*/f32[8,768]{1,0:T(8,128)}) custom-call(s32[1]{0:T(128)S(6)} %copy.64.frames_ref, bf16[3,8,800,128]{3,2,1,0:T(8,128)(2,1)} %get-tuple-element.64.grads_ref, ...), custom_call_target="tpu_custom_call" | custom-call | tf_op jit(solution)/shard_map/qkv_back/pallas_call | solution.py:725
  427.0 9.4 reshape.183
  436.4 4.8 copy.56
  442.0 8.1 copy.57
  450.1 95.8 %all-reduce.5.cloned.1.call-done = f32[24192]{0:T(1024)} async-done(((f32[24192]{0:T(1024)}), f32[24192]{0:T(1024)}) %all-reduce.5.cloned.1.call-update) | async-done | bytes 96784 | tf_op jit(solution)/shard_map/psum | solution.py:863
  557.2 91.8 %reduce-scatter.7.cloned.1.call-done = bf16[1,96,192]{2,1,0:T(8,128)(2,1)} async-done(((bf16[32,96,192]{2,1,0:T(8,128)(2,1)}), bf16[1,96,192]{2,1,0:T(8,128)(2,1)}) %reduce-scatter.7.cloned.1.call-update) | async-done | bytes 36880 | tf_op jit(solution)/shard_map/reduce_scatter | solution.py:846
  648.9 1.4 bitcast_convert_fusion.3
  650.4 107.0 %reduce-scatter.5.cloned.1.call-done = bf16[1,96,576]{2,1,0:T(8,128)(2,1)} async-done(((bf16[32,96,576]{2,1,0:T(8,128)(2,1)}), bf16[1,96,576]{2,1,0:T(8,128)(2,1)}) %reduce-scatter.5.cloned.1.call-update) | async-done | bytes 110608 | tf_op jit(solution)/shard_map/reduce_scatter | solution.py:846
  757.4 1.6 bitcast_convert_fusion.2
  759.0 109.8 %reduce-scatter.9.cloned.1.call-done = bf16[1,96,768]{2,1,0:T(8,128)(2,1)} async-done(((bf16[32,96,768]{2,1,0:T(8,128)(2,1)}), bf16[1,96,768]{2,1,0:T(8,128)(2,1)}) %reduce-scatter.9.cloned.1.call-update) | async-done | bytes 147472 | tf_op jit(solution)/shard_map/reduce_scatter | solution.py:846
  868.8 1.6 bitcast_convert_fusion.1
  870.5 110.8 %reduce-scatter.11.cloned.1.call-done = bf16[1,384,192]{1,2,0:T(8,128)(2,1)} async-done(((bf16[32,384,192]{1,2,0:T(8,128)(2,1)}), bf16[1,384,192]{1,2,0:T(8,128)(2,1)}) %reduce-scatter.11.cloned.1.call-update) | async-done | bytes 147472 | tf_op jit(solution)/shard_map/reduce_scatter | solution.py:846
  981.3 1.6 bitcast_convert_fusion
  (75 shorter events, 35.8 us)
Async XLA Ops:
  7.2 23.1 %copy-start.1 = (f32[2,19,96]{2,0,1:T(2,128)S(1)}, f32[2,19,96]{2,0,1:T(2,128)}, u32[]{:S(2)}) copy-start(f32[2,19,96]{2,0,1:T(2,128)} %param.41) | copy-start | bytes 43780
  7.2 23.1 %copy-start.3 = (f32[15,96]{1,0:T(8,128)S(1)}, f32[15,96]{1,0:T(8,128)}, u32[]{:S(2)}) copy-start(f32[15,96]{1,0:T(8,128)} %param.40) | copy-start | bytes 17284
  7.2 29.2 %copy-start = (f32[3,27,96]{2,1,0:T(8,128)S(1)}, f32[3,27,96]{2,1,0:T(8,128)}, u32[]{:S(2)}) copy-start(f32[3,27,96]{2,1,0:T(8,128)} %param.37) | copy-start | bytes 93316
  7.2 67.8 %all-gather.9.cloned.1.call-start = ((), (), s32[]{:S(2)}) async-start(), calls=%async_computation.9 | async-start | bytes 4055040 | tf_op jit(solution)/shard_map/all_gather | solution.py:840
  8.0 139.8 %all-gather.15.cloned.1.call-start = ((), (), s32[]{:S(2)}) async-start(), calls=%async_computation.12 | async-start | bytes 4866048 | tf_op jit(solution)/shard_map/all_gather | solution.py:840
  8.7 188.6 %all-gather.11.cloned.1.call-start = ((), (), s32[]{:S(2)}) async-start(), calls=%async_computation.10 | async-start | bytes 1622016 | tf_op jit(solution)/shard_map/all_gather | solution.py:840
  9.4 253.2 %all-gather.13.cloned.1.call-start = ((), (), s32[]{:S(2)}) async-start(), calls=%async_computation.11 | async-start | bytes 4866048 | tf_op jit(solution)/shard_map/all_gather | solution.py:840
  10.0 535.9 %all-reduce.5.cloned.1.call-start = ((), (), s32[]{:S(2)}) async-start(), calls=%async_computation.4 | async-start | bytes 196608 | tf_op jit(solution)/shard_map/psum | solution.py:863
  360.7 62.8 %copy-start.4 = (f32[8,768]{1,0:T(8,128)S(1)}, f32[8,768]{1,0:T(8,128)}, u32[]{:S(2)}) copy-start(f32[8,768]{1,0:T(8,128)} %get-tuple-element.76) | copy-start | bytes 73732
  360.7 65.0 %copy-start.2 = (f32[1,3072]{1,0:T(1,128)S(1)}, f32[1,3072]{1,0:T(1,128)}, u32[]{:S(2)}) copy-start(f32[1,3072]{1,0:T(1,128)} %get-tuple-element.77) | copy-start | bytes 36868
  426.4 222.5 %reduce-scatter.7.cloned.1.call-start = ((), (), s32[]{:S(2)}) async-start(), calls=%async_computation.6 | async-start | bytes 1622016 | tf_op jit(solution)/shard_map/reduce_scatter | solution.py:846
  427.0 330.4 %reduce-scatter.5.cloned.1.call-start = ((), (), s32[]{:S(2)}) async-start(), calls=%async_computation.5 | async-start | bytes 4055040 | tf_op jit(solution)/shard_map/reduce_scatter | solution.py:846
  441.2 427.7 %reduce-scatter.9.cloned.1.call-start = ((), (), s32[]{:S(2)}) async-start(), calls=%async_computation.7 | async-start | bytes 4866048 | tf_op jit(solution)/shard_map/reduce_scatter | solution.py:846
  441.9 539.4 %reduce-scatter.11.cloned.1.call-start = ((), (), s32[]{:S(2)}) async-start(), calls=%async_computation.8 | async-start | bytes 4866048 | tf_op jit(solution)/shard_map/reduce_scatter | solution.py:846
Sparse Core Ops, SparseCore 0:
  11.0 63.9 all-gather.8
  77.9 64.2 all-gather.14
  145.1 52.2 all-gather.10
  200.1 62.4 all-gather.12
  426.5 119.3 all-reduce.4
  551.0 97.8 reduce-scatter.6
  654.3 103.0 reduce-scatter.4
  762.9 105.8 reduce-scatter.8
  875.2 106.0 reduce-scatter.10

commit v2 on v1

--- a/solution.py
+++ b/solution.py
@@ -243,8 +243,22 @@
     grid_ref[...] = jnp.zeros(grid_ref.shape, grid_ref.dtype)
 
 
+def relative_bits(place_ref, d, f):
+    return {
+        "x": (d & 1) ^ place_ref[0],
+        "z1": ((d >> 1) & 1) ^ place_ref[1],
+        "z2": ((d >> 2) & 1) ^ place_ref[2],
+        "y": ((f >> 1) & 1) ^ place_ref[3],
+        "c": (f & 1) ^ place_ref[4],
+    }
+
+
+def slot(bits, order):
+    return sum(bits[name] << at for at, name in enumerate(order))
+
+
 def qkv_kernel(
-    frames_ref, normed_ref, shards_ref, qkv_bias_ref, taps_ref, gain_ref, bias_ref,
+    frames_ref, place_ref, normed_ref, first_ref, second_ref, qkv_bias_ref, taps_ref, gain_ref, bias_ref,
     heads_ref, vhat_ref, mixed_ref, weight_ref, grid_ref, pooled_ref,
 ):
     step = pl.program_id(0)
@@ -252,9 +266,15 @@
     @pl.when(step == 0)
     def _():
         clear_border(grid_ref)
-        columns = shards_ref.shape[3]
-        for f in range(shards_ref.shape[1]):
-            weight_ref[:, f * columns : (f + 1) * columns] = shards_ref[:, f].reshape(D, columns)
+        half, columns = first_ref.shape[1:]
+        for f in range(QKV // columns):
+
+            @pl.loop(0, DP_BLOCKS)
+            def _(d):
+                bits = relative_bits(place_ref, d, f)
+                for part, (source_ref, order) in enumerate(((first_ref, ROUTE_ONE), (second_ref, ROUTE_TWO))):
+                    at = pl.multiple_of((2 * d + part) * half, half)
+                    weight_ref[pl.ds(at, half), f * columns : (f + 1) * columns] = source_ref[slot(bits, order)]
 
     at = pl.multiple_of(step * GROUP, LANES)
     mixed = dot(normed_ref[...], weight_ref[:, pl.ds(at, GROUP)]) + qkv_bias_ref[...]
@@ -286,7 +306,7 @@
         vhat_ref[head] = (vhat + extra).astype(BF16)
 
 
-def query_key_value(frames, normed, shards, qkv_bias, taps, gain, bias):
+def query_key_value(frames, place, normed, first, second, qkv_bias, taps, gain, bias):
     smem = pl.BlockSpec(memory_space=pltpu.SMEM)
     return pl.pallas_call(
         qkv_kernel,
@@ -299,8 +319,10 @@
         ),
         in_specs=[
             smem,
+            smem,
             whole((ROWS, D)),
-            whole(shards.shape),
+            whole(first.shape),
+            whole(second.shape),
             pl.BlockSpec((1, GROUP), lambda g: (0, g)),
             pl.BlockSpec((1, 27, 8, GROUP), lambda g: (g // 2, 0, 0, 0)),
             pl.BlockSpec((1, 1, LANES), lambda g: (g // 2, 0, 0)),
@@ -318,7 +340,7 @@
         ],
         compiler_params=params(),
         name="query_key_value",
-    )(frames, normed, shards, qkv_bias, taps, gain, bias)
+    )(frames, place, normed, first, second, qkv_bias, taps, gain, bias)
 
 
 def attend_kernel(
@@ -396,20 +418,24 @@
 
 
 def middle_kernel(
-    att_ref, x_ref, up_ref, wp_ref, w1_ref, w2_ref, pb_ref, g2_ref, b2_ref, fb1_ref, fb2_ref,
+    place_ref, att_ref, x_ref, up_ref, wp_ref, w1_ref, w2_ref, pb_ref, g2_ref, b2_ref, fb1_ref, fb2_ref,
     out_ref, dmid_ref, datt_ref, gp_ref, gw1_ref, gw2_ref, small_ref, gb1_ref,
-    packed_ref, proj_ref, mid_ref, hidden_ref, total_ref, dhid_ref, wide_ref,
+    packed_ref, proj_ref, mid_ref, hidden_ref, total_ref, dhid_ref, wide_ref, w1_scr, w2_scr,
 ):
     step = pl.program_id(0)
     sides = wp_ref.shape[1]
     part = D // sides
+    depth = D // DP_BLOCKS
 
     @pl.when(step == 0)
     def _():
         for head in range(HEADS):
             packed_ref[:, HEAD_DIM * head : HEAD_DIM * (head + 1)] = att_ref[head][:, :HEAD_DIM]
         for f in range(sides):
-            proj_ref[:, f * part : (f + 1) * part] = wp_ref[:, f].reshape(D, part)
+            for d in range(DP_BLOCKS):
+                rows = slice(d * depth, (d + 1) * depth)
+                proj_ref[rows, f * part : f * part + LANES] = wp_ref[d, f, :depth]
+                proj_ref[rows, f * part + LANES : (f + 1) * part] = wp_ref[d, f, depth:, : part - LANES]
         middle = x_ref[...].astype(F32) + dot(packed_ref[...], proj_ref[...]) + pb_ref[...]
         mid_ref[...] = middle
         centred, rs = layer_stats(middle, D)
@@ -417,22 +443,31 @@
         total_ref[...] = middle + fb2_ref[...]
         dhid_ref[...] = jnp.zeros((ROWS, D), F32)
 
-    w1 = w1_ref[:, 0].reshape(D, CHUNK)
-    w2 = jnp.concatenate([w2_ref[0, f] for f in range(sides)], axis=1)
+    for tile in range(CHUNK // LANES):
+        lanes = slice(tile * LANES, (tile + 1) * LANES)
+        for d in range(DP_BLOCKS):
+            w1_scr[d * depth : (d + 1) * depth, lanes] = w1_ref[d, 0, tile * depth : (tile + 1) * depth]
+        for f in range(sides):
+            w2_scr[f * part : (f + 1) * part, lanes] = w2_ref[0, f, tile * part : (tile + 1) * part]
+    w1, w2 = w1_scr[...], w2_scr[...]
     before = dot(hidden_ref[...], w1) + fb1_ref[...]
     erf = lax.erf(before * (2.0**-0.5))
     cdf = 0.5 * (1.0 + erf)
     activated = (before * cdf).astype(BF16)
     slope = cdf + before * (jnp.exp(before * before * -0.5) * 0.3989422804014327)
-    dbefore = dot(up_ref[...], w2, ((1,), (1,))) * slope
+    dbefore = dot(up_ref[...], w2) * slope
     dbefore_low = dbefore.astype(BF16)
     gb1_ref[...] = jnp.sum(dbefore_low.astype(F32), axis=0, keepdims=True)
-    total_ref[...] += dot(activated, w2)
+    total_ref[...] += dot(activated, w2, ((1,), (1,)))
     grad_two = dot(activated, up_ref[...], ((0,), (0,))).astype(BF16)
     for f in range(sides):
-        gw2_ref[0, f] = grad_two[:, f * part : (f + 1) * part]
+        bits = relative_bits(place_ref, 0, f)
+        gw2_ref[bits["c"], bits["y"], 0, 0, 0] = grad_two[:, f * part : (f + 1) * part]
     dhid_ref[...] += dot(dbefore_low, w1, ((1,), (1,)))
-    gw1_ref[:, 0] = dot(hidden_ref[...], dbefore_low, ((0,), (0,))).astype(BF16).reshape(gw1_ref.shape[0], -1, CHUNK)
+    grad_one = dot(hidden_ref[...], dbefore_low, ((0,), (0,))).astype(BF16)
+    for d in range(DP_BLOCKS):
+        bits = relative_bits(place_ref, d, 0)
+        gw1_ref[0, bits["x"], 0, bits["z1"], bits["z2"]] = grad_one[d * depth : (d + 1) * depth]
 
     @pl.when(step == CHUNKS - 1)
     def _():
@@ -461,8 +496,11 @@
         small_ref[3:4, :] = jnp.sum(upstream, axis=0, keepdims=True)
         small_ref[4:8, :] = jnp.zeros((4, D), F32)
         grad_proj = dot(packed_ref[...], dproj, ((0,), (0,))).astype(BF16)
-        for f in range(sides):
-            gp_ref[:, f] = grad_proj[:, f * part : (f + 1) * part].reshape(gp_ref.shape[0], -1, part)
+        for d in range(DP_BLOCKS):
+            for f in range(sides):
+                bits = relative_bits(place_ref, d, f)
+                block = grad_proj[d * depth : (d + 1) * depth, f * part : (f + 1) * part]
+                gp_ref[bits["c"], bits["y"], bits["x"], bits["z1"], bits["z2"]] = block
         datt = dot(dproj, proj_ref[...], ((1,), (1,))).astype(BF16)
         for head in range(HEADS):
             datt_ref[head] = jnp.concatenate(
@@ -471,64 +509,76 @@
             )
 
 
-def feed_forward(att, x, up, wp, w1, w2, pb, g2, b2, fb1, fb2):
+def feed_forward(place, att, x, up, flat, pb, g2, b2, fb1, fb2):
     once = pl.Buffered(1)
+    sides = flat.shape[1]
+    part, depth = D // sides, D // DP_BLOCKS
 
     def kept(shape):
         return pl.BlockSpec(shape, lambda *_: (0,) * len(shape), pipeline_mode=once)
 
-    w1_block = (w1.shape[0], 1, w1.shape[2], CHUNK)
-    w2_block = (1,) + w2.shape[1:]
-    w1_spec = pl.BlockSpec(w1_block, lambda c: (0, c // 2, 0, c % 2))
-    w2_spec = pl.BlockSpec(w2_block, lambda c: (c, 0, 0, 0))
+    def one_place(c, place):
+        return (place[4] ^ ((c // 2) & 1), 0, place[3] ^ (c // 4), 0, 0, 0, c % 2)
+
+    def two_place(c, place):
+        return (0, 0, place[0] ^ (c & 1), place[1] ^ ((c >> 1) & 1), place[2] ^ (c >> 2), 0, 0)
+
+    def clear(c, place):
+        return (0, c)
+
     return pl.pallas_call(
         middle_kernel,
-        grid=(CHUNKS,),
         out_shape=(
             jax.ShapeDtypeStruct((ROWS, D), BF16),
             jax.ShapeDtypeStruct((ROWS, D), F32),
             jax.ShapeDtypeStruct((HEADS, ROWS, LANES), BF16),
-            jax.ShapeDtypeStruct(wp.shape, BF16),
-            jax.ShapeDtypeStruct(w1.shape, BF16),
-            jax.ShapeDtypeStruct(w2.shape, BF16),
+            jax.ShapeDtypeStruct((2, 2, 2, 2, 2, depth, part), BF16),
+            jax.ShapeDtypeStruct((2, 2, 2, 2, 2, depth, FF // sides), BF16),
+            jax.ShapeDtypeStruct((2, 2, 2, 2, 2, FF // DP_BLOCKS, part), BF16),
             jax.ShapeDtypeStruct((8, D), F32),
             jax.ShapeDtypeStruct((1, FF), F32),
         ),
-        in_specs=[
-            kept((HEADS, ROWS, LANES)),
-            kept((ROWS, D)),
-            kept((ROWS, D)),
-            kept(wp.shape),
-            w1_spec,
-            w2_spec,
-            kept((1, D)),
-            kept((1, D)),
-            kept((1, D)),
-            pl.BlockSpec((1, CHUNK), lambda c: (0, c)),
-            kept((1, D)),
-        ],
-        out_specs=(
-            kept((ROWS, D)),
-            kept((ROWS, D)),
-            kept((HEADS, ROWS, LANES)),
-            kept(wp.shape),
-            w1_spec,
-            w2_spec,
-            kept((8, D)),
-            pl.BlockSpec((1, CHUNK), lambda c: (0, c)),
-        ),
-        scratch_shapes=[
-            pltpu.VMEM((ROWS, D), BF16),
-            pltpu.VMEM((D, D), BF16),
-            pltpu.VMEM((ROWS, D), F32),
-            pltpu.VMEM((ROWS, D), BF16),
-            pltpu.VMEM((ROWS, D), F32),
-            pltpu.VMEM((ROWS, D), F32),
-            wide_scratch(D),
-        ],
+        grid_spec=pltpu.PrefetchScalarGridSpec(
+            num_scalar_prefetch=1,
+            grid=(CHUNKS,),
+            in_specs=[
+                kept((HEADS, ROWS, LANES)),
+                kept((ROWS, D)),
+                kept((ROWS, D)),
+                pl.BlockSpec((DP_BLOCKS, sides, 2 * depth, LANES), lambda c, place: (0, 0, 6, 0), pipeline_mode=once),
+                pl.BlockSpec((DP_BLOCKS, 1, 3 * depth, LANES), lambda c, place: (0, c // 2, c % 2, 0)),
+                pl.BlockSpec((1, sides, 3 * part, LANES), lambda c, place: (c, 0, 1, 0)),
+                kept((1, D)),
+                kept((1, D)),
+                kept((1, D)),
+                pl.BlockSpec((1, CHUNK), clear),
+                kept((1, D)),
+            ],
+            out_specs=(
+                kept((ROWS, D)),
+                kept((ROWS, D)),
+                kept((HEADS, ROWS, LANES)),
+                kept((2, 2, 2, 2, 2, depth, part)),
+                pl.BlockSpec((1, 2, 1, 2, 2, depth, CHUNK), one_place),
+                pl.BlockSpec((2, 2, 1, 1, 1, FF // DP_BLOCKS, part), two_place),
+                kept((8, D)),
+                pl.BlockSpec((1, CHUNK), clear),
+            ),
+            scratch_shapes=[
+                pltpu.VMEM((ROWS, D), BF16),
+                pltpu.VMEM((D, D), BF16),
+                pltpu.VMEM((ROWS, D), F32),
+                pltpu.VMEM((ROWS, D), BF16),
+                pltpu.VMEM((ROWS, D), F32),
+                pltpu.VMEM((ROWS, D), F32),
+                wide_scratch(D),
+                pltpu.VMEM((D, CHUNK), BF16),
+                pltpu.VMEM((D, CHUNK), BF16),
+            ],
+        ),
         compiler_params=params(),
         name="feed_forward",
-    )(att, x, up, wp, w1, w2, pb, g2, b2, fb1, fb2)
+    )(place, att, x, up, flat, flat, flat, pb, g2, b2, fb1, fb2)
 
 
 def attend_back_kernel(
@@ -587,38 +637,38 @@
             product = piece * parts_ref[s, 0, tap].astype(F32)[:MEM]
             gtaps_ref[s, tap : tap + 1, :] += jnp.sum(product, axis=0, keepdims=True)
 
-    @pl.when(step == HEADS - 1)
+    @pl.when(step == pl.num_programs(0) - 1)
     def _():
         gtable_ref[...] = dot(pick_ref[...], gsum_ref[...], ((0,), (0,)), lax.Precision.HIGHEST)
 
 
-def attend_back(heads, rest, aug, table, own, fold, pick, weights, pv, datt, parts):
+def attend_back(start, count, heads, rest, aug, table, own, fold, pick, weights, pv, datt, parts):
     head = (1, ROWS, LANES)
     tail = (1, 1, REST, LANES)
-    own_head = pl.BlockSpec(head, lambda h: (h, 0, 0))
+    own_head = pl.BlockSpec(head, lambda h: (start + h, 0, 0))
     return pl.pallas_call(
         attend_back_kernel,
-        grid=(HEADS,),
+        grid=(count,),
         out_shape=(
-            jax.ShapeDtypeStruct((3, HEADS, ROWS, LANES), BF16),
+            jax.ShapeDtypeStruct((3, count, ROWS, LANES), BF16),
             jax.ShapeDtypeStruct((LANES, LANES), F32),
             jax.ShapeDtypeStruct((2, 4, LANES), F32),
         ),
         in_specs=[
             own_head,
-            pl.BlockSpec(head, lambda h: (HEADS + h, 0, 0)),
-            pl.BlockSpec(head, lambda h: (2 * HEADS + h, 0, 0)),
-            pl.BlockSpec(tail, lambda h: (0, h, 0, 0)),
-            pl.BlockSpec(tail, lambda h: (1, h, 0, 0)),
+            pl.BlockSpec(head, lambda h: (HEADS + start + h, 0, 0)),
+            pl.BlockSpec(head, lambda h: (2 * HEADS + start + h, 0, 0)),
+            pl.BlockSpec(tail, lambda h: (0, start + h, 0, 0)),
+            pl.BlockSpec(tail, lambda h: (1, start + h, 0, 0)),
             whole((KEY_ROWS, LANES)),
             whole((TABLE, LANES)),
             whole((ROWS, TABLE)),
             whole((TABLE, LANES)),
             whole((TABLE, LANES)),
-            pl.BlockSpec((1, ROWS, KEY_ROWS), lambda h: (h, 0, 0)),
+            pl.BlockSpec((1, ROWS, KEY_ROWS), lambda h: (start + h, 0, 0)),
             own_head,
             own_head,
-            pl.BlockSpec((2, 1, 4, 208, LANES), lambda h: (0, h, 0, 0, 0)),
+            pl.BlockSpec((2, 1, 4, 208, LANES), lambda h: (0, start + h, 0, 0, 0)),
         ],
         out_specs=(
             pl.BlockSpec((3, 1, ROWS, LANES), lambda h: (0, h, 0, 0)),
@@ -637,10 +687,10 @@
     )(heads, heads, heads, rest, rest, aug, table, own, fold, pick.astype(F32), weights, pv, datt, parts)
 
 
-def qkv_back_kernel(
-    frames_ref, grads_ref, vhat_ref, mixed_ref, weight_ref, normed_ref, x_ref, dmid_ref, taps_ref, gain_ref, g1_ref,
-    gtok_ref, gqkv_ref, gbias_ref, gtaps_ref, gpool_ref, small_ref,
-    grid_ref, dgrid_ref, dpool_ref, dmix_ref, dnorm_ref, sums_ref, wide_ref,
+def pool_back_kernel(
+    frames_ref, first_ref, second_ref, vhat_ref, mixed_ref, taps_ref, gain_ref,
+    dmix_ref, gbias_ref, gtaps_ref, gpool_ref,
+    grid_ref, dgrid_ref, dpool_ref, sums_ref,
 ):
     step = pl.program_id(0)
 
@@ -648,11 +698,10 @@
     def _():
         clear_border(grid_ref)
         clear_border(dgrid_ref)
-        dnorm_ref[...] = jnp.zeros((ROWS, D), F32)
 
     lane = lane_index((ROWS, LANES))
     for head in range(GROUP_HEADS):
-        dy = grads_ref[0, head].astype(F32)
+        dy = jnp.where(step == 0, first_ref[0, head].astype(F32), second_ref[0, head].astype(F32))
         dy = jnp.where(lane < HEAD_DIM, dy, 0.0)
         vhat = vhat_ref[head].astype(F32)
         rs = vhat[:, HEAD_DIM : HEAD_DIM + 1] + vhat[:, HEAD_DIM + 1 : HEAD_DIM + 2]
@@ -688,84 +737,114 @@
 
     for tap in range(27):
         gtaps_ref[0, tap : tap + 1, :] = jnp.sum(sums_ref[tap], axis=0, keepdims=True)
-    dmixed = dmix_ref[...]
-    gbias_ref[...] = jnp.sum(dmixed.astype(F32), axis=0, keepdims=True)
-    gqkv_ref[...] = dot(normed_ref[...], dmixed, ((0,), (0,))).astype(BF16)
-    dnorm_ref[...] += dot(dmixed, weight_ref[...], ((1,), (1,)))
-
-    @pl.when(step == 5)
-    def _():
-        dy = dnorm_ref[...]
-        centred, rs = layer_stats(x_ref[...].astype(F32), D)
-        vhat = centred * rs
-        small_ref[0:1, :] = jnp.sum(dy * vhat, axis=0, keepdims=True)
-        small_ref[1:2, :] = jnp.sum(dy, axis=0, keepdims=True)
-        small_ref[2:8, :] = jnp.zeros((6, D), F32)
-        scaled = dy * g1_ref[...]
-        first = jnp.sum(scaled, axis=1, keepdims=True) * (1.0 / D)
-        second = jnp.sum(scaled * vhat, axis=1, keepdims=True) * (1.0 / D)
-        dnorm_ref[...] = dmid_ref[...] + rs * (scaled - first - vhat * second)
-
-        @pl.loop(0, PLACES)
-        def _(place):
-            at = pl.multiple_of(place * FRAMES, FRAMES)
-            write_place(wide_ref, place, dnorm_ref[pl.ds(at, FRAMES), :])
-
-        for tile in range(D // LANES):
-            gtok_ref[:, tile * LANES : (tile + 1) * LANES] = wide_ref[tile]
-
-
-def qkv_back(frames, grads, vhat, mixed, weight, normed, x, dmid, taps, gain, g1):
+    gbias_ref[...] = jnp.sum(dmix_ref[...].astype(F32), axis=0, keepdims=True)
+
+
+def pool_back(kind, frames, grads_a, grads_b, vhat, mixed, taps, gain):
     smem = pl.BlockSpec(memory_space=pltpu.SMEM)
-    once = pl.Buffered(1)
-
-    def kept(shape):
-        return pl.BlockSpec(shape, lambda *_: (0,) * len(shape), pipeline_mode=once)
-
     return pl.pallas_call(
-        qkv_back_kernel,
-        grid=(6,),
+        pool_back_kernel,
+        grid=(2,),
         out_shape=(
-            jax.ShapeDtypeStruct((ROWS, D), F32),
-            jax.ShapeDtypeStruct((D, QKV), BF16),
-            jax.ShapeDtypeStruct((1, QKV), F32),
-            jax.ShapeDtypeStruct((6, 27, GROUP), F32),
-            jax.ShapeDtypeStruct((3 * HEADS, 2, LANES), F32),
-            jax.ShapeDtypeStruct((8, D), F32),
+            jax.ShapeDtypeStruct((ROWS, D), BF16),
+            jax.ShapeDtypeStruct((1, D), F32),
+            jax.ShapeDtypeStruct((2, 27, GROUP), F32),
+            jax.ShapeDtypeStruct((HEADS, 2, LANES), F32),
         ),
         in_specs=[
             smem,
-            pl.BlockSpec((1, GROUP_HEADS, ROWS, LANES), lambda g: (g // 2, g % 2, 0, 0)),
-            pl.BlockSpec((GROUP_HEADS, ROWS, LANES), lambda g: (g, 0, 0)),
-            pl.BlockSpec((ROWS, GROUP), lambda g: (0, g)),
-            pl.BlockSpec((D, GROUP), lambda g: (0, g)),
-            kept((ROWS, D)),
-            kept((ROWS, D)),
-            kept((ROWS, D)),
-            pl.BlockSpec((1, 27, 8, GROUP), lambda g: (g // 2, 0, 0, 0)),
-            pl.BlockSpec((1, 1, LANES), lambda g: (g // 2, 0, 0)),
-            kept((1, D)),
+            pl.BlockSpec((1, GROUP_HEADS, ROWS, LANES), lambda g: (kind, 0, 0, 0)),
+            pl.BlockSpec((1, GROUP_HEADS, ROWS, LANES), lambda g: (kind, 0, 0, 0)),
+            pl.BlockSpec((GROUP_HEADS, ROWS, LANES), lambda g: (2 * kind + g, 0, 0)),
+            pl.BlockSpec((ROWS, GROUP), lambda g: (0, 2 * kind + g)),
+            pl.BlockSpec((1, 27, 8, GROUP), lambda g: (kind, 0, 0, 0)),
+            pl.BlockSpec((1, 1, LANES), lambda g: (kind, 0, 0)),
         ],
         out_specs=(
-            kept((ROWS, D)),
-            pl.BlockSpec((D, GROUP), lambda g: (0, g)),
+            pl.BlockSpec((ROWS, GROUP), lambda g: (0, g)),
             pl.BlockSpec((1, GROUP), lambda g: (0, g)),
             pl.BlockSpec((1, 27, GROUP), lambda g: (g, 0, 0)),
             pl.BlockSpec((GROUP_HEADS, 2, LANES), lambda g: (g, 0, 0)),
-            kept((8, D)),
         ),
         scratch_shapes=[
             pltpu.VMEM((HEIGHT + 2, WIDTH + 2, FRAMES, GROUP), F32),
             pltpu.VMEM((HEIGHT + 2, WIDTH + 2, FRAMES, GROUP), F32),
             pltpu.VMEM((ROWS, GROUP), F32),
-            pltpu.VMEM((ROWS, GROUP), BF16),
-            pltpu.VMEM((ROWS, D), F32),
             pltpu.VMEM((27, FRAMES, GROUP), F32),
-            wide_scratch(D),
         ],
         compiler_params=params(),
-        name="qkv_back",
-    )(frames, grads, vhat, mixed, weight, normed, x, dmid, taps, gain, g1)
+        name="pool_back_%d" % kind,
+    )(frames, grads_a, grads_b, vhat, mixed, taps, gain)
+
+
+def project_grad_kernel(place_ref, normed_ref, dq_ref, dk_ref, dv_ref, one_ref, two_ref, full_ref):
+    for kind, source_ref in enumerate((dq_ref, dk_ref, dv_ref)):
+        grad = dot(normed_ref[...], source_ref[...], ((0,), (0,)))
+        full_ref[:, kind * D : (kind + 1) * D] = grad.astype(BF16)
+    half, columns = one_ref.shape[5:]
+    for f in range(QKV // columns):
+
+        @pl.loop(0, DP_BLOCKS)
+        def _(d):
+            bits = relative_bits(place_ref, d, f)
+            lanes = slice(f * columns, (f + 1) * columns)
+            at = pl.multiple_of(2 * d * half, half)
+            one_ref[bits["c"], bits["x"], bits["y"], bits["z1"], bits["z2"]] = full_ref[pl.ds(at, half), lanes]
+            at = pl.multiple_of((2 * d + 1) * half, half)
+            two_ref[bits["c"], bits["y"], bits["x"], bits["z1"], bits["z2"]] = full_ref[pl.ds(at, half), lanes]
+
+
+def project_grad(place, normed, dmixed, sides):
+    vmem = pl.BlockSpec(memory_space=pltpu.VMEM)
+    half = jax.ShapeDtypeStruct((2, 2, 2, 2, 2, D // DP_BLOCKS // 2, QKV // sides), BF16)
+    return pl.pallas_call(
+        project_grad_kernel,
+        out_shape=(half, half),
+        in_specs=[pl.BlockSpec(memory_space=pltpu.SMEM)] + [vmem] * 4,
+        out_specs=(vmem, vmem),
+        scratch_shapes=[pltpu.VMEM((D, QKV), BF16)],
+        compiler_params=params(),
+        name="project_grad",
+    )(place, normed, *dmixed)
+
+
+def project_back_kernel(
+    dq_ref, dk_ref, dv_ref, weight_ref, x_ref, dmid_ref, g1_ref, gtok_ref, small_ref, dx_ref, wide_ref
+):
+    dy = None
+    for kind, source_ref in enumerate((dq_ref, dk_ref, dv_ref)):
+        term = dot(source_ref[...], weight_ref[:, kind * D : (kind + 1) * D], ((1,), (1,)))
+        dy = term if dy is None else dy + term
+    centred, rs = layer_stats(x_ref[...].astype(F32), D)
+    vhat = centred * rs
+    small_ref[0:1, :] = jnp.sum(dy * vhat, axis=0, keepdims=True)
+    small_ref[1:2, :] = jnp.sum(dy, axis=0, keepdims=True)
+    small_ref[2:8, :] = jnp.zeros((6, D), F32)
+    scaled = dy * g1_ref[...]
+    first = jnp.sum(scaled, axis=1, keepdims=True) * (1.0 / D)
+    second = jnp.sum(scaled * vhat, axis=1, keepdims=True) * (1.0 / D)
+    dx_ref[...] = dmid_ref[...] + rs * (scaled - first - vhat * second)
+
+    @pl.loop(0, PLACES)
+    def _(place):
+        at = pl.multiple_of(place * FRAMES, FRAMES)
+        write_place(wide_ref, place, dx_ref[pl.ds(at, FRAMES), :])
+
+    for tile in range(D // LANES):
+        gtok_ref[:, tile * LANES : (tile + 1) * LANES] = wide_ref[tile]
+
+
+def project_back(dmixed, weight, x, dmid, g1):
+    vmem = pl.BlockSpec(memory_space=pltpu.VMEM)
+    return pl.pallas_call(
+        project_back_kernel,
+        out_shape=(jax.ShapeDtypeStruct((ROWS, D), F32), jax.ShapeDtypeStruct((8, D), F32)),
+        in_specs=[vmem] * 7,
+        out_specs=(vmem, vmem),
+        scratch_shapes=[pltpu.VMEM((ROWS, D), F32), wide_scratch(D)],
+        compiler_params=params(),
+        name="project_back",
+    )(*dmixed, weight, x, dmid, g1)
 
 
 def row(vector):
@@ -780,10 +859,104 @@
     return jnp.pad(array, [(0, 0)] * (array.ndim - 1) + [(0, LANES - HEAD_DIM)])
 
 
-def clip_work(
-    tokens, prev_kv, memory, valid_frames, mem_len, ln1_gain, ln1_bias, qkv_bias, pool_conv, pool_gain, pool_bias,
-    rel_time, rel_space, compress, proj_bias, ln2_gain, ln2_bias, fc1_bias, fc2_bias, cotangent, gathered,
+DP_BLOCKS = 8
+ROUTE_ONE = ("z2", "z1", "y", "x", "c")
+ROUTE_TWO = ("z2", "z1", "x", "y", "c")
+BIT = {"x": ("dp", 1), "z1": ("dp", 2), "z2": ("dp", 4), "y": ("fsdp", 2), "c": ("fsdp", 1)}
+
+
+def swap(values, name, sizes):
+    axis, bit = BIT[name]
+    return lax.ppermute(values, axis, [(at, at ^ bit) for at in range(sizes[axis])])
+
+
+def together(*values):
+    return lax.optimization_barrier(values)
+
+
+def flat_shard(one, two, proj):
+    parts = tiles_of(one) + tiles_of(two.T)
+    part = proj.shape[1]
+    parts += [proj[:, :LANES], jnp.pad(proj[:, LANES:], ((0, 0), (0, 2 * LANES - part)))]
+    return jnp.concatenate(parts, axis=0)
+
+
+class Staged:
+    def __init__(self):
+        self.sizes = {"dp": 8, "fsdp": 4}
+
+    def place(self):
+        dp, fsdp = lax.axis_index("dp"), lax.axis_index("fsdp")
+        return jnp.stack([dp & 1, (dp >> 1) & 1, (dp >> 2) & 1, (fsdp >> 1) & 1, fsdp & 1]).astype(jnp.int32)
+
+    def first_weights(self, shard):
+        half = shard.shape[0] // 2
+        one, two = shard[None, :half], shard[None, half:]
+        for a, b in zip(ROUTE_ONE, ROUTE_TWO):
+            more_one, more_two = swap(one, a, self.sizes), swap(two, b, self.sizes)
+            one, two = jnp.concatenate([one, more_one]), jnp.concatenate([two, more_two])
+        return one, two
+
+    def other_weights(self, one, two, proj, after):
+        flat, _ = together(flat_shard(one, two, proj), after)
+        return lax.all_gather(flat, ("dp", "fsdp"), axis=0, tiled=False).reshape((8, 4) + flat.shape)
+
+    def halve(self, blocks, name):
+        return blocks[0], swap(blocks[1], name, self.sizes)
+
+    def total(self, vector):
+        for name in ("c", "x", "y", "z1", "z2"):
+            vector = vector + swap(vector, name, self.sizes)
+        return vector
+
+
+class Plain:
+    def __init__(self, dp, fsdp):
+        self.dp, self.fsdp = dp, fsdp
+
+    def place(self):
+        return jnp.zeros((5,), jnp.int32)
+
+    def gather(self, shard):
+        blocks = lax.all_gather(shard, ("dp", "fsdp"), axis=0, tiled=False)
+        rows, columns = shard.shape
+        joined = blocks.reshape(DP_BLOCKS, self.dp // DP_BLOCKS, self.fsdp, rows, columns).transpose(0, 2, 1, 3, 4)
+        return joined.reshape(DP_BLOCKS, self.fsdp, self.dp // DP_BLOCKS * rows, columns)
+
+    def first_weights(self, shard):
+        blocks = self.gather(shard)
+        half, columns = blocks.shape[2] // 2, blocks.shape[3]
+        bits = blocks.reshape(2, 2, 2, 2, 2, 2, half, columns)
+        at = {"z2": 0, "z1": 1, "x": 2, "y": 3, "c": 4}
+        return tuple(
+            bits.transpose([at[name] for name in reversed(route)] + [5, 6, 7])[:, :, :, :, :, side].reshape(
+                32, half, columns
+            )
+            for side, route in enumerate((ROUTE_ONE, ROUTE_TWO))
+        )
+
+    def other_weights(self, one, two, proj, after):
+        return jax.vmap(jax.vmap(flat_shard))(self.gather(one), self.gather(two), self.gather(proj))
+
+    def scatter(self, blocks, route):
+        at = {name: 4 - where for where, name in enumerate(route)}
+        rows, columns = blocks.shape[5:]
+        blocks = blocks.transpose([at[name] for name in ("z2", "z1", "x", "y", "c")] + [5, 6])
+        split = blocks.reshape(DP_BLOCKS, self.fsdp, self.dp // DP_BLOCKS, rows * DP_BLOCKS // self.dp, columns)
+        split = split.transpose(0, 2, 1, 3, 4).reshape(self.dp * self.fsdp, -1, columns)
+        return lax.psum_scatter(split, ("dp", "fsdp"), scatter_dimension=0, tiled=False).astype(F32)
+
+    def total(self, vector):
+        return lax.psum(vector, ("dp", "fsdp"))
+
+
+def run(
+    comm, staged, tokens, prev_kv, memory, valid_frames, mem_len, ln1_gain, ln1_bias, w_qkv, qkv_bias, pool_conv, pool_gain,
+    pool_bias, rel_time, rel_space, compress, w_proj, proj_bias, ln2_gain, ln2_bias, w_fc1, fc1_bias, w_fc2,
+    fc2_bias, cotangent,
 ):
+    place = comm.place()
+    first, second = comm.first_weights(w_qkv)
     one_hot, own, fold, pick = (jnp.asarray(c, BF16) for c in constants())
     tables = jnp.concatenate([rel_time, rel_space[0], rel_space[1]], axis=0)
     tables = jnp.pad(tables, ((0, LANES - tables.shape[0]), (0, LANES - HEAD_DIM)))
@@ -793,84 +966,79 @@
         valid_frames, mem_len, tokens, cotangent, row(ln1_gain), row(ln1_bias), one_hot, tables, pick
     )
     rest, parts = squeeze(prev_kv, memory, tiled_lanes(compress))
-    w_qkv, w_proj, w_fc1, w_fc2 = gathered
-    heads, vhat, mixed, weight = query_key_value(valid_frames, normed, w_qkv, row(qkv_bias), taps, gains, biases)
+    flat = comm.other_weights(w_fc1, w_fc2, w_proj, first)
+    heads, vhat, mixed, weight = query_key_value(
+        valid_frames, place, normed, first, second, row(qkv_bias), taps, gains, biases
+    )
     weights, pv, attended = attend(heads, rest, aug, table, own, fold)
     out, dmid, datt, gp, gw1, gw2, small_two, gb1 = feed_forward(
-        attended, x, upstream, w_proj, w_fc1, w_fc2, row(proj_bias), row(ln2_gain), row(ln2_bias),
-        row(fc1_bias), row(fc2_bias),
+        place, attended, x, upstream, flat, row(proj_bias), row(ln2_gain), row(ln2_bias), row(fc1_bias), row(fc2_bias)
     )
-    grads, gtable, gcompress = attend_back(heads, rest, aug, table, own, fold, pick, weights, pv, datt, parts)
-    gtok, gqkv, gqkv_bias, gtaps, gpool, small_one = qkv_back(
-        valid_frames, grads, vhat, mixed, weight, normed, x, dmid, taps, gains, row(ln1_gain)
-    )
-    gconv = jnp.sum(gtaps.reshape(3, 2, 27, GROUP_HEADS, HEAD_DIM), axis=(1, 3))
-    gpool = jnp.sum(gpool.reshape(3, HEADS, 2, LANES), axis=1)[:, :, :HEAD_DIM]
+    middle = {"proj": (gp, ROUTE_TWO), "one": (gw1, ROUTE_ONE), "two": (gw2, ROUTE_TWO)}
+    big, routes = {k: v[0] for k, v in middle.items()}, {k: v[1] for k, v in middle.items()}
+
+    def start(stage):
+        return {k: comm.halve(big[k], routes[k][4 - stage]) for k in big} if staged else None
+
+    def finish(moving, *after):
+        if not staged:
+            return after
+        flying = [v for pair in moving.values() for v in pair]
+        tied = together(*flying, *after)
+        for at, k in enumerate(moving):
+            big[k] = tied[2 * at] + tied[2 * at + 1]
+        return tied[2 * len(moving) :]
+
+    def back(start_head, datt):
+        return attend_back(
+            start_head, HEADS // 2, heads, rest, aug, table, own, fold, pick, weights, pv, datt, parts
+        )
+
+    moving = start(0)
+    grads_a, gtable_a, gcompress_a = back(0, datt)
+    (grads_a, datt) = finish(moving, grads_a, datt)
+    moving = start(1)
+    grads_b, gtable_b, gcompress_b = back(HEADS // 2, datt)
+    (grads_a, grads_b) = finish(moving, grads_a, grads_b)
+    dmixed, gbias, gtaps, gpool = [], [], [], []
+    for kind in range(3):
+        moving = start(2 + kind)
+        pieces = pool_back(kind, valid_frames, grads_a, grads_b, vhat, mixed, taps, gains)
+        (piece, grads_a) = finish(moving, pieces[0], grads_a)
+        dmixed.append(piece)
+        gbias.append(pieces[1])
+        gtaps.append(pieces[2])
+        gpool.append(pieces[3])
+    qkv_one, qkv_two = project_grad(place, normed, dmixed, QKV // w_qkv.shape[1])
+    if staged:
+        for stage in range(5):
+            kept_one, more_one = comm.halve(qkv_one, ROUTE_ONE[4 - stage])
+            kept_two, more_two = comm.halve(qkv_two, ROUTE_TWO[4 - stage])
+            qkv_one, qkv_two = kept_one + more_one, kept_two + more_two
+    gtok, small_one = project_back(dmixed, weight, x, dmid, row(ln1_gain))
+    gconv = jnp.sum(jnp.stack(gtaps).reshape(3, 2, 27, GROUP_HEADS, HEAD_DIM), axis=(1, 3))
+    gpool = jnp.sum(jnp.stack(gpool), axis=1)[:, :, :HEAD_DIM]
+    gtable, gcompress = gtable_a + gtable_b, gcompress_a + gcompress_b
     smalls = (
-        small_one[0], small_one[1], gqkv_bias[0], gconv, gpool[:, 0], gpool[:, 1],
+        small_one[0], small_one[1], jnp.concatenate(gbias, axis=1)[0], gconv, gpool[:, 0], gpool[:, 1],
         gtable[:15, :HEAD_DIM], gtable[15:53, :HEAD_DIM].reshape(2, 19, HEAD_DIM), gcompress[:, :, :HEAD_DIM],
         small_two[0], small_two[1], small_two[2], gb1[0], small_two[3],
     )
-    return out, gtok, (gqkv, gp, gw1, gw2), smalls
-
-
-DP_BLOCKS = 8
-
-
-def canonical(gathered, dp, fsdp):
-    rows, columns = gathered.shape[2:]
-    if dp == DP_BLOCKS:
-        return gathered
-    joined = gathered.reshape(DP_BLOCKS, dp // DP_BLOCKS, fsdp, rows, columns).transpose(0, 2, 1, 3, 4)
-    return joined.reshape(DP_BLOCKS, fsdp, dp // DP_BLOCKS * rows, columns)
-
-
-def device_blocks(blocks, dp, fsdp):
-    rows, columns = blocks.shape[2:]
-    if dp == DP_BLOCKS:
-        return blocks
-    split = blocks.reshape(DP_BLOCKS, fsdp, dp // DP_BLOCKS, rows * DP_BLOCKS // dp, columns).transpose(0, 2, 1, 3, 4)
-    return split.reshape(dp, fsdp, rows * DP_BLOCKS // dp, columns)
-
-
-def on_device(dp, fsdp):
-    axes = ("dp", "fsdp")
-
-    def gather(shard):
-        flat = lax.all_gather(shard, axes, axis=0, tiled=False)
-        return canonical(flat.reshape((dp, fsdp) + shard.shape), dp, fsdp)
-
-    def scatter(blocks):
-        split = device_blocks(blocks, dp, fsdp)
-        split = split.reshape((dp * fsdp,) + split.shape[2:])
-        return lax.psum_scatter(split, axes, scatter_dimension=0, tiled=False).astype(F32)
-
-    def run(
-        tokens, prev_kv, memory, valid_frames, mem_len, ln1_gain, ln1_bias, w_qkv, qkv_bias, pool_conv, pool_gain,
-        pool_bias, rel_time, rel_space, compress, w_proj, proj_bias, ln2_gain, ln2_bias, w_fc1, fc1_bias, w_fc2,
-        fc2_bias, cotangent,
-    ):
-        gathered = tuple(gather(shard) for shard in (w_qkv, w_proj, w_fc1, w_fc2))
-        out, gtok, big, smalls = clip_work(
-            tokens, prev_kv, memory, valid_frames, mem_len, ln1_gain, ln1_bias, qkv_bias, pool_conv, pool_gain,
-            pool_bias, rel_time, rel_space, compress, proj_bias, ln2_gain, ln2_bias, fc1_bias, fc2_bias, cotangent,
-            gathered,
-        )
-        gqkv, gp, gw1, gw2 = big
-        gqkv = gqkv.reshape(DP_BLOCKS, D // DP_BLOCKS, fsdp, QKV // fsdp).transpose(0, 2, 1, 3)
-        sums = [scatter(g) for g in (gqkv, gp, gw1, gw2)]
-        flat = jnp.concatenate([s.reshape(-1) for s in smalls])
-        flat = lax.psum(flat, axes)
-        totals, at = [], 0
-        for s in smalls:
-            totals.append(flat[at : at + s.size].reshape(s.shape))
-            at += s.size
-        return (
-            out, gtok, totals[0], totals[1], sums[0], totals[2], totals[3], totals[4], totals[5], totals[6],
-            totals[7], totals[8], sums[1], totals[9], totals[10], totals[11], sums[2], totals[12], sums[3], totals[13],
-        )
-
-    return run
+    vector = comm.total(jnp.concatenate([s.reshape(-1) for s in smalls]))
+    totals, at = [], 0
+    for s in smalls:
+        totals.append(vector[at : at + s.size].reshape(s.shape))
+        at += s.size
+    if staged:
+        qkv = jnp.concatenate([qkv_one, qkv_two], axis=0).astype(F32)
+        sums = [qkv] + [big[k].astype(F32) for k in ("proj", "one", "two")]
+    else:
+        qkv_one = comm.scatter(jnp.concatenate([qkv_one, jnp.moveaxis(qkv_two, 1, 2)], axis=5), ROUTE_ONE)
+        sums = [qkv_one] + [comm.scatter(big[k], routes[k]) for k in ("proj", "one", "two")]
+    return (
+        out, gtok, totals[0], totals[1], sums[0], totals[2], totals[3], totals[4], totals[5], totals[6],
+        totals[7], totals[8], sums[1], totals[9], totals[10], totals[11], sums[2], totals[12], sums[3], totals[13],
+    )
 
 
 def solution(mesh):
@@ -879,8 +1047,10 @@
     second = P(None, ("dp", "fsdp"), None)
     blocks = P("dp", "fsdp")
     none = P()
+    dp, fsdp = mesh.shape["dp"], mesh.shape["fsdp"]
+    staged = (dp, fsdp) == (8, 4)
     return jax.shard_map(
-        on_device(mesh.shape["dp"], mesh.shape["fsdp"]),
+        functools.partial(run, Staged() if staged else Plain(dp, fsdp), staged),
         mesh=mesh,
         in_specs=(
             rows, second, second, both, both, none, none, blocks, none, none, none, none, none, none, none, blocks,

time: 991 us -> 496 us (0.50)
  waiting for transfers between devices: 664 us -> 81.7 us
  starting transfers between devices: 0.35 us -> 46.7 us
  Pallas kernels: 240 us -> 260 us
  other arithmetic: 10.3 us -> 21.1 us
    reduce_scatter x4 -> x0, waiting for transfers between devices: 419 us -> none  [scatter(): lax.psum_scatter(split, axes, scatter_dimension=0, tiled=False).astype(F32)]
    all_gather x4 -> x1, waiting for transfers between devices: 145 us -> 0.01 us  [other_weights(): lax.all_gather(flat, ('dp', 'fsdp'), axis=0, tiled=False)]
    psum x1 -> x0, waiting for transfers between devices: 95.8 us -> none  [run(): flat = lax.psum(flat, axes)]
    ppermute x0 -> x40, waiting for transfers between devices: none -> 81.7 us  [swap(): lax.ppermute(values, axis, [(at, at ^ bit) for at in range(sizes[axis])])]
    ppermute x0 -> x40, starting transfers between devices: none -> 46.7 us  [swap(): lax.ppermute(values, axis, [(at, at ^ bit) for at in range(sizes[axis])])]
    squeeze x1 -> x29, local copies, waits for them, and re-layouts: 0.01 us -> 23.1 us  [the longest x28 23.1 us: halve(): return (blocks[0], swap(blocks[1], name, self.sizes))]
    reshape x12 -> x5, local copies, waits for them, and re-layouts: 23 us -> 1.02 us  [the longest x2 0.78 us: run(): totals.append(vector[at:at + s.size].reshape(s.shape))]
    pallas_call x3 -> x8, Pallas kernels: 157 us -> 176 us  [the longest x3 52.2 us: pool_back(): pl.pallas_call(pool_back_kernel, grid=(2,), out_shape=(jax.ShapeDtypeStru...]
  transfers between devices with their start and end apart: 9 -> 41, of which waited for: 8 -> 21; matrix products, arithmetic and copies ran while one was open for 6% -> 13% of each run, Pallas kernels for 8% -> 38%
where the time goes in v2:
time: 496 us; the launch traced here: 488 us
  Pallas kernels  260 us (52%)
  waiting for transfers between devices  81.7 us (16%)
  local copies, waits for them, and re-layouts  62.3 us (13%)
  starting transfers between devices  46.7 us (9%)
  other arithmetic  21.1 us (4%)
  between operations  16.9 us (3%)
    ppermute x40, waiting for transfers between devices, swap(): lax.ppermute(values, axis, [(at, at ^ bit) for at in range(sizes[axis])])  81.7 us
    pallas_call x3, Pallas kernels, pool_back(): pl.pallas_call(pool_back_kernel, grid=(2,), out_shape=(jax.ShapeDtypeStru...  52.2 us
    pallas_call x1, Pallas kernels, feed_forward(): pl.pallas_call(middle_kernel, out_shape=(jax.ShapeDtypeStruct((ROWS, D),...  51.3 us
    pallas_call x2, Pallas kernels, attend_back(): pl.pallas_call(attend_back_kernel, grid=(count,), out_shape=(jax.ShapeDty...  51 us
    ppermute x40, starting transfers between devices, swap(): lax.ppermute(values, axis, [(at, at ^ bit) for at in range(sizes[axis])])  46.7 us
    pallas_call x1, Pallas kernels, attend(): pl.pallas_call(attend_kernel, grid=(HEADS,), out_shape=(jax.ShapeDtypeStr...  36.4 us
    pallas_call x1, Pallas kernels, query_key_value(): pl.pallas_call(qkv_kernel, grid=(6,), out_shape=(jax.ShapeDtypeStruct((3...  36.2 us
    squeeze x28, local copies, waits for them, and re-layouts, halve(): return (blocks[0], swap(blocks[1], name, self.sizes))  23.1 us
  transfers between devices with their start and end apart: 41, of which 21 were waited for; matrix products, arithmetic and copies ran while one was open for 13% of the time, Pallas kernels for 38%

profile of v2, /device:TPU:0, one launch (start us, length us, event | category | flops | bytes accessed | tf_op | source)
XLA Modules:
  0.0 488.3 jit_solution(9578096915756047192)
XLA Ops:
  8.1 4.1 collective-permute-start
  31.9 5.9 %collective-permute-done.3 = bf16[8,48,576]{2,1,0:T(8,128)(2,1)S(1)} collective-permute-done((bf16[8,48,576]{2,1,0:T(8,128)(2,1)S(1)}, bf16[8,48,576]{2,1,0:T(8,128)(2,1)S(1)}, u32[]{:S(2)}, u32[]{:S(2)}) %collective-permute-start.3) | collective-permute-done | bytes 442400 | tf_op jit(solution)/shard_map/ppermute | solution.py:870
  50.0 4.9 %collective-permute-done.6 = bf16[2,48,576]{2,1,0:T(8,128)(2,1)S(1)} collective-permute-done((bf16[2,48,576]{2,1,0:T(8,128)(2,1)S(1)}, bf16[2,48,576]{2,1,0:T(8,128)(2,1)S(1)}, u32[]{:S(2)}, u32[]{:S(2)}) %collective-permute-start.6) | collective-permute-done | bytes 110624 | tf_op jit(solution)/shard_map/ppermute | solution.py:870
  56.7 6.4 %collective-permute-done.7 = bf16[4,48,576]{2,1,0:T(8,128)(2,1)S(1)} collective-permute-done((bf16[4,48,576]{2,1,0:T(8,128)(2,1)S(1)}, bf16[4,48,576]{2,1,0:T(8,128)(2,1)S(1)}, u32[]{:S(2)}, u32[]{:S(2)}) %collective-permute-start.7) | collective-permute-done | bytes 221216 | tf_op jit(solution)/shard_map/ppermute | solution.py:870
  66.7 11.9 %collective-permute-done.8 = bf16[8,48,576]{2,1,0:T(8,128)(2,1)S(1)} collective-permute-done((bf16[8,48,576]{2,1,0:T(8,128)(2,1)S(1)}, bf16[8,48,576]{2,1,0:T(8,128)(2,1)S(1)}, u32[]{:S(2)}, u32[]{:S(2)}) %collective-permute-start.8) | collective-permute-done | bytes 442400 | tf_op jit(solution)/shard_map/ppermute | solution.py:870
  86.7 5.9 %squeeze.241 = (bf16[2,8,480,128]{3,2,1,0:T(8,128)(2,1)}, bf16[2,8,4,208,128]{4,3,2,1,0:T(8,128)(2,1)}) custom-call(bf16[2,800,768]{2,1,0:T(8,128)(2,1)} %prev_ref.1, bf16[2,200,768]{2,1,0:T(8,128)(2,1)} %mem_ref.1, f32[2,4,384]{2,1,0:T(4,128)} %pad_maximum_fusion.7.taps_ref), custom_call_target="tpu_custom_call" | custom-call | tf_op jit(solution)/shard_map/squeeze/pallas_call | solution.py:197
  94.0 5.4 %prepare.1 = (bf16[800,768]{1,0:T(8,128)(2,1)}, bf16[800,768]{1,0:T(8,128)(2,1)}, bf16[800,768]{1,0:T(8,128)(2,1)}, bf16[1280,128]{1,0:T(8,128)(2,1)}, bf16[384,128]{1,0:T(8,128)(2,1)}) custom-call(s32[1]{0:T(128)S(6)} %copy.103.frames_ref, s32[1]{0:T(128)S(6)} %copy.104.length_ref, bf16[800,768]{1,0:T(8,128)(2,1)} %tokens_ref.1, bf16[800,768]{1,0:T(8,128)(2,1)} %cot_ref.1, ...), custom_call_target="tpu_custom_call" | custom-call | tf_op jit(solution)/shard_map/prepare/pallas_call | solution.py:140
  101.3 36.2 %query_key_value.1 = (bf16[24,800,128]{2,1,0:T(8,128)(2,1)}, bf16[24,800,128]{2,1,0:T(8,128)(2,1)}, bf16[800,2304]{1,0:T(8,128)(2,1)}, bf16[768,2304]{1,0:T(8,128)(2,1)}) custom-call(s32[1]{0:T(128)S(6)} %copy.103.frames_ref, s32[5]{0:T(128)} %stack.47.place_ref, bf16[800,768]{1,0:T(8,128)(2,1)} %get-tuple-element.104.normed_ref, ...), custom_call_target="tpu_custom_call" | custom-call | tf_op jit(solution)/shard_map/query_key_value/pallas_call | solution.py:311
  137.5 36.4 %attend.1 = (bf16[8,800,1280]{2,1,0:T(8,128)(2,1)}, bf16[8,800,128]{2,1,0:T(8,128)(2,1)}, bf16[8,800,128]{2,1,0:T(8,128)(2,1)}) custom-call(bf16[24,800,128]{2,1,0:T(8,128)(2,1)} %get-tuple-element.105.q_ref.k_ref.v_ref, bf16[24,800,128]{2,1,0:T(8,128)(2,1)} %get-tuple-element.105.q_ref.k_ref.v_ref, ...), custom_call_target="tpu_custom_call" | custom-call | tf_op jit(solution)/shard_map/attend/pallas_call | solution.py:382
  173.9 51.3 %feed_forward.1 = (bf16[800,768]{1,0:T(8,128)(2,1)}, f32[800,768]{1,0:T(8,128)}, bf16[8,800,128]{2,1,0:T(8,128)(2,1)}, bf16[2,2,2,2,2,96,192]{6,5,4,3,2,1,0:T(8,...) custom-call(s32[5]{0:T(128)} %stack.47.place_ref, ...), custom_call_target="tpu_custom_call" | custom-call | tf_op jit(solution)/shard_map/feed_forward/pallas_call | solution.py:529
  225.2 5.1 %slice_bitcast_fusion.2 = (bf16[2,2,2,2,96,768]{5,4,3,2,1,0:T(8,128)(2,1)}, bf16[2,2,2,2,96,768]{5,4,3,2,1,0:T(8,128)(2,1)}) fusion(bf16[2,2,2,2,2,96,768]{6,5,4,3,2,1,0:T(8,128)(2,1)} %get-tuple-element.115), kind=kLoop, calls=%fused_computation.2 | loop fusion | bytes 9437184 | tf_op jit(solution)/shard_map/squeeze | solution.py:905
  233.0 4.7 copy.60
  240.9 25.3 %attend_back.2 = (bf16[3,4,800,128]{3,2,1,0:T(8,128)(2,1)}, f32[128,128]{1,0:T(8,128)}, f32[2,4,128]{2,1,0:T(4,128)}) custom-call(bf16[24,800,128]{2,1,0:T(8,128)(2,1)} %get-tuple-element.105.q_ref.k_ref.v_ref, bf16[24,800,128]{2,1,0:T(8,128)(2,1)} %get-tuple-element.105.q_ref.k_ref.v_ref, bf16[24,800,128]{2,1,0:T(8,128)(2,1)} %get-tuple-element.105.q_ref.k_ref.v_ref, ...), custom_call_target="tpu_custom_call" | custom-call | tf_op jit(solution)/shard_map/attend_back/pallas_call | solution.py:649
  270.9 4.5 copy.61
  284.4 25.6 %attend_back.3 = (bf16[3,4,800,128]{3,2,1,0:T(8,128)(2,1)}, f32[128,128]{1,0:T(8,128)}, f32[2,4,128]{2,1,0:T(4,128)}) custom-call(bf16[24,800,128]{2,1,0:T(8,128)(2,1)} %get-tuple-element.105.q_ref.k_ref.v_ref, bf16[24,800,128]{2,1,0:T(8,128)(2,1)} %get-tuple-element.105.q_ref.k_ref.v_ref, bf16[24,800,128]{2,1,0:T(8,128)(2,1)} %get-tuple-element.105.q_ref.k_ref.v_ref, ...), custom_call_target="tpu_custom_call" | custom-call | tf_op jit(solution)/shard_map/attend_back/pallas_call | solution.py:649
  310.1 7.4 %collective-permute-done.13 = bf16[2,2,2,96,192]{4,3,2,1,0:T(8,128)(2,1)S(1)} collective-permute-done((bf16[2,2,2,96,192]{4,3,2,1,0:T(8,128)(2,1)S(1)}, bf16[2,2,2,96,192]{4,3,2,1,0:T(8,128)(2,1)S(1)}, u32[]{:S(2)}, u32[]{:S(2)}) %collective-permute-start.13) | collective-permute-done | bytes 294944 | tf_op jit(solution)/shard_map/ppermute | solution.py:870
  327.6 17.4 %pool_back_0.1 = (bf16[800,768]{1,0:T(8,128)(2,1)}, f32[1,768]{1,0:T(1,128)}, f32[2,27,384]{2,1,0:T(8,128)}, f32[8,2,128]{2,1,0:T(2,128)}) custom-call(s32[1]{0:T(128)S(6)} %copy.103.frames_ref, bf16[3,4,800,128]{3,2,1,0:T(8,128)(2,1)} %get-tuple-element.158.first_ref, bf16[3,4,800,128]{3,2,1,0:T(8,128)(2,1)} %get-tuple-element.138.second_ref, ...), custom_call_target="tpu_custom_call" | custom-call | tf_op jit(solution)/shard_map/pool_back_0/pallas_call | solution.py:745
  351.7 17.3 %pool_back_1.1 = (bf16[800,768]{1,0:T(8,128)(2,1)}, f32[1,768]{1,0:T(1,128)}, f32[2,27,384]{2,1,0:T(8,128)}, f32[8,2,128]{2,1,0:T(2,128)}) custom-call(s32[1]{0:T(128)S(6)} %copy.103.frames_ref, bf16[3,4,800,128]{3,2,1,0:T(8,128)(2,1)} %get-tuple-element.158.first_ref, bf16[3,4,800,128]{3,2,1,0:T(8,128)(2,1)} %get-tuple-element.138.second_ref, ...), custom_call_target="tpu_custom_call" | custom-call | tf_op jit(solution)/shard_map/pool_back_1/pallas_call | solution.py:745
  374.7 17.5 %pool_back_2.1 = (bf16[800,768]{1,0:T(8,128)(2,1)}, f32[1,768]{1,0:T(1,128)}, f32[2,27,384]{2,1,0:T(8,128)}, f32[8,2,128]{2,1,0:T(2,128)}) custom-call(s32[1]{0:T(128)S(6)} %copy.103.frames_ref, bf16[3,4,800,128]{3,2,1,0:T(8,128)(2,1)} %get-tuple-element.158.first_ref, bf16[3,4,800,128]{3,2,1,0:T(8,128)(2,1)} %get-tuple-element.138.second_ref, ...), custom_call_target="tpu_custom_call" | custom-call | tf_op jit(solution)/shard_map/pool_back_2/pallas_call | solution.py:745
  397.3 10.3 %project_grad.1 = (bf16[2,2,2,2,2,48,576]{6,5,4,3,2,1,0:T(8,128)(2,1)}, bf16[2,2,2,2,2,48,576]{6,5,4,3,2,1,0:T(8,128)(2,1)}) custom-call(s32[5]{0:T(128)} %stack.47.place_ref, bf16[800,768]{1,0:T(8,128)(2,1)} %get-tuple-element.104.normed_ref, bf16[800,768]{1,0:T(8,128)(2,1)} %get-tuple-element.142.dq_ref, bf16[800,768]{1,0:T(8,128)(2,1)} %get-tuple-element.151.dk_ref, ...), custom_call_target="tpu_custom_call" | custom-call | tf_op jit(solution)/shard_map/project_grad/pallas_call | solution.py:800
  407.7 10.8 %project_back.1 = (f32[800,768]{1,0:T(8,128)}, f32[8,768]{1,0:T(8,128)}) custom-call(bf16[800,768]{1,0:T(8,128)(2,1)} %get-tuple-element.142.dq_ref, bf16[800,768]{1,0:T(8,128)(2,1)} %get-tuple-element.151.dk_ref, bf16[800,768]{1,0:T(8,128)(2,1)} %get-tuple-element.160.dv_ref, bf16[768,2304]{1,0:T(8,128)(2,1)} %get-tuple-element.161.weight_ref, ...), custom_call_target="tpu_custom_call" | custom-call | tf_op jit(solution)/shard_map/project_back/pallas_call | solution.py:839
  426.1 4.3 collective-permute-done.27
  452.6 6.1 %collective-permute-done.36 = bf16[2,2,2,48,576]{4,3,2,1,0:T(8,128)(2,1)S(1)} collective-permute-done((bf16[2,2,2,48,576]{4,3,2,1,0:T(8,128)(2,1)S(1)}, bf16[2,2,2,48,576]{4,3,2,1,0:T(8,128)(2,1)S(1)}, u32[]{:S(2)}, u32[]{:S(2)}) %collective-permute-start.36) | collective-permute-done | bytes 442400 | tf_op jit(solution)/shard_map/ppermute | solution.py:870
  476.0 4.2 collective-permute-done.34
  (302 shorter events, 142.3 us)
Async XLA Ops:
  7.2 166.7 %all-gather.3.cloned.1.call-start = ((), (), s32[]{:S(2)}) async-start(), calls=%async_computation | async-start | bytes 11354112 | tf_op jit(solution)/shard_map/all_gather | solution.py:902
  8.1 7.9 %collective-permute-start = (bf16[1,48,576]{2,1,0:T(8,128)(2,1)S(1)}, bf16[1,48,576]{2,1,0:T(8,128)(2,1)S(1)}, u32[]{:S(2)}, u32[]{:S(2)}) collective-permute-start(bf16[1,48,576]{2,1,0:T(8,128)(2,1)S(1)} %get-tuple-element.299), channel_id=1, source_target_pairs={{0,16},{4,20},{8,24},{12,28},{16,0},{20,4},{24,8},{28,12},{1,17},{... | collective-permute-start | bytes 165896 | tf_op jit(solution)/shard_map/ppermute | solution.py:870
  27.4 10.4 %collective-permute-start.3 = (bf16[8,48,576]{2,1,0:T(8,128)(2,1)S(1)}, bf16[8,48,576]{2,1,0:T(8,128)(2,1)S(1)}, u32[]{:S(2)}, u32[]{:S(2)}) collective-permute-start(bf16[8,48,576]{2,1,0:T(8,128)(2,1)S(1)} %pad_maximum_fusion), channel_id=1, source_target_pairs={{0,4},{4,0},{8,12},{12,8},{16,20},{20,16},{24,28},{28,24},{1,5},{5... | collective-permute-start | bytes 1327112 | tf_op jit(solution)/shard_map/ppermute | solution.py:870
  55.1 7.9 %collective-permute-start.7 = (bf16[4,48,576]{2,1,0:T(8,128)(2,1)S(1)}, bf16[4,48,576]{2,1,0:T(8,128)(2,1)S(1)}, u32[]{:S(2)}, u32[]{:S(2)}) collective-permute-start(bf16[4,48,576]{2,1,0:T(8,128)(2,1)S(1)} %pad_maximum_fusion.3), channel_id=1, source_target_pairs={{0,4},{4,0},{8,12},{12,8},{16,20},{20,16},{24,28},{28,24},{1,5},{5... | collective-permute-start | bytes 663560 | tf_op jit(solution)/shard_map/ppermute | solution.py:870
  63.1 15.5 %collective-permute-start.8 = (bf16[8,48,576]{2,1,0:T(8,128)(2,1)S(1)}, bf16[8,48,576]{2,1,0:T(8,128)(2,1)S(1)}, u32[]{:S(2)}, u32[]{:S(2)}) collective-permute-start(bf16[8,48,576]{2,1,0:T(8,128)(2,1)S(1)} %pad_maximum_fusion.1), channel_id=1, source_target_pairs={{0,2},{1,3},{2,0},{3,1},{4,6},{5,7},{6,4},{7,5},{8,10},{9,11},{10,... | collective-permute-start | bytes 1327112 | tf_op jit(solution)/shard_map/ppermute | solution.py:870
  79.5 20.1 %collective-permute-start.9 = (bf16[16,48,576]{2,1,0:T(8,128)(2,1)}, bf16[16,48,576]{2,1,0:T(8,128)(2,1)S(1)}, u32[]{:S(2)}, u32[]{:S(2)}) collective-permute-start(bf16[16,48,576]{2,1,0:T(8,128)(2,1)} %get-tuple-element.276), channel_id=1, source_target_pairs={{0,1},{1,0},{2,3},{3,2},{4,5},{5,4},{6,7},{7,6},{8,9},{9,8},{10,11... | collective-permute-start | bytes 2654216 | tf_op jit(solution)/shard_map/ppermute | solution.py:870
  230.3 36.0 %collective-permute-start.11 = (bf16[2,2,2,2,96,768]{5,4,3,2,1,0:T(8,128)(2,1)}, bf16[2,2,2,2,96,768]{5,4,3,2,1,0:T(8,128)(2,1)}, u32[]{:S(2)}, u32[]{:S(2)}) collective-permute-start(bf16[2,2,2,2,96,768]{5,4,3,2,1,0:T(8,128)(2,1)} %get-tuple-element.258), channel_id=1, source_target_pairs={{0,1},{1,0},{2,3},{3,2},{4,5},{5,4},{6,7},{7,6},{8,9},{9,8},{10,11... | collective-permute-start | bytes 7077896 | tf_op jit(solution)/shard_map/ppermute | solution.py:870
  237.7 28.6 %collective-permute-start.12 = (bf16[2,2,2,2,384,192]{4,5,3,2,1,0:T(8,128)(2,1)}, bf16[2,2,2,2,384,192]{4,5,3,2,1,0:T(8,128)(2,1)}, u32[]{:S(2)}, u32[]{:S(2)}) collective-permute-start(bf16[2,2,2,2,384,192]{4,5,3,2,1,0:T(8,128)(2,1)} %copy.60), channel_id=1, source_target_pairs={{0,1},{1,0},{2,3},{3,2},{4,5},{5,4},{6,7},{7,6},{8,9},{9,8},{10,11... | collective-permute-start | bytes 7077896 | tf_op jit(solution)/shard_map/ppermute | solution.py:870
  240.5 25.8 %collective-permute-start.10 = (bf16[2,2,2,2,96,192]{5,4,3,2,1,0:T(8,128)(2,1)}, bf16[2,2,2,2,96,192]{5,4,3,2,1,0:T(8,128)(2,1)}, u32[]{:S(2)}, u32[]{:S(2)}) collective-permute-start(bf16[2,2,2,2,96,192]{5,4,3,2,1,0:T(8,128)(2,1)} %get-tuple-element.266), channel_id=1, source_target_pairs={{0,1},{1,0},{2,3},{3,2},{4,5},{5,4},{6,7},{7,6},{8,9},{9,8},{10,11... | collective-permute-start | bytes 1769480 | tf_op jit(solution)/shard_map/ppermute | solution.py:870
  270.9 46.5 %collective-permute-start.14 = (bf16[2,2,2,96,768]{4,3,2,1,0:T(8,128)(2,1)}, bf16[2,2,2,96,768]{4,3,2,1,0:T(8,128)(2,1)}, u32[]{:S(2)}, u32[]{:S(2)}) collective-permute-start(bf16[2,2,2,96,768]{4,3,2,1,0:T(8,128)(2,1)} %get-tuple-element.262), channel_id=1, source_target_pairs={{0,4},{4,0},{8,12},{12,8},{16,20},{20,16},{24,28},{28,24},{1,5},{5... | collective-permute-start | bytes 3538952 | tf_op jit(solution)/shard_map/ppermute | solution.py:870
  280.1 37.4 %collective-permute-start.15 = (bf16[2,2,2,384,192]{3,4,2,1,0:T(8,128)(2,1)}, bf16[2,2,2,384,192]{3,4,2,1,0:T(8,128)(2,1)}, u32[]{:S(2)}, u32[]{:S(2)}) collective-permute-start(bf16[2,2,2,384,192]{3,4,2,1,0:T(8,128)(2,1)} %copy.62), channel_id=1, source_target_pairs={{0,2},{1,3},{2,0},{3,1},{4,6},{5,7},{6,4},{7,5},{8,10},{9,11},{10,... | collective-permute-start | bytes 3538952 | tf_op jit(solution)/shard_map/ppermute | solution.py:870
  284.4 33.1 %collective-permute-start.13 = (bf16[2,2,2,96,192]{4,3,2,1,0:T(8,128)(2,1)S(1)}, bf16[2,2,2,96,192]{4,3,2,1,0:T(8,128)(2,1)S(1)}, u32[]{:S(2)}, u32[]{:S(2)}) collective-permute-start(bf16[2,2,2,96,192]{4,3,2,1,0:T(8,128)(2,1)S(1)} %get-tuple-element.272), channel_id=1, source_target_pairs={{0,2},{1,3},{2,0},{3,1},{4,6},{5,7},{6,4},{7,5},{8,10},{9,11},{10,... | collective-permute-start | bytes 884744 | tf_op jit(solution)/shard_map/ppermute | solution.py:870
  320.3 24.7 %collective-permute-start.17 = (bf16[2,2,96,768]{3,2,1,0:T(8,128)(2,1)}, bf16[2,2,96,768]{3,2,1,0:T(8,128)(2,1)}, u32[]{:S(2)}, u32[]{:S(2)}) collective-permute-start(bf16[2,2,96,768]{3,2,1,0:T(8,128)(2,1)} %get-tuple-element.268), channel_id=1, source_target_pairs={{0,2},{1,3},{2,0},{3,1},{4,6},{5,7},{6,4},{7,5},{8,10},{9,11},{10,... | collective-permute-start | bytes 1769480 | tf_op jit(solution)/shard_map/ppermute | solution.py:870
  325.3 19.7 %collective-permute-start.18 = (bf16[2,2,384,192]{2,3,1,0:T(8,128)(2,1)}, bf16[2,2,384,192]{2,3,1,0:T(8,128)(2,1)S(1)}, u32[]{:S(2)}, u32[]{:S(2)}) collective-permute-start(bf16[2,2,384,192]{2,3,1,0:T(8,128)(2,1)} %copy.64), channel_id=1, source_target_pairs={{0,4},{4,0},{8,12},{12,8},{16,20},{20,16},{24,28},{28,24},{1,5},{5... | collective-permute-start | bytes 1769480 | tf_op jit(solution)/shard_map/ppermute | solution.py:870
  327.2 17.8 %collective-permute-start.16 = (bf16[2,2,96,192]{3,2,1,0:T(8,128)(2,1)S(1)}, bf16[2,2,96,192]{3,2,1,0:T(8,128)(2,1)S(1)}, u32[]{:S(2)}, u32[]{:S(2)}) collective-permute-start(bf16[2,2,96,192]{3,2,1,0:T(8,128)(2,1)S(1)} %get-tuple-element.282), channel_id=1, source_target_pairs={{0,4},{4,0},{8,12},{12,8},{16,20},{20,16},{24,28},{28,24},{1,5},{5... | collective-permute-start | bytes 442376 | tf_op jit(solution)/shard_map/ppermute | solution.py:870
  346.2 23.9 %collective-permute-start.20 = (bf16[2,96,768]{2,1,0:T(8,128)(2,1)S(1)}, bf16[2,96,768]{2,1,0:T(8,128)(2,1)S(1)}, u32[]{:S(2)}, u32[]{:S(2)}) collective-permute-start(bf16[2,96,768]{2,1,0:T(8,128)(2,1)S(1)} %get-tuple-element.274), channel_id=1, source_target_pairs={{0,8},{4,12},{8,0},{12,4},{16,24},{20,28},{24,16},{28,20},{1,9},{5... | collective-permute-start | bytes 884744 | tf_op jit(solution)/shard_map/ppermute | solution.py:870
  348.9 21.2 %collective-permute-start.21 = (bf16[2,384,192]{2,1,0:T(8,128)(2,1)S(1)}, bf16[2,384,192]{2,1,0:T(8,128)(2,1)S(1)}, u32[]{:S(2)}, u32[]{:S(2)}) collective-permute-start(bf16[2,384,192]{2,1,0:T(8,128)(2,1)S(1)} %get-tuple-element.270), channel_id=1, source_target_pairs={{0,8},{4,12},{8,0},{12,4},{16,24},{20,28},{24,16},{28,20},{1,9},{5... | collective-permute-start | bytes 884744 | tf_op jit(solution)/shard_map/ppermute | solution.py:870
  349.1 21.0 %collective-permute-start.19 = (bf16[2,96,192]{2,1,0:T(8,128)(2,1)S(1)}, bf16[2,96,192]{2,1,0:T(8,128)(2,1)S(1)}, u32[]{:S(2)}, u32[]{:S(2)}) collective-permute-start(bf16[2,96,192]{2,1,0:T(8,128)(2,1)S(1)} %get-tuple-element.290), channel_id=1, source_target_pairs={{0,8},{4,12},{8,0},{12,4},{16,24},{20,28},{24,16},{28,20},{1,9},{5... | collective-permute-start | bytes 221192 | tf_op jit(solution)/shard_map/ppermute | solution.py:870
  370.9 26.4 %collective-permute-start.23 = (bf16[96,768]{1,0:T(8,128)(2,1)S(1)}, bf16[96,768]{1,0:T(8,128)(2,1)S(1)}, u32[]{:S(2)}, u32[]{:S(2)}) collective-permute-start(bf16[96,768]{1,0:T(8,128)(2,1)S(1)} %get-tuple-element.284), channel_id=1, source_target_pairs={{0,16},{4,20},{8,24},{12,28},{16,0},{20,4},{24,8},{28,12},{1,17},{... | collective-permute-start | bytes 442376 | tf_op jit(solution)/shard_map/ppermute | solution.py:870
  371.0 26.3 %collective-permute-start.24 = (bf16[384,192]{1,0:T(8,128)(2,1)S(1)}, bf16[384,192]{1,0:T(8,128)(2,1)S(1)}, u32[]{:S(2)}, u32[]{:S(2)}) collective-permute-start(bf16[384,192]{1,0:T(8,128)(2,1)S(1)} %get-tuple-element.280), channel_id=1, source_target_pairs={{0,16},{4,20},{8,24},{12,28},{16,0},{20,4},{24,8},{28,12},{1,17},{... | collective-permute-start | bytes 442376 | tf_op jit(solution)/shard_map/ppermute | solution.py:870
  423.7 23.7 %collective-permute-start.35 = (bf16[2,2,2,2,48,576]{5,4,3,2,1,0:T(8,128)(2,1)}, bf16[2,2,2,2,48,576]{5,4,3,2,1,0:T(8,128)(2,1)}, u32[]{:S(2)}, u32[]{:S(2)}) collective-permute-start(bf16[2,2,2,2,48,576]{5,4,3,2,1,0:T(8,128)(2,1)} %slice_bitcast_fusion.8), channel_id=1, source_target_pairs={{0,1},{1,0},{2,3},{3,2},{4,5},{5,4},{6,7},{7,6},{8,9},{9,8},{10,11... | collective-permute-start | bytes 2654216 | tf_op jit(solution)/shard_map/ppermute | solution.py:870
  432.1 17.3 %collective-permute-start.30 = (bf16[2,2,2,2,48,576]{5,4,3,2,1,0:T(8,128)(2,1)S(1)}, bf16[2,2,2,2,48,576]{5,4,3,2,1,0:T(8,128)(2,1)}, u32[]{:S(2)}, u32[]{:S(2)}) collective-permute-start(bf16[2,2,2,2,48,576]{5,4,3,2,1,0:T(8,128)(2,1)S(1)} %slice_bitcast_fusion.9), channel_id=1, source_target_pairs={{0,1},{1,0},{2,3},{3,2},{4,5},{5,4},{6,7},{7,6},{8,9},{9,8},{10,11... | collective-permute-start | bytes 2654216 | tf_op jit(solution)/shard_map/ppermute | solution.py:870
  449.0 9.7 %collective-permute-start.36 = (bf16[2,2,2,48,576]{4,3,2,1,0:T(8,128)(2,1)S(1)}, bf16[2,2,2,48,576]{4,3,2,1,0:T(8,128)(2,1)S(1)}, u32[]{:S(2)}, u32[]{:S(2)}) collective-permute-start(bf16[2,2,2,48,576]{4,3,2,1,0:T(8,128)(2,1)S(1)} %slice_bitcast_fusion.16), channel_id=1, source_target_pairs={{0,2},{1,3},{2,0},{3,1},{4,6},{5,7},{6,4},{7,5},{8,10},{9,11},{10,... | collective-permute-start | bytes 1327112 | tf_op jit(solution)/shard_map/ppermute | solution.py:870
  450.8 11.5 %collective-permute-start.31 = (bf16[2,2,2,48,576]{4,3,2,1,0:T(8,128)(2,1)S(1)}, bf16[2,2,2,48,576]{4,3,2,1,0:T(8,128)(2,1)S(1)}, u32[]{:S(2)}, u32[]{:S(2)}) collective-permute-start(bf16[2,2,2,48,576]{4,3,2,1,0:T(8,128)(2,1)S(1)} %slice_bitcast_fusion.18), channel_id=1, source_target_pairs={{0,4},{4,0},{8,12},{12,8},{16,20},{20,16},{24,28},{28,24},{1,5},{5... | collective-permute-start | bytes 1327112 | tf_op jit(solution)/shard_map/ppermute | solution.py:870
  (59 other events, 699.6 us)
Sparse Core Ops, SparseCore 0:
  42.8 90.9 all-gather.2

commit v3 on v2

--- a/solution.py
+++ b/solution.py
@@ -92,8 +92,15 @@
     return [values[:, at : at + LANES] for at in range(0, values.shape[1], LANES)]
 
 
-def read_place(wide_ref, place):
-    parts = [wide_ref[tile, pl.ds(place, FRAMES, stride=PLACES), :] for tile in range(wide_ref.shape[0])]
+def flat_pieces(one, two, proj):
+    at = 0
+    for part in tiles_of(one) + tiles_of(two.T) + tiles_of(proj):
+        yield at, part
+        at += part.shape[0]
+
+
+def read_place(wide_ref, place, tiles=D // LANES):
+    parts = [wide_ref[tile, pl.ds(place, FRAMES, stride=PLACES), :] for tile in range(tiles)]
     return jnp.concatenate(parts, axis=1)
 
 
@@ -106,10 +113,109 @@
     return pltpu.VMEM((columns // LANES, ROWS, LANES), F32)
 
 
+PARTS = 3
+MESH = pl.DeviceIdType.MESH
+
+
+class Gather:
+    def __init__(self, shard_ref, all_ref, own_sem, send_sem, recv_sem):
+        dp, fsdp = lax.axis_index("dp"), lax.axis_index("fsdp")
+        self.z, self.x = dp // 2, dp % 2
+        self.y, self.c = fsdp // 2, fsdp % 2
+        self.shard_ref, self.all_ref = shard_ref, all_ref
+        self.own_sem, self.send_sem, self.recv_sem = own_sem, send_sem, recv_sem
+        self.rows = shard_ref.shape[0] // (2 * PARTS)
+        self.copies = {}
+
+    def device(self, z, x, y, c):
+        return (2 * z + x, 2 * y + c)
+
+    def partners(self):
+        z, x, y, c = self.z, self.x, self.y, self.c
+        along = [self.device((z + k) % 4, x, y, c) for k in (1, 2, 3)]
+        return along + [self.device(z, 1 - x, y, c), self.device(z, x, 1 - y, c), self.device(z, x, y, 1 - c)]
+
+    def begin(self):
+        barrier = pltpu.get_barrier_semaphore()
+        for partner in self.partners():
+            pl.semaphore_signal(barrier, inc=1, device_id=partner, device_id_type=MESH)
+        self.own = pltpu.make_async_copy(self.shard_ref, self.all_ref.at[self.z, self.x, self.y, self.c], self.own_sem)
+        self.own.start()
+        pl.semaphore_wait(barrier, 6)
+        for part in range(PARTS):
+            for route in range(2):
+                for k in (1, 2, 3):
+                    self.send(part, route, k - 1)
+
+    def send(self, part, route, stage):
+        z, x, y, c = self.z, self.x, self.y, self.c
+        rows = pl.ds((2 * part + route) * self.rows, self.rows)
+        partner = self.partners()[stage if stage < 3 or stage == 5 else 3 + (stage - 3 + route) % 2]
+        every = slice(None)
+        if stage < 3:
+            place = (z, x, y, c)
+        elif stage == 3:
+            place = (every, x, y, c)
+        elif stage == 4:
+            place = (every, every, y, c) if route == 0 else (every, x, every, c)
+        else:
+            place = (every, every, every, c)
+        target = self.all_ref.at[(*place, rows)]
+        source = self.shard_ref.at[rows] if stage < 3 else target
+        at = (2 * part + route) * 6 + stage
+        copy = pltpu.make_async_remote_copy(
+            src_ref=source,
+            dst_ref=target,
+            send_sem=self.send_sem.at[at],
+            recv_sem=self.recv_sem.at[at],
+            device_id=partner,
+            device_id_type=MESH,
+        )
+        copy.start()
+        self.copies[part, route, stage] = copy
+
+    def advance(self, part, level):
+        if level == 0 and part == 0:
+            self.own.wait()
+        for route in range(2):
+            for stage in ((0, 1, 2), (3,), (4,), (5,))[level]:
+                self.copies[part, route, stage].wait_recv()
+        if level < 3:
+            for route in range(2):
+                self.send(part, route, 3 + level)
+
+    def steps(self):
+        order = []
+        for turn in range(PARTS + 3):
+            for level in reversed(range(4)):
+                if 0 <= turn - level < PARTS:
+                    order.append((turn - level, level))
+        return [functools.partial(self.advance, *step) for step in order]
+
+    def end(self):
+        for copy in self.copies.values():
+            copy.wait_send()
+
+
 def prepare_kernel(
-    frames_ref, length_ref, tokens_ref, cot_ref, gain_ref, bias_ref, one_hot_ref, tables_ref, pick_ref,
-    x_ref, normed_ref, upstream_ref, aug_ref, table_ref, wide_ref,
+    communicate, frames_ref, length_ref, tokens_ref, cot_ref, gain_ref, bias_ref, one_hot_ref, time_ref, space_ref,
+    pick_ref, prev_ref, mem_ref, taps_ref, *refs,
 ):
+    if communicate:
+        shard_ref, one_ref, two_ref, proj_ref, all_ref, flat_ref = refs[:6]
+        refs = refs[6:]
+    x_ref, normed_ref, upstream_ref, aug_ref, table_ref, rest_ref, tap_ref, wide_ref, sums_ref, parts_ref = refs[:10]
+    tables_ref = refs[10]
+    steps = []
+    if communicate:
+        gather = Gather(shard_ref, all_ref, *refs[11:])
+        gather.begin()
+        steps = gather.steps()
+
+    def advance(count=1):
+        for _ in range(min(count, len(steps))):
+            steps.pop(0)()
+
     def permute(source_ref, target_ref):
         for tile, part in enumerate(tiles_of(source_ref[...])):
             wide_ref[tile] = part.astype(F32)
@@ -121,103 +227,120 @@
             at = pl.multiple_of(pair * 16, 16)
             target_ref[pl.ds(at, 16), :] = jnp.concatenate([first, second], axis=0).astype(BF16)
 
+    if communicate:
+        for at, part in flat_pieces(one_ref[...], two_ref[...], proj_ref[...]):
+            flat_ref[at : at + part.shape[0], : part.shape[1]] = part
     permute(cot_ref, upstream_ref)
     permute(tokens_ref, x_ref)
+    advance()
     centred, rs = layer_stats(x_ref[...].astype(F32), D)
-    normed_ref[...] = (centred * rs * gain_ref[...] + bias_ref[...]).astype(BF16)
+    normed_ref[...] = (centred * rs * gain_ref[...].reshape(1, D) + bias_ref[...].reshape(1, D)).astype(BF16)
     row = lax.broadcasted_iota(jnp.int32, (KEY_ROWS, LANES), 0)
     frames, length = frames_ref[0], length_ref[0]
     place = jnp.where(row < MEM_AT, row & 7, jnp.where(row < SQUEEZE_AT, row - MEM_AT, row - SQUEEZE_AT))
     limit = jnp.where(row < MEM_AT, frames, jnp.where(row < SQUEEZE_AT, length, MEM))
     off = jnp.where(place >= limit, jnp.where(lane_index((KEY_ROWS, LANES)) == MASK_LANE, MASKED, 0.0), 0.0)
     aug_ref[...] = (one_hot_ref[...].astype(F32) + off).astype(BF16)
+    tables_ref[...] = jnp.zeros((LANES, LANES), F32)
+    spans = 2 * HEIGHT - 1
+    tables_ref[0 : 2 * FRAMES - 1, :HEAD_DIM] = time_ref[...]
+    tables_ref[15 : 15 + spans, :HEAD_DIM] = space_ref[0]
+    tables_ref[15 + spans : 15 + 2 * spans, :HEAD_DIM] = space_ref[1]
     table_ref[...] = dot(pick_ref[...], tables_ref[...].astype(BF16)).astype(BF16)
-
-
-def prepare(frames, length, tokens, cot, gain, bias, one_hot, tables, pick):
+    advance()
+
+    def head_of(values, head):
+        return values[:, HEAD_DIM * head : HEAD_DIM * head + HEAD_DIM]
+
+    for s in range(2):
+        for group in range(2):
+            columns = slice(group * GROUP, (group + 1) * GROUP)
+            for tile, part in enumerate(tiles_of(prev_ref[s, :, columns])):
+                wide_ref[tile] = part.astype(F32)
+
+            taps = [tiled_lanes(taps_ref[s, tap : tap + 1, :]) for tap in range(4)]
+
+            @pl.loop(0, HEIGHT // 2)
+            def _(i):
+                for j in range(WIDTH // 2):
+                    total = None
+                    at = pl.multiple_of((i * (WIDTH // 2) + j) * FRAMES, FRAMES)
+                    for tap in range(4):
+                        place = (2 * i + tap // 2) * WIDTH + 2 * j + tap % 2
+                        part = read_place(wide_ref, place, GROUP // LANES)
+                        parts_ref[tap, pl.ds(at, FRAMES), :] = part
+                        term = part * taps[tap]
+                        total = term if total is None else total + term
+                    sums_ref[pl.ds(at, FRAMES), :] = total
+
+            old = mem_ref[s, :, columns].astype(F32)
+            for head in range(GROUP_HEADS):
+                rest = jnp.concatenate(
+                    [
+                        head_of(old, head),
+                        jnp.zeros((SQUEEZE_AT - MEM_AT - MEM, HEAD_DIM), F32),
+                        head_of(sums_ref[...], head),
+                        jnp.zeros((KEY_ROWS - SQUEEZE_AT - MEM, HEAD_DIM), F32),
+                    ],
+                    axis=0,
+                )
+                rest = jnp.concatenate([rest, jnp.zeros((REST, LANES - HEAD_DIM), F32)], axis=1)
+                rest_ref[s, group * GROUP_HEADS + head] = rest.astype(BF16)
+                for tap in range(4):
+                    part = jnp.concatenate([head_of(parts_ref[tap], head), jnp.zeros((8, HEAD_DIM), F32)], axis=0)
+                    part = jnp.concatenate([part, jnp.zeros((208, LANES - HEAD_DIM), F32)], axis=1)
+                    tap_ref[s, group * GROUP_HEADS + head, tap] = part.astype(BF16)
+            advance(3 if group + s else 2)
+    advance(len(steps))
+    if communicate:
+        gather.end()
+
+
+def prepare(frames, length, tokens, cot, gain, bias, one_hot, rel_time, rel_space, pick, prev, memory, taps, shards=None):
     smem = pl.BlockSpec(memory_space=pltpu.SMEM)
     vmem = pl.BlockSpec(memory_space=pltpu.VMEM)
+    communicate = shards is not None
+    out_shape = [
+        jax.ShapeDtypeStruct((ROWS, D), BF16),
+        jax.ShapeDtypeStruct((ROWS, D), BF16),
+        jax.ShapeDtypeStruct((ROWS, D), BF16),
+        jax.ShapeDtypeStruct((KEY_ROWS, LANES), BF16),
+        jax.ShapeDtypeStruct((TABLE, LANES), BF16),
+        jax.ShapeDtypeStruct((2, HEADS, REST, LANES), BF16),
+        jax.ShapeDtypeStruct((2, HEADS, 4, 208, LANES), BF16),
+    ]
+    in_specs, out_specs = [smem, smem] + [vmem] * 11, [vmem] * 7
+    operands = [frames, length, tokens, cot, gain, bias, one_hot, rel_time, rel_space, pick, prev, memory, taps]
+    scratch = [
+        wide_scratch(D),
+        pltpu.VMEM((MEM, GROUP), F32),
+        pltpu.VMEM((4, MEM, GROUP), F32),
+        pltpu.VMEM((LANES, LANES), F32),
+    ]
+    more = {}
+    if communicate:
+        anywhere = pl.BlockSpec(memory_space=pl.ANY)
+        shard, one, two, proj = shards
+        rows = (one.size + two.size) // LANES + 2 * proj.shape[0]
+        out_shape = [
+            jax.ShapeDtypeStruct((4, 2, 2, 2) + shard.shape, BF16),
+            jax.ShapeDtypeStruct((rows, LANES), BF16),
+        ] + out_shape
+        in_specs += [anywhere, vmem, vmem, vmem]
+        out_specs = [anywhere, vmem] + out_specs
+        operands += shards
+        count = 2 * PARTS * 6
+        scratch += [pltpu.SemaphoreType.DMA, pltpu.SemaphoreType.DMA((count,)), pltpu.SemaphoreType.DMA((count,))]
+        more = {"collective_id": 0, "has_side_effects": True}
     return pl.pallas_call(
-        prepare_kernel,
-        out_shape=(
-            jax.ShapeDtypeStruct((ROWS, D), BF16),
-            jax.ShapeDtypeStruct((ROWS, D), BF16),
-            jax.ShapeDtypeStruct((ROWS, D), BF16),
-            jax.ShapeDtypeStruct((KEY_ROWS, LANES), BF16),
-            jax.ShapeDtypeStruct((TABLE, LANES), BF16),
-        ),
-        in_specs=[smem, smem] + [vmem] * 7,
-        out_specs=(vmem,) * 5,
-        scratch_shapes=[wide_scratch(D)],
-        compiler_params=params(),
+        functools.partial(prepare_kernel, communicate),
+        out_shape=tuple(out_shape),
+        in_specs=in_specs,
+        out_specs=tuple(out_specs),
+        scratch_shapes=scratch,
+        compiler_params=params(**more),
         name="prepare",
-    )(frames, length, tokens, cot, gain, bias, one_hot, tables, pick)
-
-
-def squeeze_kernel(prev_ref, mem_ref, taps_ref, rest_ref, tap_ref, wide_ref, sums_ref, parts_ref):
-    for tile, part in enumerate(tiles_of(prev_ref[0])):
-        wide_ref[tile] = part.astype(F32)
-
-    @pl.loop(0, HEIGHT // 2)
-    def _(i):
-        for j in range(WIDTH // 2):
-            total = None
-            at = pl.multiple_of((i * (WIDTH // 2) + j) * FRAMES, FRAMES)
-            for tap in range(4):
-                place = (2 * i + tap // 2) * WIDTH + 2 * j + tap % 2
-                part = read_place(wide_ref, place)
-                parts_ref[tap, pl.ds(at, FRAMES), :] = part
-                term = part * taps_ref[0, tap : tap + 1, :]
-                total = term if total is None else total + term
-            sums_ref[pl.ds(at, FRAMES), :] = total
-
-    def head_of(values, head):
-        return values[:, HEAD_DIM * head : HEAD_DIM * head + HEAD_DIM]
-
-    old = mem_ref[0].astype(F32)
-    for head in range(GROUP_HEADS):
-        rest = jnp.concatenate(
-            [
-                head_of(old, head),
-                jnp.zeros((SQUEEZE_AT - MEM_AT - MEM, HEAD_DIM), F32),
-                head_of(sums_ref[...], head),
-                jnp.zeros((KEY_ROWS - SQUEEZE_AT - MEM, HEAD_DIM), F32),
-            ],
-            axis=0,
-        )
-        rest = jnp.concatenate([rest, jnp.zeros((REST, LANES - HEAD_DIM), F32)], axis=1)
-        rest_ref[0, head] = rest.astype(BF16)
-        for tap in range(4):
-            part = jnp.concatenate([head_of(parts_ref[tap], head), jnp.zeros((8, HEAD_DIM), F32)], axis=0)
-            part = jnp.concatenate([part, jnp.zeros((208, LANES - HEAD_DIM), F32)], axis=1)
-            tap_ref[0, head, tap] = part.astype(BF16)
-
-
-def squeeze(prev, memory, taps):
-    return pl.pallas_call(
-        squeeze_kernel,
-        grid=(2, 2),
-        out_shape=(
-            jax.ShapeDtypeStruct((2, HEADS, REST, LANES), BF16),
-            jax.ShapeDtypeStruct((2, HEADS, 4, 208, LANES), BF16),
-        ),
-        in_specs=[
-            pl.BlockSpec((1, ROWS, GROUP), lambda s, g: (s, 0, g)),
-            pl.BlockSpec((1, MEM, GROUP), lambda s, g: (s, 0, g)),
-            pl.BlockSpec((1, 4, GROUP), lambda s, g: (s, 0, 0)),
-        ],
-        out_specs=(
-            pl.BlockSpec((1, GROUP_HEADS, REST, LANES), lambda s, g: (s, g, 0, 0)),
-            pl.BlockSpec((1, GROUP_HEADS, 4, 208, LANES), lambda s, g: (s, g, 0, 0, 0)),
-        ),
-        scratch_shapes=[
-            wide_scratch(GROUP),
-            pltpu.VMEM((MEM, GROUP), F32),
-            pltpu.VMEM((4, MEM, GROUP), F32),
-        ],
-        compiler_params=params(),
-        name="squeeze",
-    )(prev, memory, taps)
+    )(*operands)
 
 
 def shift_frames(values, step):
@@ -234,9 +357,15 @@
             window = grid_ref[i + b, e : e + WIDTH, :, lanes]
             for a in range(3):
                 tap = 9 * a + 3 * b + e
-                term = window * taps_ref[0, 26 - tap if flip else tap, :, lanes][None]
+                term = window * taps_ref[26 - tap if flip else tap, :, lanes][None]
                 sums[a] = term if sums[a] is None else sums[a] + term
     return sums[1] + shift_frames(sums[0], 1) + shift_frames(sums[2], -1)
+
+
+def spread_taps(raw_ref, taps_ref):
+    for tap in range(27):
+        line = tiled_lanes(raw_ref[0, tap : tap + 1, :])
+        taps_ref[tap] = jnp.broadcast_to(line, (FRAMES, GROUP))
 
 
 def clear_border(grid_ref):
@@ -258,23 +387,22 @@
 
 
 def qkv_kernel(
-    frames_ref, place_ref, normed_ref, first_ref, second_ref, qkv_bias_ref, taps_ref, gain_ref, bias_ref,
-    heads_ref, vhat_ref, mixed_ref, weight_ref, grid_ref, pooled_ref,
+    frames_ref, normed_ref, shards_ref, qkv_bias_ref, taps_raw_ref, gain_ref, bias_ref,
+    heads_ref, vhat_ref, mixed_ref, weight_ref, grid_ref, pooled_ref, taps_ref,
 ):
     step = pl.program_id(0)
 
     @pl.when(step == 0)
     def _():
         clear_border(grid_ref)
-        half, columns = first_ref.shape[1:]
+        depth, columns = shards_ref.shape[2:]
         for f in range(QKV // columns):
-
-            @pl.loop(0, DP_BLOCKS)
-            def _(d):
-                bits = relative_bits(place_ref, d, f)
-                for part, (source_ref, order) in enumerate(((first_ref, ROUTE_ONE), (second_ref, ROUTE_TWO))):
-                    at = pl.multiple_of((2 * d + part) * half, half)
-                    weight_ref[pl.ds(at, half), f * columns : (f + 1) * columns] = source_ref[slot(bits, order)]
+            for d in range(DP_BLOCKS):
+                weight_ref[d * depth : (d + 1) * depth, f * columns : (f + 1) * columns] = shards_ref[d, f]
+
+    @pl.when(step % 2 == 0)
+    def _():
+        spread_taps(taps_raw_ref, taps_ref)
 
     at = pl.multiple_of(step * GROUP, LANES)
     mixed = dot(normed_ref[...], weight_ref[:, pl.ds(at, GROUP)]) + qkv_bias_ref[...]
@@ -306,7 +434,7 @@
         vhat_ref[head] = (vhat + extra).astype(BF16)
 
 
-def query_key_value(frames, place, normed, first, second, qkv_bias, taps, gain, bias):
+def query_key_value(frames, normed, shards, qkv_bias, taps, gain, bias):
     smem = pl.BlockSpec(memory_space=pltpu.SMEM)
     return pl.pallas_call(
         qkv_kernel,
@@ -319,12 +447,10 @@
         ),
         in_specs=[
             smem,
-            smem,
             whole((ROWS, D)),
-            whole(first.shape),
-            whole(second.shape),
+            whole(shards.shape),
             pl.BlockSpec((1, GROUP), lambda g: (0, g)),
-            pl.BlockSpec((1, 27, 8, GROUP), lambda g: (g // 2, 0, 0, 0)),
+            pl.BlockSpec((1, 27, HEAD_DIM), lambda g: (g // 2, 0, 0)),
             pl.BlockSpec((1, 1, LANES), lambda g: (g // 2, 0, 0)),
             pl.BlockSpec((1, 1, LANES), lambda g: (g // 2, 0, 0)),
         ],
@@ -337,10 +463,11 @@
         scratch_shapes=[
             pltpu.VMEM((HEIGHT + 2, WIDTH + 2, FRAMES, GROUP), F32),
             pltpu.VMEM((ROWS, GROUP + LANES), F32),
+            pltpu.VMEM((27, FRAMES, GROUP), F32),
         ],
         compiler_params=params(),
         name="query_key_value",
-    )(frames, place, normed, first, second, qkv_bias, taps, gain, bias)
+    )(frames, normed, shards, qkv_bias, taps, gain, bias)
 
 
 def attend_kernel(
@@ -688,14 +815,15 @@
 
 
 def pool_back_kernel(
-    frames_ref, first_ref, second_ref, vhat_ref, mixed_ref, taps_ref, gain_ref,
+    frames_ref, first_ref, second_ref, vhat_ref, mixed_ref, taps_raw_ref, gain_ref,
     dmix_ref, gbias_ref, gtaps_ref, gpool_ref,
-    grid_ref, dgrid_ref, dpool_ref, sums_ref,
+    grid_ref, dgrid_ref, dpool_ref, sums_ref, taps_ref,
 ):
     step = pl.program_id(0)
 
     @pl.when(step == 0)
     def _():
+        spread_taps(taps_raw_ref, taps_ref)
         clear_border(grid_ref)
         clear_border(dgrid_ref)
 
@@ -757,7 +885,7 @@
             pl.BlockSpec((1, GROUP_HEADS, ROWS, LANES), lambda g: (kind, 0, 0, 0)),
             pl.BlockSpec((GROUP_HEADS, ROWS, LANES), lambda g: (2 * kind + g, 0, 0)),
             pl.BlockSpec((ROWS, GROUP), lambda g: (0, 2 * kind + g)),
-            pl.BlockSpec((1, 27, 8, GROUP), lambda g: (kind, 0, 0, 0)),
+            pl.BlockSpec((1, 27, HEAD_DIM), lambda g: (kind, 0, 0)),
             pl.BlockSpec((1, 1, LANES), lambda g: (kind, 0, 0)),
         ],
         out_specs=(
@@ -770,6 +898,7 @@
             pltpu.VMEM((HEIGHT + 2, WIDTH + 2, FRAMES, GROUP), F32),
             pltpu.VMEM((HEIGHT + 2, WIDTH + 2, FRAMES, GROUP), F32),
             pltpu.VMEM((ROWS, GROUP), F32),
+            pltpu.VMEM((27, FRAMES, GROUP), F32),
             pltpu.VMEM((27, FRAMES, GROUP), F32),
         ],
         compiler_params=params(),
@@ -875,10 +1004,9 @@
 
 
 def flat_shard(one, two, proj):
-    parts = tiles_of(one) + tiles_of(two.T)
-    part = proj.shape[1]
-    parts += [proj[:, :LANES], jnp.pad(proj[:, LANES:], ((0, 0), (0, 2 * LANES - part)))]
-    return jnp.concatenate(parts, axis=0)
+    pieces = [part for _, part in flat_pieces(one, two, proj)]
+    pieces[-1] = jnp.pad(pieces[-1], ((0, 0), (0, LANES - pieces[-1].shape[1])))
+    return jnp.concatenate(pieces, axis=0)
 
 
 class Staged:
@@ -889,16 +1017,7 @@
         dp, fsdp = lax.axis_index("dp"), lax.axis_index("fsdp")
         return jnp.stack([dp & 1, (dp >> 1) & 1, (dp >> 2) & 1, (fsdp >> 1) & 1, fsdp & 1]).astype(jnp.int32)
 
-    def first_weights(self, shard):
-        half = shard.shape[0] // 2
-        one, two = shard[None, :half], shard[None, half:]
-        for a, b in zip(ROUTE_ONE, ROUTE_TWO):
-            more_one, more_two = swap(one, a, self.sizes), swap(two, b, self.sizes)
-            one, two = jnp.concatenate([one, more_one]), jnp.concatenate([two, more_two])
-        return one, two
-
-    def other_weights(self, one, two, proj, after):
-        flat, _ = together(flat_shard(one, two, proj), after)
+    def other_weights(self, flat):
         return lax.all_gather(flat, ("dp", "fsdp"), axis=0, tiled=False).reshape((8, 4) + flat.shape)
 
     def halve(self, blocks, name):
@@ -923,19 +1042,7 @@
         joined = blocks.reshape(DP_BLOCKS, self.dp // DP_BLOCKS, self.fsdp, rows, columns).transpose(0, 2, 1, 3, 4)
         return joined.reshape(DP_BLOCKS, self.fsdp, self.dp // DP_BLOCKS * rows, columns)
 
-    def first_weights(self, shard):
-        blocks = self.gather(shard)
-        half, columns = blocks.shape[2] // 2, blocks.shape[3]
-        bits = blocks.reshape(2, 2, 2, 2, 2, 2, half, columns)
-        at = {"z2": 0, "z1": 1, "x": 2, "y": 3, "c": 4}
-        return tuple(
-            bits.transpose([at[name] for name in reversed(route)] + [5, 6, 7])[:, :, :, :, :, side].reshape(
-                32, half, columns
-            )
-            for side, route in enumerate((ROUTE_ONE, ROUTE_TWO))
-        )
-
-    def other_weights(self, one, two, proj, after):
+    def other_weights(self, one, two, proj):
         return jax.vmap(jax.vmap(flat_shard))(self.gather(one), self.gather(two), self.gather(proj))
 
     def scatter(self, blocks, route):
@@ -956,20 +1063,18 @@
     fc2_bias, cotangent,
 ):
     place = comm.place()
-    first, second = comm.first_weights(w_qkv)
     one_hot, own, fold, pick = (jnp.asarray(c, BF16) for c in constants())
-    tables = jnp.concatenate([rel_time, rel_space[0], rel_space[1]], axis=0)
-    tables = jnp.pad(tables, ((0, LANES - tables.shape[0]), (0, LANES - HEAD_DIM)))
-    taps = jnp.broadcast_to(tiled_lanes(pool_conv)[:, :, None, :], (3, 27, 8, GROUP))
-    gains, biases = head_lanes(pool_gain)[:, None], head_lanes(pool_bias)[:, None]
-    x, normed, upstream, aug, table = prepare(
-        valid_frames, mem_len, tokens, cotangent, row(ln1_gain), row(ln1_bias), one_hot, tables, pick
+    taps, gains, biases = pool_conv, head_lanes(pool_gain)[:, None], head_lanes(pool_bias)[:, None]
+    prepared = prepare(
+        valid_frames, mem_len, tokens, cotangent, ln1_gain, ln1_bias, one_hot, rel_time, rel_space, pick,
+        prev_kv, memory, compress, [w_qkv, w_fc1, w_fc2, w_proj] if staged else None,
     )
-    rest, parts = squeeze(prev_kv, memory, tiled_lanes(compress))
-    flat = comm.other_weights(w_fc1, w_fc2, w_proj, first)
-    heads, vhat, mixed, weight = query_key_value(
-        valid_frames, place, normed, first, second, row(qkv_bias), taps, gains, biases
-    )
+    x, normed, upstream, aug, table, rest, parts = prepared[-7:]
+    if staged:
+        first, flat = prepared[0].reshape(8, 4, *w_qkv.shape), comm.other_weights(prepared[1])
+    else:
+        first, flat = comm.gather(w_qkv), comm.other_weights(w_fc1, w_fc2, w_proj)
+    heads, vhat, mixed, weight = query_key_value(valid_frames, normed, first, row(qkv_bias), taps, gains, biases)
     weights, pv, attended = attend(heads, rest, aug, table, own, fold)
     out, dmid, datt, gp, gw1, gw2, small_two, gb1 = feed_forward(
         place, attended, x, upstream, flat, row(proj_bias), row(ln2_gain), row(ln2_bias), row(fc1_bias), row(fc2_bias)

time: 496 us -> 469 us (0.946)
  Pallas kernels: 260 us -> 293 us
  waiting for transfers between devices: 81.7 us -> 51 us
  starting transfers between devices: 46.7 us -> 27.3 us
  local copies, waits for them, and re-layouts: 62.3 us -> 57 us
  other arithmetic: 21.1 us -> 15.9 us
    ppermute x40 -> x30, waiting for transfers between devices: 81.7 us -> 39.3 us  [swap(): lax.ppermute(values, axis, [(at, at ^ bit) for at in range(sizes[axis])])]
    pallas_call x2 -> x1, Pallas kernels: 11.4 us -> 46.2 us  [prepare(): pl.pallas_call(functools.partial(prepare_kernel, communicate), out_shape=...]
    ppermute x40 -> x30, starting transfers between devices: 46.7 us -> 27.2 us  [swap(): lax.ppermute(values, axis, [(at, at ^ bit) for at in range(sizes[axis])])]
    all_gather x1, waiting for transfers between devices: 0.01 us -> 11.7 us  [other_weights(): lax.all_gather(flat, ('dp', 'fsdp'), axis=0, tiled=False)]
    unnamed x101 -> x76, local copies, waits for them, and re-layouts: 12.4 us -> 5.85 us
    squeeze x28, local copies, waits for them, and re-layouts: 23.1 us -> 28.8 us  [halve(): return (blocks[0], swap(blocks[1], name, self.sizes))]
  transfers between devices with their start and end apart: 41 -> 31, of which waited for: 21 -> 14; matrix products, arithmetic and copies ran while one was open for 13% -> 9% of each run, Pallas kernels for 38% -> 38%
where the time goes in v3:
time: 469 us; the launch traced here: 461 us
  Pallas kernels  293 us (62%)
  local copies, waits for them, and re-layouts  57 us (12%)
  waiting for transfers between devices  51 us (11%)
  starting transfers between devices  27.3 us (6%)
  between operations  16.6 us (4%)
  other arithmetic  15.9 us (3%)
    pallas_call x3, Pallas kernels, pool_back(): pl.pallas_call(pool_back_kernel, grid=(2,), out_shape=(jax.ShapeDtypeStru...  52.4 us
    pallas_call x1, Pallas kernels, feed_forward(): pl.pallas_call(middle_kernel, out_shape=(jax.ShapeDtypeStruct((ROWS, D),...  51 us
    pallas_call x2, Pallas kernels, attend_back(): pl.pallas_call(attend_back_kernel, grid=(count,), out_shape=(jax.ShapeDty...  50.9 us
    pallas_call x1, Pallas kernels, prepare(): pl.pallas_call(functools.partial(prepare_kernel, communicate), out_shape=...  46.2 us
    ppermute x30, waiting for transfers between devices, swap(): lax.ppermute(values, axis, [(at, at ^ bit) for at in range(sizes[axis])])  39.3 us
    pallas_call x1, Pallas kernels, attend(): pl.pallas_call(attend_kernel, grid=(HEADS,), out_shape=(jax.ShapeDtypeStr...  36.4 us
    pallas_call x1, Pallas kernels, query_key_value(): pl.pallas_call(qkv_kernel, grid=(6,), out_shape=(jax.ShapeDtypeStruct((3...  35.8 us
    squeeze x28, local copies, waits for them, and re-layouts, halve(): return (blocks[0], swap(blocks[1], name, self.sizes))  28.8 us
  transfers between devices with their start and end apart: 31, of which 14 were waited for; matrix products, arithmetic and copies ran while one was open for 9% of the time, Pallas kernels for 38%

profile of v3, /device:TPU:0, one launch (start us, length us, event | category | flops | bytes accessed | tf_op | source)
XLA Modules:
  0.0 461.0 jit_solution(17189738554928579655)
XLA Ops:
  11.7 46.2 %prepare.1 = (bf16[4,2,2,2,96,576]{5,4,3,2,1,0:T(8,128)(2,1)}, bf16[1344,128]{1,0:T(8,128)(2,1)}, bf16[800,768]{1,0:T(8,128)(2,1)}, bf16[800,768]{1,0:T(8,128)(2...) custom-call(s32[1]{0:T(128)S(6)} %copy.71.frames_ref, ...), custom_call_target="tpu_custom_call" | custom-call | tf_op jit(solution)/shard_map/prepare/pallas_call | solution.py:335
  62.7 35.8 %query_key_value.1 = (bf16[24,800,128]{2,1,0:T(8,128)(2,1)}, bf16[24,800,128]{2,1,0:T(8,128)(2,1)}, bf16[800,2304]{1,0:T(8,128)(2,1)}, bf16[768,2304]{1,0:T(8,128)(2,1)}) custom-call(s32[1]{0:T(128)S(6)} %copy.71.frames_ref, bf16[800,768]{1,0:T(8,128)(2,1)} %get-tuple-element.105.normed_ref, bf16[8,4,96,576]{3,2,1,0:T(8,128)(2,1)} %bitcast.137, ...), custom_call_target="tpu_custom_call" | custom-call | tf_op jit(solution)/shard_map/query_key_value/pallas_call | solution.py:439
  98.5 36.4 %attend.1 = (bf16[8,800,1280]{2,1,0:T(8,128)(2,1)}, bf16[8,800,128]{2,1,0:T(8,128)(2,1)}, bf16[8,800,128]{2,1,0:T(8,128)(2,1)}) custom-call(bf16[24,800,128]{2,1,0:T(8,128)(2,1)} %get-tuple-element.107.q_ref.k_ref.v_ref, bf16[24,800,128]{2,1,0:T(8,128)(2,1)} %get-tuple-element.107.q_ref.k_ref.v_ref, ...), custom_call_target="tpu_custom_call" | custom-call | tf_op jit(solution)/shard_map/attend/pallas_call | solution.py:509
  134.9 11.7 %all-gather.3.cloned.1.call-done = bf16[43008,128]{1,0:T(8,128)(2,1)} async-done(((bf16[1344,128]{1,0:T(8,128)(2,1)}), bf16[43008,128]{1,0:T(8,128)(2,1)}) %all-gather.3.cloned.1.call-update) | async-done | bytes 11010064 | tf_op jit(solution)/shard_map/all_gather | solution.py:1021
  146.6 51.0 %feed_forward.1 = (bf16[800,768]{1,0:T(8,128)(2,1)}, f32[800,768]{1,0:T(8,128)}, bf16[8,800,128]{2,1,0:T(8,128)(2,1)}, bf16[2,2,2,2,2,96,192]{6,5,4,3,2,1,0:T(8,...) custom-call(s32[5]{0:T(128)} %stack.47.place_ref, ...), custom_call_target="tpu_custom_call" | custom-call | tf_op jit(solution)/shard_map/feed_forward/pallas_call | solution.py:656
  197.6 5.0 %slice_bitcast_fusion = (bf16[2,2,2,2,384,192]{5,4,3,2,1,0:T(8,128)(2,1)}, bf16[2,2,2,2,384,192]{5,4,3,2,1,0:T(8,128)(2,1)S(1)}) fusion(bf16[2,2,2,2,2,384,192]{6,5,4,3,2,1,0:T(8,128)(2,1)} %get-tuple-element.118), kind=kLoop, calls=%fused_computation | loop fusion | bytes 9437184 | tf_op jit(solution)/shard_map/squeeze | solution.py:1024
  202.6 4.9 %copy.60 = bf16[2,2,2,2,384,192]{4,5,3,2,1,0:T(8,128)(2,1)} copy(bf16[2,2,2,2,384,192]{5,4,3,2,1,0:T(8,128)(2,1)} %get-tuple-element.258) | data formatting | bytes 4718592 | tf_op jit(solution)/shard_map/squeeze | solution.py:1024
  207.8 5.1 %slice_bitcast_fusion.2 = (bf16[2,2,2,2,96,768]{5,4,3,2,1,0:T(8,128)(2,1)}, bf16[2,2,2,2,96,768]{5,4,3,2,1,0:T(8,128)(2,1)}) fusion(bf16[2,2,2,2,2,96,768]{6,5,4,3,2,1,0:T(8,128)(2,1)} %get-tuple-element.117), kind=kLoop, calls=%fused_computation.2 | loop fusion | bytes 9437184 | tf_op jit(solution)/shard_map/squeeze | solution.py:1024
  214.7 25.3 %attend_back.2 = (bf16[3,4,800,128]{3,2,1,0:T(8,128)(2,1)}, f32[128,128]{1,0:T(8,128)}, f32[2,4,128]{2,1,0:T(4,128)}) custom-call(bf16[24,800,128]{2,1,0:T(8,128)(2,1)} %get-tuple-element.107.q_ref.k_ref.v_ref, bf16[24,800,128]{2,1,0:T(8,128)(2,1)} %get-tuple-element.107.q_ref.k_ref.v_ref, bf16[24,800,128]{2,1,0:T(8,128)(2,1)} %get-tuple-element.107.q_ref.k_ref.v_ref, ...), custom_call_target="tpu_custom_call" | custom-call | tf_op jit(solution)/shard_map/attend_back/pallas_call | solution.py:776
  240.1 4.5 copy.61
  244.6 2.9 add.102
  260.5 25.5 %attend_back.3 = (bf16[3,4,800,128]{3,2,1,0:T(8,128)(2,1)}, f32[128,128]{1,0:T(8,128)}, f32[2,4,128]{2,1,0:T(4,128)}) custom-call(bf16[24,800,128]{2,1,0:T(8,128)(2,1)} %get-tuple-element.107.q_ref.k_ref.v_ref, bf16[24,800,128]{2,1,0:T(8,128)(2,1)} %get-tuple-element.107.q_ref.k_ref.v_ref, bf16[24,800,128]{2,1,0:T(8,128)(2,1)} %get-tuple-element.107.q_ref.k_ref.v_ref, ...), custom_call_target="tpu_custom_call" | custom-call | tf_op jit(solution)/shard_map/attend_back/pallas_call | solution.py:776
  298.8 17.4 %pool_back_0.1 = (bf16[800,768]{1,0:T(8,128)(2,1)}, f32[1,768]{1,0:T(1,128)}, f32[2,27,384]{2,1,0:T(8,128)}, f32[8,2,128]{2,1,0:T(2,128)}) custom-call(s32[1]{0:T(128)S(6)} %copy.71.frames_ref, bf16[3,4,800,128]{3,2,1,0:T(8,128)(2,1)} %get-tuple-element.160.first_ref, bf16[3,4,800,128]{3,2,1,0:T(8,128)(2,1)} %get-tuple-element.140.second_ref, ...), custom_call_target="tpu_custom_call" | custom-call | tf_op jit(solution)/shard_map/pool_back_0/pallas_call | solution.py:873
  322.0 17.6 %pool_back_1.1 = (bf16[800,768]{1,0:T(8,128)(2,1)}, f32[1,768]{1,0:T(1,128)}, f32[2,27,384]{2,1,0:T(8,128)}, f32[8,2,128]{2,1,0:T(2,128)}) custom-call(s32[1]{0:T(128)S(6)} %copy.71.frames_ref, bf16[3,4,800,128]{3,2,1,0:T(8,128)(2,1)} %get-tuple-element.160.first_ref, bf16[3,4,800,128]{3,2,1,0:T(8,128)(2,1)} %get-tuple-element.140.second_ref, ...), custom_call_target="tpu_custom_call" | custom-call | tf_op jit(solution)/shard_map/pool_back_1/pallas_call | solution.py:873
  345.3 17.4 %pool_back_2.1 = (bf16[800,768]{1,0:T(8,128)(2,1)}, f32[1,768]{1,0:T(1,128)}, f32[2,27,384]{2,1,0:T(8,128)}, f32[8,2,128]{2,1,0:T(2,128)}) custom-call(s32[1]{0:T(128)S(6)} %copy.71.frames_ref, bf16[3,4,800,128]{3,2,1,0:T(8,128)(2,1)} %get-tuple-element.160.first_ref, bf16[3,4,800,128]{3,2,1,0:T(8,128)(2,1)} %get-tuple-element.140.second_ref, ...), custom_call_target="tpu_custom_call" | custom-call | tf_op jit(solution)/shard_map/pool_back_2/pallas_call | solution.py:873
  368.3 10.3 %project_grad.1 = (bf16[2,2,2,2,2,48,576]{6,5,4,3,2,1,0:T(8,128)(2,1)}, bf16[2,2,2,2,2,48,576]{6,5,4,3,2,1,0:T(8,128)(2,1)}) custom-call(s32[5]{0:T(128)} %stack.47.place_ref, bf16[800,768]{1,0:T(8,128)(2,1)} %get-tuple-element.105.normed_ref, bf16[800,768]{1,0:T(8,128)(2,1)} %get-tuple-element.144.dq_ref, bf16[800,768]{1,0:T(8,128)(2,1)} %get-tuple-element.153.dk_ref, ...), custom_call_target="tpu_custom_call" | custom-call | tf_op jit(solution)/shard_map/project_grad/pallas_call | solution.py:929
  378.6 10.4 %project_back.1 = (f32[800,768]{1,0:T(8,128)}, f32[8,768]{1,0:T(8,128)}) custom-call(bf16[800,768]{1,0:T(8,128)(2,1)} %get-tuple-element.144.dq_ref, bf16[800,768]{1,0:T(8,128)(2,1)} %get-tuple-element.153.dk_ref, bf16[800,768]{1,0:T(8,128)(2,1)} %get-tuple-element.162.dv_ref, bf16[768,2304]{1,0:T(8,128)(2,1)} %get-tuple-element.163.weight_ref, ...), custom_call_target="tpu_custom_call" | custom-call | tf_op jit(solution)/shard_map/project_back/pallas_call | solution.py:968
  394.4 3.4 collective-permute-done.16
  398.1 4.3 collective-permute-done.17
  403.7 3.4 collective-permute-done.18
  409.3 4.5 collective-permute-done.19
  424.8 5.7 %collective-permute-done.21 = bf16[2,2,2,48,576]{4,3,2,1,0:T(8,128)(2,1)S(1)} collective-permute-done((bf16[2,2,2,48,576]{4,3,2,1,0:T(8,128)(2,1)S(1)}, bf16[2,2,2,48,576]{4,3,2,1,0:T(8,128)(2,1)S(1)}, u32[]{:S(2)}, u32[]{:S(2)}) %collective-permute-start.21) | collective-permute-done | bytes 442400 | tf_op jit(solution)/shard_map/ppermute | solution.py:999
  431.5 3.6 collective-permute-done.26
  448.5 4.5 collective-permute-done.29
  (235 shorter events, 87.6 us)
Async XLA Ops:
  7.2 139.4 %all-gather.3.cloned.1.call-start = ((), (), s32[]{:S(2)}) async-start(), calls=%async_computation | async-start | bytes 11354112 | tf_op jit(solution)/shard_map/all_gather | solution.py:1021
  207.5 32.6 %collective-permute-start.2 = (bf16[2,2,2,2,384,192]{4,5,3,2,1,0:T(8,128)(2,1)}, bf16[2,2,2,2,384,192]{4,5,3,2,1,0:T(8,128)(2,1)}, u32[]{:S(2)}, u32[]{:S(2)}) collective-permute-start(bf16[2,2,2,2,384,192]{4,5,3,2,1,0:T(8,128)(2,1)} %copy.60), channel_id=1, source_target_pairs={{0,1},{1,0},{2,3},{3,2},{4,5},{5,4},{6,7},{7,6},{8,9},{9,8},{10,11... | collective-permute-start | bytes 7077896 | tf_op jit(solution)/shard_map/ppermute | solution.py:999
  212.9 27.2 %collective-permute-start.1 = (bf16[2,2,2,2,96,768]{5,4,3,2,1,0:T(8,128)(2,1)}, bf16[2,2,2,2,96,768]{5,4,3,2,1,0:T(8,128)(2,1)}, u32[]{:S(2)}, u32[]{:S(2)}) collective-permute-start(bf16[2,2,2,2,96,768]{5,4,3,2,1,0:T(8,128)(2,1)} %get-tuple-element.260), channel_id=1, source_target_pairs={{0,1},{1,0},{2,3},{3,2},{4,5},{5,4},{6,7},{7,6},{8,9},{9,8},{10,11... | collective-permute-start | bytes 7077896 | tf_op jit(solution)/shard_map/ppermute | solution.py:999
  214.5 25.6 %collective-permute-start = (bf16[2,2,2,2,96,192]{5,4,3,2,1,0:T(8,128)(2,1)}, bf16[2,2,2,2,96,192]{5,4,3,2,1,0:T(8,128)(2,1)}, u32[]{:S(2)}, u32[]{:S(2)}) collective-permute-start(bf16[2,2,2,2,96,192]{5,4,3,2,1,0:T(8,128)(2,1)} %get-tuple-element.268), channel_id=1, source_target_pairs={{0,1},{1,0},{2,3},{3,2},{4,5},{5,4},{6,7},{7,6},{8,9},{9,8},{10,11... | collective-permute-start | bytes 1769480 | tf_op jit(solution)/shard_map/ppermute | solution.py:999
  252.0 36.8 %collective-permute-start.5 = (bf16[2,2,2,384,192]{3,4,2,1,0:T(8,128)(2,1)}, bf16[2,2,2,384,192]{3,4,2,1,0:T(8,128)(2,1)}, u32[]{:S(2)}, u32[]{:S(2)}) collective-permute-start(bf16[2,2,2,384,192]{3,4,2,1,0:T(8,128)(2,1)} %copy.62), channel_id=1, source_target_pairs={{0,2},{1,3},{2,0},{3,1},{4,6},{5,7},{6,4},{7,5},{8,10},{9,11},{10,... | collective-permute-start | bytes 3538952 | tf_op jit(solution)/shard_map/ppermute | solution.py:999
  256.9 31.9 %collective-permute-start.4 = (bf16[2,2,2,96,768]{4,3,2,1,0:T(8,128)(2,1)}, bf16[2,2,2,96,768]{4,3,2,1,0:T(8,128)(2,1)S(1)}, u32[]{:S(2)}, u32[]{:S(2)}) collective-permute-start(bf16[2,2,2,96,768]{4,3,2,1,0:T(8,128)(2,1)} %get-tuple-element.264), channel_id=1, source_target_pairs={{0,4},{4,0},{8,12},{12,8},{16,20},{20,16},{24,28},{28,24},{1,5},{5... | collective-permute-start | bytes 3538952 | tf_op jit(solution)/shard_map/ppermute | solution.py:999
  259.3 29.5 %collective-permute-start.3 = (bf16[2,2,2,96,192]{4,3,2,1,0:T(8,128)(2,1)S(1)}, bf16[2,2,2,96,192]{4,3,2,1,0:T(8,128)(2,1)S(1)}, u32[]{:S(2)}, u32[]{:S(2)}) collective-permute-start(bf16[2,2,2,96,192]{4,3,2,1,0:T(8,128)(2,1)S(1)} %get-tuple-element.274), channel_id=1, source_target_pairs={{0,2},{1,3},{2,0},{3,1},{4,6},{5,7},{6,4},{7,5},{8,10},{9,11},{10,... | collective-permute-start | bytes 884744 | tf_op jit(solution)/shard_map/ppermute | solution.py:999
  293.2 23.0 %collective-permute-start.8 = (bf16[2,2,384,192]{2,3,1,0:T(8,128)(2,1)}, bf16[2,2,384,192]{2,3,1,0:T(8,128)(2,1)}, u32[]{:S(2)}, u32[]{:S(2)}) collective-permute-start(bf16[2,2,384,192]{2,3,1,0:T(8,128)(2,1)} %copy.64), channel_id=1, source_target_pairs={{0,4},{4,0},{8,12},{12,8},{16,20},{20,16},{24,28},{28,24},{1,5},{5... | collective-permute-start | bytes 1769480 | tf_op jit(solution)/shard_map/ppermute | solution.py:999
  295.9 20.4 %collective-permute-start.7 = (bf16[2,2,96,768]{3,2,1,0:T(8,128)(2,1)S(1)}, bf16[2,2,96,768]{3,2,1,0:T(8,128)(2,1)S(1)}, u32[]{:S(2)}, u32[]{:S(2)}) collective-permute-start(bf16[2,2,96,768]{3,2,1,0:T(8,128)(2,1)S(1)} %get-tuple-element.270), channel_id=1, source_target_pairs={{0,2},{1,3},{2,0},{3,1},{4,6},{5,7},{6,4},{7,5},{8,10},{9,11},{10,... | collective-permute-start | bytes 1769480 | tf_op jit(solution)/shard_map/ppermute | solution.py:999
  297.0 19.2 %collective-permute-start.6 = (bf16[2,2,96,192]{3,2,1,0:T(8,128)(2,1)S(1)}, bf16[2,2,96,192]{3,2,1,0:T(8,128)(2,1)S(1)}, u32[]{:S(2)}, u32[]{:S(2)}) collective-permute-start(bf16[2,2,96,192]{3,2,1,0:T(8,128)(2,1)S(1)} %get-tuple-element.280), channel_id=1, source_target_pairs={{0,4},{4,0},{8,12},{12,8},{16,20},{20,16},{24,28},{28,24},{1,5},{5... | collective-permute-start | bytes 442376 | tf_op jit(solution)/shard_map/ppermute | solution.py:999
  317.9 22.9 %collective-permute-start.11 = (bf16[2,384,192]{2,1,0:T(8,128)(2,1)S(1)}, bf16[2,384,192]{2,1,0:T(8,128)(2,1)S(1)}, u32[]{:S(2)}, u32[]{:S(2)}) collective-permute-start(bf16[2,384,192]{2,1,0:T(8,128)(2,1)S(1)} %get-tuple-element.272), channel_id=1, source_target_pairs={{0,8},{4,12},{8,0},{12,4},{16,24},{20,28},{24,16},{28,20},{1,9},{5... | collective-permute-start | bytes 884744 | tf_op jit(solution)/shard_map/ppermute | solution.py:999
  319.3 21.5 %collective-permute-start.10 = (bf16[2,96,768]{2,1,0:T(8,128)(2,1)S(1)}, bf16[2,96,768]{2,1,0:T(8,128)(2,1)S(1)}, u32[]{:S(2)}, u32[]{:S(2)}) collective-permute-start(bf16[2,96,768]{2,1,0:T(8,128)(2,1)S(1)} %get-tuple-element.276), channel_id=1, source_target_pairs={{0,8},{4,12},{8,0},{12,4},{16,24},{20,28},{24,16},{28,20},{1,9},{5... | collective-permute-start | bytes 884744 | tf_op jit(solution)/shard_map/ppermute | solution.py:999
  320.3 20.4 %collective-permute-start.9 = (bf16[2,96,192]{2,1,0:T(8,128)(2,1)S(1)}, bf16[2,96,192]{2,1,0:T(8,128)(2,1)S(1)}, u32[]{:S(2)}, u32[]{:S(2)}) collective-permute-start(bf16[2,96,192]{2,1,0:T(8,128)(2,1)S(1)} %get-tuple-element.284), channel_id=1, source_target_pairs={{0,8},{4,12},{8,0},{12,4},{16,24},{20,28},{24,16},{28,20},{1,9},{5... | collective-permute-start | bytes 221192 | tf_op jit(solution)/shard_map/ppermute | solution.py:999
  340.9 27.4 %collective-permute-start.14 = (bf16[384,192]{1,0:T(8,128)(2,1)S(1)}, bf16[384,192]{1,0:T(8,128)(2,1)S(1)}, u32[]{:S(2)}, u32[]{:S(2)}) collective-permute-start(bf16[384,192]{1,0:T(8,128)(2,1)S(1)} %get-tuple-element.278), channel_id=1, source_target_pairs={{0,16},{4,20},{8,24},{12,28},{16,0},{20,4},{24,8},{28,12},{1,17},{... | collective-permute-start | bytes 442376 | tf_op jit(solution)/shard_map/ppermute | solution.py:999
  342.8 25.5 %collective-permute-start.13 = (bf16[96,768]{1,0:T(8,128)(2,1)S(1)}, bf16[96,768]{1,0:T(8,128)(2,1)S(1)}, u32[]{:S(2)}, u32[]{:S(2)}) collective-permute-start(bf16[96,768]{1,0:T(8,128)(2,1)S(1)} %get-tuple-element.282), channel_id=1, source_target_pairs={{0,16},{4,20},{8,24},{12,28},{16,0},{20,4},{24,8},{28,12},{1,17},{... | collective-permute-start | bytes 442376 | tf_op jit(solution)/shard_map/ppermute | solution.py:999
  362.7 5.6 %collective-permute-start.12 = (bf16[96,192]{1,0:T(8,128)(2,1)S(1)}, bf16[96,192]{1,0:T(8,128)(2,1)S(1)}, u32[]{:S(2)}, u32[]{:S(2)}) collective-permute-start(bf16[96,192]{1,0:T(8,128)(2,1)S(1)} %get-tuple-element.295), channel_id=1, source_target_pairs={{0,16},{4,20},{8,24},{12,28},{16,0},{20,4},{24,8},{28,12},{1,17},{... | collective-permute-start | bytes 110600 | tf_op jit(solution)/shard_map/ppermute | solution.py:999
  392.4 27.5 %collective-permute-start.20 = (bf16[2,2,2,2,48,576]{5,4,3,2,1,0:T(8,128)(2,1)}, bf16[2,2,2,2,48,576]{5,4,3,2,1,0:T(8,128)(2,1)S(1)}, u32[]{:S(2)}, u32[]{:S(2)}) collective-permute-start(bf16[2,2,2,2,48,576]{5,4,3,2,1,0:T(8,128)(2,1)} %slice_bitcast_fusion.9), channel_id=1, source_target_pairs={{0,1},{1,0},{2,3},{3,2},{4,5},{5,4},{6,7},{7,6},{8,9},{9,8},{10,11... | collective-permute-start | bytes 2654216 | tf_op jit(solution)/shard_map/ppermute | solution.py:999
  407.1 6.6 %collective-permute-start.19 = (f32[24192]{0:T(1024)S(1)}, f32[24192]{0:T(1024)S(1)}, u32[]{:S(2)}, u32[]{:S(2)}) collective-permute-start(f32[24192]{0:T(1024)S(1)} %add.117), channel_id=1, source_target_pairs={{0,16},{4,20},{8,24},{12,28},{16,0},{20,4},{24,8},{28,12},{1,17},{... | collective-permute-start | bytes 290312 | tf_op jit(solution)/shard_map/ppermute | solution.py:999
  409.3 12.3 %collective-permute-start.25 = (bf16[2,2,2,2,48,576]{5,4,3,2,1,0:T(8,128)(2,1)}, bf16[2,2,2,2,48,576]{5,4,3,2,1,0:T(8,128)(2,1)}, u32[]{:S(2)}, u32[]{:S(2)}) collective-permute-start(bf16[2,2,2,2,48,576]{5,4,3,2,1,0:T(8,128)(2,1)} %slice_bitcast_fusion.8), channel_id=1, source_target_pairs={{0,1},{1,0},{2,3},{3,2},{4,5},{5,4},{6,7},{7,6},{8,9},{9,8},{10,11... | collective-permute-start | bytes 2654216 | tf_op jit(solution)/shard_map/ppermute | solution.py:999
  421.3 9.2 %collective-permute-start.21 = (bf16[2,2,2,48,576]{4,3,2,1,0:T(8,128)(2,1)S(1)}, bf16[2,2,2,48,576]{4,3,2,1,0:T(8,128)(2,1)S(1)}, u32[]{:S(2)}, u32[]{:S(2)}) collective-permute-start(bf16[2,2,2,48,576]{4,3,2,1,0:T(8,128)(2,1)S(1)} %slice_bitcast_fusion.18), channel_id=1, source_target_pairs={{0,4},{4,0},{8,12},{12,8},{16,20},{20,16},{24,28},{28,24},{1,5},{5... | collective-permute-start | bytes 1327112 | tf_op jit(solution)/shard_map/ppermute | solution.py:999
  423.0 12.1 %collective-permute-start.26 = (bf16[2,2,2,48,576]{4,3,2,1,0:T(8,128)(2,1)S(1)}, bf16[2,2,2,48,576]{4,3,2,1,0:T(8,128)(2,1)S(1)}, u32[]{:S(2)}, u32[]{:S(2)}) collective-permute-start(bf16[2,2,2,48,576]{4,3,2,1,0:T(8,128)(2,1)S(1)} %slice_bitcast_fusion.16), channel_id=1, source_target_pairs={{0,2},{1,3},{2,0},{3,1},{4,6},{5,7},{6,4},{7,5},{8,10},{9,11},{10,... | collective-permute-start | bytes 1327112 | tf_op jit(solution)/shard_map/ppermute | solution.py:999
  430.6 7.1 %collective-permute-start.22 = (bf16[2,2,48,576]{3,2,1,0:T(8,128)(2,1)S(1)}, bf16[2,2,48,576]{3,2,1,0:T(8,128)(2,1)S(1)}, u32[]{:S(2)}, u32[]{:S(2)}) collective-permute-start(bf16[2,2,48,576]{3,2,1,0:T(8,128)(2,1)S(1)} %slice_bitcast_fusion.28), channel_id=1, source_target_pairs={{0,2},{1,3},{2,0},{3,1},{4,6},{5,7},{6,4},{7,5},{8,10},{9,11},{10,... | collective-permute-start | bytes 663560 | tf_op jit(solution)/shard_map/ppermute | solution.py:999
  435.2 6.3 %collective-permute-start.27 = (bf16[2,2,48,576]{3,2,1,0:T(8,128)(2,1)S(1)}, bf16[2,2,48,576]{3,2,1,0:T(8,128)(2,1)S(1)}, u32[]{:S(2)}, u32[]{:S(2)}) collective-permute-start(bf16[2,2,48,576]{3,2,1,0:T(8,128)(2,1)S(1)} %slice_bitcast_fusion.26), channel_id=1, source_target_pairs={{0,4},{4,0},{8,12},{12,8},{16,20},{20,16},{24,28},{28,24},{1,5},{5... | collective-permute-start | bytes 663560 | tf_op jit(solution)/shard_map/ppermute | solution.py:999
  447.1 5.8 %collective-permute-start.29 = (bf16[48,576]{1,0:T(8,128)(2,1)S(1)}, bf16[48,576]{1,0:T(8,128)(2,1)S(1)}, u32[]{:S(2)}, u32[]{:S(2)}) collective-permute-start(bf16[48,576]{1,0:T(8,128)(2,1)S(1)} %slice_bitcast_fusion.42), channel_id=1, source_target_pairs={{0,16},{4,20},{8,24},{12,28},{16,0},{20,4},{24,8},{28,12},{1,17},{... | collective-permute-start | bytes 165896 | tf_op jit(solution)/shard_map/ppermute | solution.py:999
  (43 other events, 599.0 us)
Sparse Core Ops, SparseCore 0:
  58.0 88.5 all-gather.2
